TPU v7x, 32 devices: a whole 2x2x4 slice. The times are simulated.
32 devices in a mesh: gx: 8 (over y, x, core), gz: 4 (over z).
Axes of the slice: x: 2, y: 2, z: 4, core: 2. Of those that a mesh axis runs over, the one named last changes fastest.
Arguments:
- factor: float32 [3, 256, 4, 32, 256], P(None, 'gz', None, 'gx'), may hold values from -6 to 6
- gain: float32 [3, 256, 4, 32, 256], P(None, 'gz', None, 'gx'), may hold values from -6 to 6
- base_flow: float32 [256, 32, 256], P('gz', 'gx'), may hold values from 0.25 to 2
- shift_index: int32 [1], replicated, may hold values from 0 to 7
- sensor_cells: int32 [4, 4], replicated, may hold values from 0 to 255, as said below
Outputs:
- new_factor: float32 [3, 256, 4, 32, 256], P(None, 'gz', None, 'gx')
- new_gain: float32 [3, 256, 4, 32, 256], P(None, 'gz', None, 'gx')
- gram: float32 [4, 4], replicated
Inputs may be any that keep to these rules, and one draw needn't show every extreme that they name: `sensor_cells`: row i gives sensor i's velocity component (0 to 2), spanwise index (0 to 255), streamwise index (0 to 31) and wall-normal index (0 to 255); in every draw some sensor sits at spanwise index 255, some at streamwise index 31 and some at wall-normal index 255.
All inputs are finite; a program needn't handle non-finite values.
Results may differ from a plain program's by a relative error of at most 0.03.
Values sent between devices are 32-bit elements; how exact they have to be, the bound alone decides.
No kernel may reach another device: no remote copies, remote signals or barrier semaphores. Data moves between devices by JAX's collectives and lax.ppermute only.
A program may use at most 64 MiB of HBM per device.

v0:
```python
import math

import jax
import jax.numpy as jnp
from jax import lax
from jax.sharding import PartitionSpec as P

SWEEPS = 3
POISSON = 4
SHIFTS = 8


viscosity = 0.4
shift_table = (0.6, 0.8, 1.0, 1.25, 1.6, 2.0, 2.5, 3.2)
chebyshev_weights = (1.0 / 1.9352976, 1.0 / 1.4752809, 1.0 / 0.8247191, 1.0 / 0.3647024)
highest = lax.Precision.HIGHEST


def padded_2(cells, sides, width, closed):
    for axis, dim in sides:
        count = lax.axis_size(axis)
        ends = count if closed else count - 1
        head = lax.slice_in_dim(cells, 0, width, axis=dim)
        tail = lax.slice_in_dim(cells, cells.shape[dim] - width, cells.shape[dim], axis=dim)
        cells = jnp.concatenate(
            [
                lax.ppermute(tail, axis, [(i, (i + 1) % count) for i in range(ends)]),
                cells,
                lax.ppermute(head, axis, [((i + 1) % count, i) for i in range(ends)]),
            ],
            axis=dim,
        )
    return cells


def around_sum(padded):
    summed = padded[:, 1:-1, :, 2:, 1:-1] + padded[:, 1:-1, :, :-2, 1:-1]
    summed = summed + padded[:, 1:-1, :, 1:-1, 2:] + padded[:, 1:-1, :, 1:-1, :-2]
    return summed + padded[:, 2:, :, 1:-1, 1:-1] + padded[:, :-2, :, 1:-1, 1:-1]


def shards(factor, gain, base_flow, shift_index, sensor_cells):
    components, span_cells, columns, stream_cells, normal_cells = factor.shape
    stream_start = lax.axis_index("gx") * stream_cells
    span_start = lax.axis_index("gz") * span_cells
    stream_total = stream_cells * lax.axis_size("gx")
    span_total = span_cells * lax.axis_size("gz")
    shift_values = jnp.asarray(shift_table, jnp.float32)
    shift_value = jnp.sum(jnp.where(jnp.arange(SHIFTS) == shift_index[0], shift_values, 0.0))
    base_field = base_flow[None, :, None, :, :]
    diagonal = shift_value + 6.0 * viscosity + base_field
    source = -factor

    def stream_inside(extent, margin):
        positions = stream_start - margin + jnp.arange(extent)
        return ((positions >= 0) & (positions < stream_total)).astype(jnp.float32)

    def extend(grid_field):
        padded = padded_2(grid_field, (("gx", 3), ("gz", 1)), 1, True)
        padded = padded * stream_inside(stream_cells + 2, 1)[None, None, None, :, None]
        return jnp.pad(padded, ((0, 0), (0, 0), (0, 0), (0, 0), (1, 1)))

    velocity = source / diagonal
    for sweep_index in range(SWEEPS):
        padded = extend(velocity)
        velocity = (
            source + viscosity * around_sum(padded) + base_field * padded[:, 1:-1, :, :-2, 1:-1]
        ) / diagonal
    padded = extend(velocity)
    divergence = 2.0 * (velocity[0] - padded[0, 1:-1, :, :-2, 1:-1])
    divergence = divergence + (velocity[1] - padded[1, 1:-1, :, 1:-1, :-2])
    divergence = divergence + (velocity[2] - padded[2, :-2, :, 1:-1, 1:-1])
    span_index = jnp.arange(span_total)
    products = span_index[:, None] * span_index[None, :] % span_total
    angles = 2.0 * math.pi * products.astype(jnp.float32) / span_total
    hartley_table = (jnp.cos(angles) + jnp.sin(angles)) / math.sqrt(span_total)

    def turn_modes(exchanged):
        turned = jnp.einsum("kz,zay->kay", hartley_table, exchanged, precision=highest)
        return lax.all_to_all(turned, "gz", split_axis=0, concat_axis=1, tiled=True)

    def transform(grid_field):
        flat = grid_field.reshape(span_cells, columns * stream_cells, normal_cells)
        result = turn_modes(lax.all_to_all(flat, "gz", split_axis=1, concat_axis=0, tiled=True))
        return result.reshape(span_cells, columns, stream_cells, normal_cells)

    modes_rhs = -transform(divergence)
    wave_index = span_start + jnp.arange(span_cells)
    wavenumber = 2.0 * math.pi * wave_index.astype(jnp.float32) / span_total
    mode_diagonal = (10.0 + (2.0 - 2.0 * jnp.cos(wavenumber)))[:, None, None, None]
    pressure = chebyshev_weights[0] * modes_rhs / mode_diagonal
    for sweep_level in range(1, POISSON):
        padded = padded_2(pressure, (("gx", 2),), 1, False)
        padded = jnp.pad(padded, ((0, 0), (0, 0), (0, 0), (1, 1)))
        beside_all = (
            4.0 * (padded[:, :, 2:, 1:-1] + padded[:, :, :-2, 1:-1])
            + padded[:, :, 1:-1, 2:]
            + padded[:, :, 1:-1, :-2]
        )
        pressure = (
            pressure
            + chebyshev_weights[sweep_level]
            * (modes_rhs - (mode_diagonal * pressure - beside_all))
            / mode_diagonal
        )
    pressure = transform(pressure)
    padded = extend(pressure[None])[0]
    gradient = jnp.stack(
        [
            2.0 * (padded[1:-1, :, 2:, 1:-1] - pressure),
            padded[1:-1, :, 1:-1, 2:] - pressure,
            padded[2:, :, 1:-1, 1:-1] - pressure,
        ]
    )
    solved = velocity - gradient
    span_ids = span_start + jnp.arange(span_cells)
    stream_ids = stream_start + jnp.arange(stream_cells)
    normal_ids = jnp.arange(normal_cells)
    located = span_ids[None, :, None, None] == sensor_cells[:, 1][:, None, None, None]
    located = located & (stream_ids[None, None, :, None] == sensor_cells[:, 2][:, None, None, None])
    located = located & (normal_ids[None, None, None, :] == sensor_cells[:, 3][:, None, None, None])
    picked = jnp.einsum("szxy,czjxy->scj", located.astype(jnp.float32), solved, precision=highest)
    chooser = (jnp.arange(3)[None, :] == sensor_cells[:, 0:1]).astype(jnp.float32)
    readout_local = jnp.sum(picked * chooser[:, :, None], axis=1)
    new_factor = factor + 2.0 * shift_value * solved
    gram_local = jnp.einsum("czixy,czjxy->ij", new_factor, new_factor, precision=highest)
    gram_total, readout = lax.psum((gram_local, readout_local), ("gx", "gz"))
    gram = gram_total / (3.0 * stream_total * normal_cells * span_total)
    new_gain = gain + 2.0 * shift_value * jnp.einsum(
        "czjxy,ij->czixy", solved, readout, precision=highest
    )
    return (new_factor, new_gain, gram)


def solution(mesh):
    placed = (
        P(None, "gz", None, "gx", None),
        P(None, "gz", None, "gx", None),
        P("gz", "gx", None),
        P(),
        P(),
    )
    return jax.shard_map(
        shards,
        mesh=mesh,
        in_specs=placed,
        out_specs=(P(None, "gz", None, "gx", None), P(None, "gz", None, "gx", None), P()),
        check_vma=False,
    )
```

profile of v0, /device:TPU:0, one launch (start us, length us, event | category | flops | bytes accessed | tf_op | source)
XLA Modules:
  0.0 419.2 jit_solution(3506419593793594025)
XLA Ops:
  1.3 1.3 fusion.91
  4.3 3.8 fusion.31
  8.1 1.3 slice_bitcast_fusion.7
  9.9 2.9 collective-permute-start.1
  13.5 15.0 %collective-permute-done = f32[3,64,4,1,256]{4,1,3,2,0:T(8,128)} collective-permute-done((f32[3,64,4,1,256]{4,1,3,2,0:T(8,128)}, f32[3,64,4,1,256]{4,1,3,2,0:T(8,128)}, u32[]{:S(2)}, u32[]{:S(2)}) %collective-permute-start) | collective-permute-done | bytes 786464 | tf_op jit(solution)/shard_map/ppermute | solution.py:27
  28.5 1.5 collective-permute-done.1
  30.0 1.1 pad_maximum_fusion.17
  31.2 1.6 collective-permute-start.2
  32.8 2.2 collective-permute-start.3
  35.1 2.4 collective-permute-done.2
  37.5 1.7 collective-permute-done.3
  39.2 2.2 maximum_multiply_fusion
  41.5 4.8 %fusion.7 = f32[3,64,4,4,256]{4,1,2,3,0:T(8,128)S(1)} fusion(f32[3,66,4,6,256]{4,1,2,3,0:T(8,128)S(1)} %maximum_multiply_fusion, f32[3,64,4,4,256]{4,3,2,1,0:T(4,128)S(1)} %copy-done, f32[64,4,256]{2,0,1:T(8,128)S(1)} %copy-done.5, f32[64,4,256]{2,0,1:T(8,128)S(1)} %copy.41), kind=kLoop, calls=%fused_computation.20 | loop fusion | flops 8650752 | bytes 24707072 | tf_op jit(solution)/shard_map/div | solution.py:66
  46.6 2.5 collective-permute-start.5
  49.1 17.0 %collective-permute-done.4 = f32[3,64,4,1,256]{4,1,3,2,0:T(8,128)S(1)} collective-permute-done((f32[3,64,4,1,256]{4,1,3,2,0:T(8,128)S(1)}, f32[3,64,4,1,256]{4,1,3,2,0:T(8,128)S(1)}, u32[]{:S(2)}, u32[]{:S(2)}) %collective-permute-start.4) | collective-permute-done | bytes 786464 | tf_op jit(solution)/shard_map/ppermute | solution.py:27
  67.2 3.0 collective-permute-start.7
  70.2 3.2 collective-permute-done.6
  73.8 1.1 maximum_multiply_fusion.1
  74.9 4.8 %fusion.15 = f32[3,64,4,4,256]{4,1,2,3,0:T(8,128)S(1)} fusion(f32[3,66,4,6,256]{4,1,2,3,0:T(8,128)S(1)} %maximum_multiply_fusion.1, f32[3,64,4,4,256]{4,3,2,1,0:T(4,128)S(1)} %copy-done, f32[64,4,256]{2,0,1:T(8,128)S(1)} %copy-done.5, f32[64,4,256]{2,0,1:T(8,128)S(1)} %copy.41), kind=kLoop, calls=%fused_computation.28 | loop fusion | flops 8650752 | bytes 24707072 | tf_op jit(solution)/shard_map/div | solution.py:66
  80.0 2.5 collective-permute-start.9
  82.6 17.0 %collective-permute-done.8 = f32[3,64,4,1,256]{4,1,3,2,0:T(8,128)S(1)} collective-permute-done((f32[3,64,4,1,256]{4,1,3,2,0:T(8,128)S(1)}, f32[3,64,4,1,256]{4,1,3,2,0:T(8,128)S(1)}, u32[]{:S(2)}, u32[]{:S(2)}) %collective-permute-start.8) | collective-permute-done | bytes 786464 | tf_op jit(solution)/shard_map/ppermute | solution.py:27
  99.8 4.3 %collective-permute-start.11 = (f32[3,1,4,6,256]{4,1,2,3,0:T(1,128)S(1)}, f32[3,1,4,6,256]{4,1,2,3,0:T(1,128)S(1)}, u32[]{:S(2)}, u32[]{:S(2)}) collective-permute-start(f32[3,1,4,6,256]{4,1,2,3,0:T(1,128)S(1)} %get-tuple-element.26), channel_id=1, source_target_pairs={{1,0},{2,1},{3,2},{0,3},{5,4},{6,5},{7,6},{4,7},{9,8},{10,9},{11,1... | collective-permute-start | bytes 221192 | tf_op jit(solution)/shard_map/ppermute | solution.py:29
  104.0 2.4 collective-permute-done.10
  107.2 1.1 maximum_multiply_fusion.2
  108.3 4.8 %fusion.23 = f32[3,64,4,4,256]{4,1,2,3,0:T(8,128)S(1)} fusion(f32[3,66,4,6,256]{4,1,2,3,0:T(8,128)S(1)} %maximum_multiply_fusion.2, f32[3,64,4,4,256]{4,3,2,1,0:T(4,128)S(1)} %copy-done, f32[64,4,256]{2,0,1:T(8,128)S(1)} %copy-done.5, f32[64,4,256]{2,0,1:T(8,128)S(1)} %copy.41), kind=kLoop, calls=%fused_computation.36 | loop fusion | flops 8650752 | bytes 24707072 | tf_op jit(solution)/shard_map/div | solution.py:66
  113.4 2.6 collective-permute-start.13
  116.0 15.7 %collective-permute-done.12 = f32[3,64,4,1,256]{4,1,3,2,0:T(8,128)S(1)} collective-permute-done((f32[3,64,4,1,256]{4,1,3,2,0:T(8,128)S(1)}, f32[3,64,4,1,256]{4,1,3,2,0:T(8,128)S(1)}, u32[]{:S(2)}, u32[]{:S(2)}) %collective-permute-start.12) | collective-permute-done | bytes 786464 | tf_op jit(solution)/shard_map/ppermute | solution.py:27
  131.8 2.6 collective-permute-start.14
  134.5 1.6 collective-permute-start.15
  136.0 3.1 collective-permute-done.14
  140.0 1.2 maximum_multiply_fusion.3
  141.9 29.5 %all_to_all.60 = f32[64,16,256]{2,0,1:T(8,128)S(1)} all-to-all(f32[64,16,256]{2,0,1:T(8,128)S(1)} %bitcast.93), channel_id=1, replica_groups=mesh['gx'=8,'gz'=4] {'gz'}, dimensions={1} | all-to-all | bytes 2097152 | tf_op jit(solution)/shard_map/all_to_all | solution.py:84
  171.5 2.1 fusion.84
  173.7 1.6 copy.61
  175.3 4.2 %all-to-all-start.1 = ((f32[256,4,256]{2,1,0:T(4,128)}), f32[256,4,256]{2,1,0:T(4,128)}, u32[]{:S(2)}, u32[]{:S(2)}) async-start(f32[256,4,256]{2,1,0:T(4,128)} %copy.61), calls=%async_computation.1 | async-start | bytes 2097152 | tf_op jit(solution)/shard_map/all_to_all | solution.py:80
  179.6 24.9 %all-to-all-done.1 = f32[256,4,256]{2,1,0:T(4,128)} async-done(((f32[256,4,256]{2,1,0:T(4,128)}), f32[256,4,256]{2,1,0:T(4,128)}, u32[]{:S(2)}, u32[]{:S(2)}) %all-to-all-start.1) | async-done | bytes 1048608 | tf_op jit(solution)/shard_map/all_to_all | solution.py:80
  204.5 1.5 copy_negate_fusion.1
  206.2 1.3 collective-permute-start.16
  207.5 3.0 collective-permute-start.17
  210.6 1.1 collective-permute-done.17
  212.9 1.3 collective-permute-start.18
  214.2 5.1 %collective-permute-start.19 = (f32[64,4,1,256]{3,0,1,2:T(8,128)S(1)}, f32[64,4,1,256]{3,0,1,2:T(8,128)S(1)}, u32[]{:S(2)}, u32[]{:S(2)}) collective-permute-start(f32[64,4,1,256]{3,0,1,2:T(8,128)S(1)} %get-tuple-element.48), channel_id=1, source_target_pairs={{0,4},{4,8},{8,12},{12,16},{16,20},{20,24},{24,28},{1,5},{5,9},{9,... | collective-permute-start | bytes 786440 | tf_op jit(solution)/shard_map/ppermute | solution.py:27
  219.4 1.1 collective-permute-done.19
  221.7 1.3 collective-permute-start.20
  223.0 7.0 %collective-permute-start.21 = (f32[64,4,1,256]{3,0,1,2:T(8,128)S(1)}, f32[64,4,1,256]{3,0,1,2:T(8,128)S(1)}, u32[]{:S(2)}, u32[]{:S(2)}) collective-permute-start(f32[64,4,1,256]{3,0,1,2:T(8,128)S(1)} %get-tuple-element.46), channel_id=1, source_target_pairs={{0,4},{4,8},{8,12},{12,16},{16,20},{20,24},{24,28},{1,5},{5,9},{9,... | collective-permute-start | bytes 786440 | tf_op jit(solution)/shard_map/ppermute | solution.py:27
  230.0 1.1 collective-permute-done.21
  232.4 27.6 %all_to_all.61 = f32[64,16,256]{2,0,1:T(8,128)S(1)} all-to-all(f32[64,16,256]{2,0,1:T(8,128)S(1)} %bitcast.96), channel_id=1, replica_groups=mesh['gx'=8,'gz'=4] {'gz'}, dimensions={1} | all-to-all | bytes 2097152 | tf_op jit(solution)/shard_map/all_to_all | solution.py:84
  260.1 2.1 fusion.82
  262.2 1.6 copy.65
  263.9 4.2 %all-to-all-start.3 = ((f32[256,4,256]{2,1,0:T(4,128)}), f32[256,4,256]{2,1,0:T(4,128)}, u32[]{:S(2)}, u32[]{:S(2)}) async-start(f32[256,4,256]{2,1,0:T(4,128)} %copy.65), calls=%async_computation.3 | async-start | bytes 2097152 | tf_op jit(solution)/shard_map/all_to_all | solution.py:80
  268.5 26.1 %all-to-all-done.3 = f32[256,4,256]{2,1,0:T(4,128)} async-done(((f32[256,4,256]{2,1,0:T(4,128)}), f32[256,4,256]{2,1,0:T(4,128)}, u32[]{:S(2)}, u32[]{:S(2)}) %all-to-all-start.3) | async-done | bytes 1048608 | tf_op jit(solution)/shard_map/all_to_all | solution.py:80
  294.5 1.4 copy.66
  296.7 2.0 collective-permute-start.23
  298.8 4.0 collective-permute-done.22
  302.8 3.3 collective-permute-done.23
  306.8 12.3 %collective-permute-start.25 = (f32[1,1,4,6,256]{4,1,2,3,0:T(1,128)S(1)}, f32[1,1,4,6,256]{4,1,2,3,0:T(1,128)S(1)}, u32[]{:S(2)}, u32[]{:S(2)}) collective-permute-start(f32[1,1,4,6,256]{4,1,2,3,0:T(1,128)S(1)} %get-tuple-element.43), channel_id=1, source_target_pairs={{1,0},{2,1},{3,2},{0,3},{5,4},{6,5},{7,6},{4,7},{9,8},{10,9},{11,1... | collective-permute-start | bytes 73736 | tf_op jit(solution)/shard_map/ppermute | solution.py:29
  320.6 1.6 maximum_multiply_fusion.4
  324.9 2.1 multiply_add_fusion
  327.0 14.5 %fusion.43 = f32[4,4]{1,0:T(4,128)S(1)} fusion(f32[3,64,4,4,256]{4,1,2,3,0:T(8,128)S(1)} %get-tuple-element.21), kind=kOutput, calls=%fused_computation.63 | convolution fusion | flops 37748736 | bytes 3145792 | tf_op jit(solution)/shard_map/czixy,czjxy->ij/dot_general | solution.py:126
  341.5 17.3 %fusion.40 = f32[4,4]{1,0:T(4,128)S(1)} fusion(f32[3,64,4,4,256]{4,1,2,3,0:T(8,128)S(1)} %get-tuple-element.22, pred[4,256]{1,0:T(4,128)(4,1)S(1)} %iota_compare_fusion.2, pred[4,64,4]{0,1,2:T(8,128)(4,1)S(1)} %broadcast_and_fusion, f32[4,3]{0,1:T(4,128)S(1)} %fusion.90), kind=kOutput, calls=%fused_computation.62 | convolution fusion | flops 38010960 | bytes 3147888 | tf_op jit(solution)/shard_map/szxy,czjxy->scj/dot_general | solution.py:122
  358.8 3.7 copy.73
  362.5 42.1 %all-reduce.8 = (f32[4,4]{1,0:T(4,128)S(1)}, f32[4,4]{1,0:T(4,128)S(1)}) all-reduce(f32[4,4]{1,0:T(4,128)S(1)} %fusion.40, f32[4,4]{1,0:T(4,128)S(1)} %fusion.43), channel_id=1, replica_groups=mesh['gx'=8,'gz'=4] {'gx','gz'}, use_global_device_ids=true, to_apply=%region_2.3 | all-reduce | flops 32 | bytes 256 | tf_op jit(solution)/shard_map/psum | solution.py:127
  404.7 11.0 %bitcast_add_fusion = f32[3,64,4,4,256]{4,2,3,1,0:T(4,128)S(1)} fusion(f32[3,64,4,4,256]{4,3,2,1,0:T(4,128)} %param.7, f32[3,64,4,4,256]{4,1,2,3,0:T(8,128)} %copy-done.4, f32[]{:T(128)S(6)} %mul.194, f32[4,4]{1,0:T(4,128)S(1)} %get-tuple-element.19), kind=kOutput, calls=%fused_computation.41 | convolution fusion | flops 39321600 | bytes 9437252 | tf_op jit(solution)/shard_map/czjxy,ij->czixy/dot_general | solution.py:129
  415.7 2.5 copy.74
  (76 shorter events, 17.1 us)
Async XLA Ops:
  8.1 4.6 %copy-start.7 = (f32[64,4,256]{2,1,0:T(4,128)S(1)}, f32[64,4,256]{2,1,0:T(4,128)}, u32[]{:S(2)}) copy-start(f32[64,4,256]{2,1,0:T(4,128)} %param.8) | copy-start | bytes 786436
  9.4 19.1 %collective-permute-start = (f32[3,64,4,1,256]{4,1,3,2,0:T(8,128)}, f32[3,64,4,1,256]{4,1,3,2,0:T(8,128)}, u32[]{:S(2)}, u32[]{:S(2)}) collective-permute-start(f32[3,64,4,1,256]{4,1,3,2,0:T(8,128)} %get-tuple-element.40), channel_id=1, source_target_pairs={{0,4},{4,8},{8,12},{12,16},{16,20},{20,24},{24,28},{28,0},{1,5},{5... | collective-permute-start | bytes 2359304 | tf_op jit(solution)/shard_map/ppermute | solution.py:27
  9.9 20.2 %collective-permute-start.1 = (f32[3,64,4,1,256]{4,1,3,2,0:T(8,128)}, f32[3,64,4,1,256]{4,1,3,2,0:T(8,128)}, u32[]{:S(2)}, u32[]{:S(2)}) collective-permute-start(f32[3,64,4,1,256]{4,1,3,2,0:T(8,128)} %get-tuple-element.41), channel_id=1, source_target_pairs={{4,0},{8,4},{12,8},{16,12},{20,16},{24,20},{28,24},{0,28},{5,1},{9... | collective-permute-start | bytes 2359304 | tf_op jit(solution)/shard_map/ppermute | solution.py:29
  31.2 6.3 %collective-permute-start.2 = (f32[3,1,4,6,256]{4,1,2,3,0:T(1,128)S(1)}, f32[3,1,4,6,256]{4,1,2,3,0:T(1,128)S(1)}, u32[]{:S(2)}, u32[]{:S(2)}) collective-permute-start(f32[3,1,4,6,256]{4,1,2,3,0:T(1,128)S(1)} %get-tuple-element.29), channel_id=1, source_target_pairs={{0,1},{1,2},{2,3},{3,0},{4,5},{5,6},{6,7},{7,4},{8,9},{9,10},{10,1... | collective-permute-start | bytes 221192 | tf_op jit(solution)/shard_map/ppermute | solution.py:27
  32.8 6.4 %collective-permute-start.3 = (f32[3,1,4,6,256]{4,1,2,3,0:T(1,128)S(1)}, f32[3,1,4,6,256]{4,1,2,3,0:T(1,128)S(1)}, u32[]{:S(2)}, u32[]{:S(2)}) collective-permute-start(f32[3,1,4,6,256]{4,1,2,3,0:T(1,128)S(1)} %get-tuple-element.30), channel_id=1, source_target_pairs={{1,0},{2,1},{3,2},{0,3},{5,4},{6,5},{7,6},{4,7},{9,8},{10,9},{11,1... | collective-permute-start | bytes 221192 | tf_op jit(solution)/shard_map/ppermute | solution.py:29
  35.1 6.4 %copy-start = (f32[3,64,4,4,256]{4,3,2,1,0:T(4,128)S(1)}, f32[3,64,4,4,256]{4,3,2,1,0:T(4,128)}, u32[]{:S(2)}) copy-start(f32[3,64,4,4,256]{4,3,2,1,0:T(4,128)} %param.6) | copy-start | bytes 9437188
  35.1 6.4 %copy-start.5 = (f32[64,4,256]{2,0,1:T(8,128)S(1)}, f32[64,4,256]{2,0,1:T(8,128)}, u32[]{:S(2)}) copy-start(f32[64,4,256]{2,0,1:T(8,128)} %copy.46) | copy-start | bytes 786436
  46.4 19.7 %collective-permute-start.4 = (f32[3,64,4,1,256]{4,1,3,2,0:T(8,128)S(1)}, f32[3,64,4,1,256]{4,1,3,2,0:T(8,128)S(1)}, u32[]{:S(2)}, u32[]{:S(2)}) collective-permute-start(f32[3,64,4,1,256]{4,1,3,2,0:T(8,128)S(1)} %get-tuple-element.38), channel_id=1, source_target_pairs={{0,4},{4,8},{8,12},{12,16},{16,20},{20,24},{24,28},{28,0},{1,5},{5... | collective-permute-start | bytes 2359304 | tf_op jit(solution)/shard_map/ppermute | solution.py:27
  46.6 19.5 %collective-permute-start.5 = (f32[3,64,4,1,256]{4,1,3,2,0:T(8,128)S(1)}, f32[3,64,4,1,256]{4,1,3,2,0:T(8,128)S(1)}, u32[]{:S(2)}, u32[]{:S(2)}) collective-permute-start(f32[3,64,4,1,256]{4,1,3,2,0:T(8,128)S(1)} %get-tuple-element.39), channel_id=1, source_target_pairs={{4,0},{8,4},{12,8},{16,12},{20,16},{24,20},{28,24},{0,28},{5,1},{9... | collective-permute-start | bytes 2359304 | tf_op jit(solution)/shard_map/ppermute | solution.py:29
  66.3 7.0 %collective-permute-start.6 = (f32[3,1,4,6,256]{4,1,2,3,0:T(1,128)S(1)}, f32[3,1,4,6,256]{4,1,2,3,0:T(1,128)S(1)}, u32[]{:S(2)}, u32[]{:S(2)}) collective-permute-start(f32[3,1,4,6,256]{4,1,2,3,0:T(1,128)S(1)} %get-tuple-element.27), channel_id=1, source_target_pairs={{0,1},{1,2},{2,3},{3,0},{4,5},{5,6},{6,7},{7,4},{8,9},{9,10},{10,1... | collective-permute-start | bytes 221192 | tf_op jit(solution)/shard_map/ppermute | solution.py:27
  67.2 6.6 %collective-permute-start.7 = (f32[3,1,4,6,256]{4,1,2,3,0:T(1,128)S(1)}, f32[3,1,4,6,256]{4,1,2,3,0:T(1,128)S(1)}, u32[]{:S(2)}, u32[]{:S(2)}) collective-permute-start(f32[3,1,4,6,256]{4,1,2,3,0:T(1,128)S(1)} %get-tuple-element.28), channel_id=1, source_target_pairs={{1,0},{2,1},{3,2},{0,3},{5,4},{6,5},{7,6},{4,7},{9,8},{10,9},{11,1... | collective-permute-start | bytes 221192 | tf_op jit(solution)/shard_map/ppermute | solution.py:29
  79.9 19.7 %collective-permute-start.8 = (f32[3,64,4,1,256]{4,1,3,2,0:T(8,128)S(1)}, f32[3,64,4,1,256]{4,1,3,2,0:T(8,128)S(1)}, u32[]{:S(2)}, u32[]{:S(2)}) collective-permute-start(f32[3,64,4,1,256]{4,1,3,2,0:T(8,128)S(1)} %get-tuple-element.36), channel_id=1, source_target_pairs={{0,4},{4,8},{8,12},{12,16},{16,20},{20,24},{24,28},{28,0},{1,5},{5... | collective-permute-start | bytes 2359304 | tf_op jit(solution)/shard_map/ppermute | solution.py:27
  80.0 19.6 %collective-permute-start.9 = (f32[3,64,4,1,256]{4,1,3,2,0:T(8,128)S(1)}, f32[3,64,4,1,256]{4,1,3,2,0:T(8,128)S(1)}, u32[]{:S(2)}, u32[]{:S(2)}) collective-permute-start(f32[3,64,4,1,256]{4,1,3,2,0:T(8,128)S(1)} %get-tuple-element.37), channel_id=1, source_target_pairs={{4,0},{8,4},{12,8},{16,12},{20,16},{24,20},{28,24},{0,28},{5,1},{9... | collective-permute-start | bytes 2359304 | tf_op jit(solution)/shard_map/ppermute | solution.py:29
  99.7 6.7 %collective-permute-start.10 = (f32[3,1,4,6,256]{4,1,2,3,0:T(1,128)S(1)}, f32[3,1,4,6,256]{4,1,2,3,0:T(1,128)S(1)}, u32[]{:S(2)}, u32[]{:S(2)}) collective-permute-start(f32[3,1,4,6,256]{4,1,2,3,0:T(1,128)S(1)} %get-tuple-element.25), channel_id=1, source_target_pairs={{0,1},{1,2},{2,3},{3,0},{4,5},{5,6},{6,7},{7,4},{8,9},{9,10},{10,1... | collective-permute-start | bytes 221192 | tf_op jit(solution)/shard_map/ppermute | solution.py:27
  99.8 7.4 %collective-permute-start.11 = (f32[3,1,4,6,256]{4,1,2,3,0:T(1,128)S(1)}, f32[3,1,4,6,256]{4,1,2,3,0:T(1,128)S(1)}, u32[]{:S(2)}, u32[]{:S(2)}) collective-permute-start(f32[3,1,4,6,256]{4,1,2,3,0:T(1,128)S(1)} %get-tuple-element.26), channel_id=1, source_target_pairs={{1,0},{2,1},{3,2},{0,3},{5,4},{6,5},{7,6},{4,7},{9,8},{10,9},{11,1... | collective-permute-start | bytes 221192 | tf_op jit(solution)/shard_map/ppermute | solution.py:29
  113.3 18.4 %collective-permute-start.12 = (f32[3,64,4,1,256]{4,1,3,2,0:T(8,128)S(1)}, f32[3,64,4,1,256]{4,1,3,2,0:T(8,128)S(1)}, u32[]{:S(2)}, u32[]{:S(2)}) collective-permute-start(f32[3,64,4,1,256]{4,1,3,2,0:T(8,128)S(1)} %get-tuple-element.34), channel_id=1, source_target_pairs={{0,4},{4,8},{8,12},{12,16},{16,20},{20,24},{24,28},{28,0},{1,5},{5... | collective-permute-start | bytes 2359304 | tf_op jit(solution)/shard_map/ppermute | solution.py:27
  113.4 18.3 %collective-permute-start.13 = (f32[3,64,4,1,256]{4,1,3,2,0:T(8,128)S(1)}, f32[3,64,4,1,256]{4,1,3,2,0:T(8,128)S(1)}, u32[]{:S(2)}, u32[]{:S(2)}) collective-permute-start(f32[3,64,4,1,256]{4,1,3,2,0:T(8,128)S(1)} %get-tuple-element.35), channel_id=1, source_target_pairs={{4,0},{8,4},{12,8},{16,12},{20,16},{24,20},{28,24},{0,28},{5,1},{9... | collective-permute-start | bytes 2359304 | tf_op jit(solution)/shard_map/ppermute | solution.py:29
  131.8 7.3 %collective-permute-start.14 = (f32[3,1,4,6,256]{4,1,2,3,0:T(1,128)S(1)}, f32[3,1,4,6,256]{4,1,2,3,0:T(1,128)S(1)}, u32[]{:S(2)}, u32[]{:S(2)}) collective-permute-start(f32[3,1,4,6,256]{4,1,2,3,0:T(1,128)S(1)} %get-tuple-element.23), channel_id=1, source_target_pairs={{0,1},{1,2},{2,3},{3,0},{4,5},{5,6},{6,7},{7,4},{8,9},{9,10},{10,1... | collective-permute-start | bytes 221192 | tf_op jit(solution)/shard_map/ppermute | solution.py:27
  134.5 5.6 %collective-permute-start.15 = (f32[3,1,4,6,256]{4,1,2,3,0:T(1,128)S(1)}, f32[3,1,4,6,256]{4,1,2,3,0:T(1,128)S(1)}, u32[]{:S(2)}, u32[]{:S(2)}) collective-permute-start(f32[3,1,4,6,256]{4,1,2,3,0:T(1,128)S(1)} %get-tuple-element.24), channel_id=1, source_target_pairs={{1,0},{2,1},{3,2},{0,3},{5,4},{6,5},{7,6},{4,7},{9,8},{10,9},{11,1... | collective-permute-start | bytes 221192 | tf_op jit(solution)/shard_map/ppermute | solution.py:29
  175.3 29.2 %all-to-all-start.1 = ((f32[256,4,256]{2,1,0:T(4,128)}), f32[256,4,256]{2,1,0:T(4,128)}, u32[]{:S(2)}, u32[]{:S(2)}) async-start(f32[256,4,256]{2,1,0:T(4,128)} %copy.61), calls=%async_computation.1 | async-start | bytes 2097152 | tf_op jit(solution)/shard_map/all_to_all | solution.py:80
  206.2 4.4 %collective-permute-start.16 = (f32[64,4,1,256]{3,0,1,2:T(8,128)S(1)}, f32[64,4,1,256]{3,0,1,2:T(8,128)S(1)}, u32[]{:S(2)}, u32[]{:S(2)}) collective-permute-start(f32[64,4,1,256]{3,0,1,2:T(8,128)S(1)} %get-tuple-element.51), channel_id=1, source_target_pairs={{4,0},{8,4},{12,8},{16,12},{20,16},{24,20},{28,24},{5,1},{9,5},{13... | collective-permute-start | bytes 786440 | tf_op jit(solution)/shard_map/ppermute | solution.py:29
  207.5 4.2 collective-permute-start.17
  212.9 6.4 %collective-permute-start.18 = (f32[64,4,1,256]{3,0,1,2:T(8,128)S(1)}, f32[64,4,1,256]{3,0,1,2:T(8,128)S(1)}, u32[]{:S(2)}, u32[]{:S(2)}) collective-permute-start(f32[64,4,1,256]{3,0,1,2:T(8,128)S(1)} %get-tuple-element.49), channel_id=1, source_target_pairs={{4,0},{8,4},{12,8},{16,12},{20,16},{24,20},{28,24},{5,1},{9,5},{13... | collective-permute-start | bytes 786440 | tf_op jit(solution)/shard_map/ppermute | solution.py:29
  214.2 6.3 %collective-permute-start.19 = (f32[64,4,1,256]{3,0,1,2:T(8,128)S(1)}, f32[64,4,1,256]{3,0,1,2:T(8,128)S(1)}, u32[]{:S(2)}, u32[]{:S(2)}) collective-permute-start(f32[64,4,1,256]{3,0,1,2:T(8,128)S(1)} %get-tuple-element.48), channel_id=1, source_target_pairs={{0,4},{4,8},{8,12},{12,16},{16,20},{20,24},{24,28},{1,5},{5,9},{9,... | collective-permute-start | bytes 786440 | tf_op jit(solution)/shard_map/ppermute | solution.py:27
  221.7 8.4 %collective-permute-start.20 = (f32[64,4,1,256]{3,0,1,2:T(8,128)S(1)}, f32[64,4,1,256]{3,0,1,2:T(8,128)S(1)}, u32[]{:S(2)}, u32[]{:S(2)}) collective-permute-start(f32[64,4,1,256]{3,0,1,2:T(8,128)S(1)} %get-tuple-element.47), channel_id=1, source_target_pairs={{4,0},{8,4},{12,8},{16,12},{20,16},{24,20},{28,24},{5,1},{9,5},{13... | collective-permute-start | bytes 786440 | tf_op jit(solution)/shard_map/ppermute | solution.py:29
  223.0 8.2 %collective-permute-start.21 = (f32[64,4,1,256]{3,0,1,2:T(8,128)S(1)}, f32[64,4,1,256]{3,0,1,2:T(8,128)S(1)}, u32[]{:S(2)}, u32[]{:S(2)}) collective-permute-start(f32[64,4,1,256]{3,0,1,2:T(8,128)S(1)} %get-tuple-element.46), channel_id=1, source_target_pairs={{0,4},{4,8},{8,12},{12,16},{16,20},{20,24},{24,28},{1,5},{5,9},{9,... | collective-permute-start | bytes 786440 | tf_op jit(solution)/shard_map/ppermute | solution.py:27
  260.1 8.1 %copy-start.8 = (s32[4,4]{1,0:T(4,128)S(1)}, s32[4,4]{1,0:T(4,128)}, u32[]{:S(2)}) copy-start(s32[4,4]{1,0:T(4,128)} %param.10) | copy-start | bytes 196
  263.9 30.6 %all-to-all-start.3 = ((f32[256,4,256]{2,1,0:T(4,128)}), f32[256,4,256]{2,1,0:T(4,128)}, u32[]{:S(2)}, u32[]{:S(2)}) async-start(f32[256,4,256]{2,1,0:T(4,128)} %copy.65), calls=%async_computation.3 | async-start | bytes 2097152 | tf_op jit(solution)/shard_map/all_to_all | solution.py:80
  296.0 10.1 %copy-start.2 = (f32[256,4,256]{2,0,1:T(8,128)}, f32[256,4,256]{2,0,1:T(8,128)S(1)}, u32[]{:S(2)}) copy-start(f32[256,4,256]{2,0,1:T(8,128)S(1)} %copy.66) | copy-start | bytes 3145732
  296.0 6.7 %collective-permute-start.22 = (f32[1,64,4,1,256]{4,1,2,3,0:T(8,128)S(1)}, f32[1,64,4,1,256]{4,1,2,3,0:T(8,128)S(1)}, u32[]{:S(2)}, u32[]{:S(2)}) collective-permute-start(f32[1,64,4,1,256]{4,1,2,3,0:T(8,128)S(1)} %get-tuple-element.44), channel_id=1, source_target_pairs={{0,4},{4,8},{8,12},{12,16},{16,20},{20,24},{24,28},{28,0},{1,5},{5... | collective-permute-start | bytes 786440 | tf_op jit(solution)/shard_map/ppermute | solution.py:27
  296.7 9.4 %collective-permute-start.23 = (f32[1,64,4,1,256]{4,1,2,3,0:T(8,128)S(1)}, f32[1,64,4,1,256]{4,1,2,3,0:T(8,128)S(1)}, u32[]{:S(2)}, u32[]{:S(2)}) collective-permute-start(f32[1,64,4,1,256]{4,1,2,3,0:T(8,128)S(1)} %get-tuple-element.45), channel_id=1, source_target_pairs={{4,0},{8,4},{12,8},{16,12},{20,16},{24,20},{28,24},{0,28},{5,1},{9... | collective-permute-start | bytes 786440 | tf_op jit(solution)/shard_map/ppermute | solution.py:29
  306.1 0.7 copy-start.6
  306.8 13.1 %collective-permute-start.24 = (f32[1,1,4,6,256]{4,1,2,3,0:T(1,128)S(1)}, f32[1,1,4,6,256]{4,1,2,3,0:T(1,128)S(1)}, u32[]{:S(2)}, u32[]{:S(2)}) collective-permute-start(f32[1,1,4,6,256]{4,1,2,3,0:T(1,128)S(1)} %get-tuple-element.42), channel_id=1, source_target_pairs={{0,1},{1,2},{2,3},{3,0},{4,5},{5,6},{6,7},{7,4},{8,9},{9,10},{10,1... | collective-permute-start | bytes 73736 | tf_op jit(solution)/shard_map/ppermute | solution.py:27
  306.8 13.8 %collective-permute-start.25 = (f32[1,1,4,6,256]{4,1,2,3,0:T(1,128)S(1)}, f32[1,1,4,6,256]{4,1,2,3,0:T(1,128)S(1)}, u32[]{:S(2)}, u32[]{:S(2)}) collective-permute-start(f32[1,1,4,6,256]{4,1,2,3,0:T(1,128)S(1)} %get-tuple-element.43), channel_id=1, source_target_pairs={{1,0},{2,1},{3,2},{0,3},{5,4},{6,5},{7,6},{4,7},{9,8},{10,9},{11,1... | collective-permute-start | bytes 73736 | tf_op jit(solution)/shard_map/ppermute | solution.py:29
  319.9 3.1 copy-start.3
  323.0 1.9 copy-start.1
  327.0 31.8 %copy-start.4 = (f32[3,64,4,4,256]{4,1,2,3,0:T(8,128)}, f32[3,64,4,4,256]{4,1,2,3,0:T(8,128)S(1)}, u32[]{:S(2)}) copy-start(f32[3,64,4,4,256]{4,1,2,3,0:T(8,128)S(1)} %get-tuple-element.22) | copy-start | bytes 9437188
where the time goes:
time: 427 us; the launch traced here: 419 us
  waiting for transfers between devices  144 us (34%)
  blocking collectives  99.2 us (23%)
  starting transfers between devices  70.2 us (16%)
  matrix products  47.1 us (11%)
  other arithmetic  38.9 us (9%)
  local copies, waits for them, and re-layouts  16.5 us (4%)
    ppermute x13, waiting for transfers between devices, padded_2(): lax.ppermute(tail, axis, [(i, (i + 1) % count) for i in range(ends)])  83.2 us
    all_to_all x2, blocking collectives, transform(): lax.all_to_all(flat, 'gz', split_axis=1, concat_axis=0, tiled=True)  57.1 us
    all_to_all x2, waiting for transfers between devices, turn_modes(): return lax.all_to_all(turned, 'gz', split_axis=0, concat_axis=1, tiled=True)  51 us
    psum x1, blocking collectives, shards(): gram_total, readout = lax.psum((gram_local, readout_local), ('gx', 'gz'))  42.1 us
    ppermute x13, starting transfers between devices, padded_2(): lax.ppermute(head, axis, [((i + 1) % count, i) for i in range(ends)])  39.7 us
    ppermute x13, starting transfers between devices, padded_2(): lax.ppermute(tail, axis, [(i, (i + 1) % count) for i in range(ends)])  22.1 us
    dot_general x1, matrix products, shards(): jnp.einsum('szxy,czjxy->scj', located.astype(jnp.float32), solved, precis...  17.3 us
    div x3, other arithmetic, shards(): (source + viscosity * around_sum(padded) + base_field * padded[:, 1:-1, :...  14.5 us
  transfers between devices with their start and end apart: 28, of which 21 were waited for; matrix products, arithmetic and copies ran while one was open for 0% of the time, Pallas kernels for 0%

commit v1 on v0

--- a/solution.py
+++ b/solution.py
@@ -2,7 +2,10 @@
 
 import jax
 import jax.numpy as jnp
+import numpy as np
 from jax import lax
+from jax.experimental import pallas as pl
+from jax.experimental.pallas import tpu as pltpu
 from jax.sharding import PartitionSpec as P
 
 SWEEPS = 3
@@ -132,6 +135,720 @@
     return (new_factor, new_gain, gram)
 
 
+HALF = 32
+PAIRS = 8
+
+
+def recurrence_tables(centre, weights):
+    ratio = centre / 2.0 - math.sqrt(centre * centre / 4.0 - 1.0)
+    order = len(weights)
+    step = ratio * np.tril(np.ones((order, order)))
+    half = np.linalg.matrix_power(step, HALF)
+    whole = np.linalg.matrix_power(step, 2 * HALF)
+    angles = 2.0 * np.pi * np.arange(4096) / 4096
+    series = [weights[0]]
+    for weight in weights[1:]:
+        longer = [0.0] + [weight * entry for entry in series]
+        for place, entry in enumerate(series):
+            longer[place] += (1.0 - weight) * entry
+        longer[0] += weight
+        series = longer
+    mixes = []
+    for power in range(1, order + 1):
+        symbol = 1.0 / (centre - 2.0 * np.cos(angles)) ** power
+        kernel = [np.mean(symbol * np.cos(angles * n)) for n in range(order + 1)]
+        matrix = [[math.comb(n + i - 1, i - 1) for i in range(1, power + 1)] for n in range(1, power + 1)]
+        sides = np.linalg.solve(
+            np.array(matrix, np.float64), [kernel[n] / ratio**n for n in range(1, power + 1)]
+        )
+        middle = kernel[0] - 2.0 * np.sum(sides)
+        mixes.append([float(series[power - 1] * entry) for entry in [middle, *sides]])
+    return float(ratio), half.tolist(), whole, mixes
+
+
+RATIO, HALF_TABLE, WHOLE_TABLE, MIXES = recurrence_tables(12.0, chebyshev_weights)
+
+
+def lower_half():
+    return lax.broadcasted_iota(jnp.int32, (8, 256), 0) < 4
+
+
+def swap(cells):
+    return pltpu.roll(cells, 4, 0)
+
+
+def below(cells):
+    lanes = lax.broadcasted_iota(jnp.int32, (8, 256), 1)
+    return jnp.where(lanes > 0, pltpu.roll(cells, 1, 1), 0.0)
+
+
+def above(cells):
+    lanes = lax.broadcasted_iota(jnp.int32, (8, 256), 1)
+    return jnp.where(lanes < 255, pltpu.roll(cells, 255, 1), 0.0)
+
+
+def shift_of(index_ref):
+    index = index_ref[0]
+    value = jnp.float32(shift_table[0])
+    for place in range(1, SHIFTS):
+        value = jnp.where(index == place, jnp.float32(shift_table[place]), value)
+    return value
+
+
+def x_odd():
+    return lax.rem(lax.axis_index("gx"), 2)
+
+
+def z_even():
+    return lax.rem(lax.axis_index("gz"), 2) == 0
+
+
+def cascade(state, cells):
+    grown = []
+    for entry in state:
+        cells = RATIO * entry + cells
+        grown.append(cells)
+    return tuple(grown)
+
+
+def half_states(read):
+    zero = jnp.zeros((8, 256), jnp.float32)
+
+    def body(t, carry):
+        forward, backward = carry
+        return cascade(forward, read(t)), cascade(backward, read(HALF - 1 - t))
+
+    return lax.fori_loop(0, HALF, body, ((zero,) * POISSON, (zero,) * POISSON), unroll=8)
+
+
+def turned(table, states, row):
+    total = None
+    for column in range(row + 1):
+        term = table[row][column] * states[column]
+        total = term if total is None else total + term
+    return total
+
+
+FACTOR_AT = 24
+PART = 152
+CORNERS = [(c, dx, side, 0) for c in range(3) for dx in (1, 2) for side in (0, 1)]
+CORNERS += [(2, 1, 0, 1), (2, 3, 0, 0)]
+
+
+def pack_kernel(factor_ref, base_ref, own_ref, a_ref, b1_ref, b2_ref, z1_ref, z2_ref):
+    odd = x_odd()
+    even = 1 - odd
+    low = lax.broadcasted_iota(jnp.int32, (8, 128), 0) < 4
+    scale = -1.0 / viscosity
+    for component in range(3):
+
+        def load(m, _, component=component):
+            for x in range(4):
+                for tile in range(2):
+                    row = (component * 64 + 2 * m) * 32 + tile * 4 + x
+                    first = factor_ref[pl.ds(row, 8, stride=8), :] * scale
+                    second = factor_ref[pl.ds(row + 1024, 8, stride=8), :] * scale
+                    lanes = slice(tile * 128, tile * 128 + 128)
+                    own_ref[component, x, 2 * m, :, lanes] = jnp.where(low, first, swap(second))
+                    own_ref[component, x, 2 * m + 1, :, lanes] = jnp.where(low, swap(first), second)
+            return 0
+
+        lax.fori_loop(0, 16, load, 0)
+
+    def edges(zz, _):
+        for component in range(3):
+            for layer in range(3):
+                at = FACTOR_AT + (component * 3 + layer) * HALF
+                a_ref[at + zz] = own_ref[component, layer + even, zz]
+                cells = own_ref[component, layer + odd, zz]
+                if at < PART:
+                    b1_ref[at + zz] = cells
+                else:
+                    b2_ref[at - PART + zz] = cells
+        return 0
+
+    lax.fori_loop(0, HALF, edges, 0)
+    for layer in range(3):
+        for group in range(8):
+            for tile in range(2):
+                lanes = slice(tile * 128, tile * 128 + 128)
+                row = group * 64 + tile * 4 + layer
+                a_ref[layer * 8 + group, :, lanes] = base_ref[pl.ds(row + even, 8, stride=8), :]
+                b1_ref[layer * 8 + group, :, lanes] = base_ref[pl.ds(row + odd, 8, stride=8), :]
+    lower = lower_half()
+    rightward = z_even()
+    for component in range(3):
+        for x in range(4):
+            for pair in range(2):
+                cells = lambda zz: own_ref[component, x, zz]
+                up = jnp.where(lower, swap(cells(31 - 2 * pair)), cells(30 - 2 * pair))
+                down = jnp.where(lower, cells(2 * pair), swap(cells(2 * pair + 1)))
+                at = (component * 4 + x) * 2 + pair
+                z1_ref[at] = jnp.where(rightward, up, down)
+                z2_ref[at] = jnp.where(rightward, down, up)
+    for k in range(4):
+        for tile in range(2):
+            lanes = slice(tile * 128, tile * 128 + 128)
+            up = base_ref[(63 - k) * 8 + tile * 4 : (63 - k) * 8 + tile * 4 + 4, :]
+            down = base_ref[k * 8 + tile * 4 : k * 8 + tile * 4 + 4, :]
+            rows = slice((k % 2) * 4, (k % 2) * 4 + 4)
+            z1_ref[24 + k // 2, rows, lanes] = jnp.where(rightward, up, down)
+            z2_ref[24 + k // 2, rows, lanes] = jnp.where(rightward, down, up)
+
+
+def corner_kernel(z1_ref, z2_ref, a_ref, b_ref):
+    odd = x_odd()
+    rightward = z_even()
+
+    def fill(behind_ref, ahead_ref):
+        for place, (component, dx, side, pair) in enumerate(CORNERS):
+            source = (behind_ref, ahead_ref)[side]
+            right_x = 4 - dx
+            left_x = dx - 1
+            a_x = jnp.where(odd == 1, left_x, right_x)
+            b_x = jnp.where(odd == 1, right_x, left_x)
+            a_ref[place] = source[(component * 4 + a_x) * 2 + pair]
+            b_ref[place] = source[(component * 4 + b_x) * 2 + pair]
+        for dx in (1, 2, 3):
+            for k in range(4):
+                for side, source in enumerate((behind_ref, ahead_ref)):
+                    from_right = source[24 + k // 2, (k % 2) * 4 + 4 - dx, :]
+                    from_left = source[24 + k // 2, (k % 2) * 4 + dx - 1, :]
+                    at = len(CORNERS) + dx - 1
+                    a_ref[at, side * 4 + k, :] = jnp.where(odd == 1, from_left, from_right)
+                    b_ref[at, side * 4 + k, :] = jnp.where(odd == 1, from_right, from_left)
+
+    @pl.when(rightward)
+    def _():
+        fill(z2_ref, z1_ref)
+
+    @pl.when(jnp.logical_not(rightward))
+    def _():
+        fill(z1_ref, z2_ref)
+
+
+def velocity_kernel(
+    index_ref, own_ref, base_ref, a_ref, b1_ref, b3_ref, b2_ref, ca_ref, cb_ref, z1_ref, z2_ref,
+    v_ref, bw_ref, s_ref,
+    flow_ref, a1_ref, r_ref, v0_ref, va_ref, vb_ref,
+):
+    odd = x_odd()
+    stream = lax.axis_index("gx")
+    last = lax.axis_size("gx") - 1
+    mask_left = jnp.where(stream > 0, 1.0, 0.0)
+    mask_right = jnp.where(stream < last, 1.0, 0.0)
+    relayed = jnp.logical_or(stream == 3, stream == 4)
+    rightward = z_even()
+    lower = lower_half()
+    shift = shift_of(index_ref)
+
+    def each_z(step):
+        @pl.when(rightward)
+        def _():
+            step(z2_ref, z1_ref)
+
+        @pl.when(jnp.logical_not(rightward))
+        def _():
+            step(z1_ref, z2_ref)
+
+    def inside(at):
+        return lambda zz: a_ref[at + zz]
+
+    def outside(first_ref):
+        def pick(at):
+            if at < PART:
+                return lambda zz: first_ref[at + zz]
+            return lambda zz: b2_ref[at - PART + zz]
+
+        return pick
+
+    def each_x(step):
+        @pl.when(jnp.logical_and(odd == 0, relayed))
+        def _():
+            step(outside(b3_ref), cb_ref, inside, ca_ref)
+
+        @pl.when(jnp.logical_and(odd == 0, jnp.logical_not(relayed)))
+        def _():
+            step(outside(b1_ref), cb_ref, inside, ca_ref)
+
+        @pl.when(jnp.logical_and(odd == 1, relayed))
+        def _():
+            step(inside, ca_ref, outside(b3_ref), cb_ref)
+
+        @pl.when(jnp.logical_and(odd == 1, jnp.logical_not(relayed)))
+        def _():
+            step(inside, ca_ref, outside(b1_ref), cb_ref)
+
+    for x in range(4):
+        for group in range(8):
+            for tile in range(2):
+                lanes = slice(tile * 128, tile * 128 + 128)
+                flow_ref[x + 3, 8 + 8 * group : 16 + 8 * group, lanes] = base_ref[
+                    pl.ds(group * 64 + tile * 4 + x, 8, stride=8), :
+                ]
+
+    def flow_span(behind_ref, ahead_ref):
+        for x in range(4):
+            for k in range(4):
+                at = 24 + k // 2
+                row = (k % 2) * 4 + x
+                flow_ref[x + 3, 7 - k, :] = behind_ref[at, row, :]
+                flow_ref[x + 3, 72 + k, :] = ahead_ref[at, row, :]
+
+    each_z(flow_span)
+
+    def flow_stream(left, left_corner, right, right_corner):
+        for dx in (1, 2, 3):
+            for place, layer, read, corner in (
+                (3 - dx, 3 - dx, left, left_corner),
+                (6 + dx, dx - 1, right, right_corner),
+            ):
+                for group in range(8):
+                    flow_ref[place, 8 + 8 * group : 16 + 8 * group, :] = read(layer * 8)(group)
+                for k in range(4):
+                    flow_ref[place, 7 - k, :] = corner[len(CORNERS) + dx - 1, k, :]
+                    flow_ref[place, 72 + k, :] = corner[len(CORNERS) + dx - 1, 4 + k, :]
+
+    each_x(flow_stream)
+
+    def coefficients(zz, _):
+        for x in range(10):
+            first = jnp.broadcast_to(flow_ref[x, pl.ds(zz + 4, 1), :], (8, 256))
+            second = jnp.broadcast_to(flow_ref[x, pl.ds(zz + 36, 1), :], (8, 256))
+            flow = jnp.where(lower, first, second)
+            scale = viscosity * (mask_left if x < 3 else mask_right if x > 6 else 1.0)
+            a1_ref[x, zz] = scale / (shift + 6.0 * viscosity + flow)
+            r_ref[x, zz] = 1.0 + flow * (1.0 / viscosity)
+        return 0
+
+    lax.fori_loop(0, 39, coefficients, 0)
+    zero = jnp.zeros((8, 256), jnp.float32)
+    for x in (0, 1, 2, 7, 8, 9):
+        for zz in (0, 1, 2, 3, 36, 37, 38):
+            v0_ref[x, zz] = zero
+
+    def sweep(source, target, margin):
+        def body(zz, _):
+            layers = {x: source[x, zz] for x in range(2 - margin, 8 + margin)}
+            for x in range(3 - margin, 7 + margin):
+                centre = layers[x]
+                total = layers[x + 1] + (below(centre) + above(centre))
+                total = total + (source[x, zz + 1] + source[x, zz - 1])
+                target[x, zz] = v0_ref[x, zz] + a1_ref[x, zz] * (total + r_ref[x, zz] * layers[x - 1])
+            return 0
+
+        lax.fori_loop(3 - margin, 36 + margin, body, 0)
+
+    for component in range(3):
+
+        def interior(zz, _, component=component):
+            for x in range(4):
+                v0_ref[x + 3, zz + 4] = own_ref[component, x, zz] * a1_ref[x + 3, zz + 4]
+            return 0
+
+        lax.fori_loop(0, HALF, interior, 0)
+
+        def before(cells, halo, k):
+            if k % 2 == 0:
+                return jnp.where(lower, halo, swap(cells))
+            return swap(jnp.where(lower, cells, halo))
+
+        def after(cells, halo, k):
+            if k % 2 == 0:
+                return swap(jnp.where(lower, halo, cells))
+            return jnp.where(lower, swap(cells), halo)
+
+        def span(behind_ref, ahead_ref, component=component):
+            for x in range(4):
+                at = (component * 4 + x) * 2
+                for k in range(4):
+                    cells = before(own_ref[component, x, 31 - k], behind_ref[at + k // 2], k)
+                    v0_ref[x + 3, 3 - k] = cells * a1_ref[x + 3, 3 - k]
+                for k in range(3):
+                    cells = after(own_ref[component, x, k], ahead_ref[at + k // 2], k)
+                    v0_ref[x + 3, 36 + k] = cells * a1_ref[x + 3, 36 + k]
+
+        each_z(span)
+
+        def sides(left, left_corner, right, right_corner, component=component):
+            for dx in (1, 2, 3):
+                for place, layer, pick, corner in (
+                    (3 - dx, 3 - dx, left, left_corner),
+                    (6 + dx, dx - 1, right, right_corner),
+                ):
+                    read = pick(FACTOR_AT + (component * 3 + layer) * HALF)
+
+                    def body(zz, _, read=read, place=place):
+                        v0_ref[place, zz + 4] = read(zz) * a1_ref[place, zz + 4]
+                        return 0
+
+                    lax.fori_loop(0, HALF, body, 0, unroll=4)
+                    for entry, (c, away, side, pair) in enumerate(CORNERS):
+                        if c != component or away != dx:
+                            continue
+                        for k in (2 * pair, 2 * pair + 1):
+                            if side == 0:
+                                cells = before(read(31 - k), corner[entry], k)
+                                v0_ref[place, 3 - k] = cells * a1_ref[place, 3 - k]
+                            else:
+                                cells = after(read(k), corner[entry], k)
+                                v0_ref[place, 36 + k] = cells * a1_ref[place, 36 + k]
+
+        each_x(sides)
+        sweep(v0_ref, va_ref, 2)
+        sweep(va_ref, vb_ref, 1)
+        sweep(vb_ref, va_ref, 0)
+
+        def diverge(zz, _, component=component):
+            for x in range(4):
+                cells = va_ref[x + 3, zz + 4]
+                v_ref[component, x, zz] = cells
+                if component == 0:
+                    inner = cells if x == 0 else cells - va_ref[x + 2, zz + 4]
+                    bw_ref[x, zz] = -2.0 * inner
+                elif component == 1:
+                    bw_ref[x, zz] = bw_ref[x, zz] - (cells - below(cells))
+                else:
+                    bw_ref[x, zz] = bw_ref[x, zz] - (cells - va_ref[x + 3, zz + 3])
+            if component == 0:
+                bw_ref[4, zz] = va_ref[6, zz + 4]
+            return 0
+
+        lax.fori_loop(0, HALF, diverge, 0)
+
+    def states(layer, _):
+        forward, backward = half_states(lambda t: bw_ref[layer, t])
+        swapped_forward = [swap(entry) for entry in forward]
+        swapped_backward = [swap(entry) for entry in backward]
+        for i in range(POISSON):
+            onward = forward[i] + turned(HALF_TABLE, swapped_forward, i)
+            back = backward[i] + turned(HALF_TABLE, swapped_backward, i)
+            s_ref[i, layer] = jnp.where(lower, back, onward)
+        s_ref[POISSON, layer] = bw_ref[layer, 0]
+        return 0
+
+    lax.fori_loop(0, 5, states, 0)
+
+
+def pressure_kernel(
+    index_ref, cells_ref, v_ref, bw_ref, ba_ref, bb_ref, inc_ref, ia_ref, ib_ref, factor_ref,
+    nf_ref, solved_ref, sums_ref,
+    f_ref, i_ref, u_ref, q_ref, t_ref,
+):
+    odd = x_odd()
+    stream = lax.axis_index("gx")
+    span = lax.axis_index("gz")
+    last = lax.axis_size("gx") - 1
+    mask_left = jnp.where(stream > 0, 1.0, 0.0)
+    mask_right = jnp.where(stream < last, 1.0, 0.0)
+    lower = lower_half()
+    shift = shift_of(index_ref)
+
+    def gather(left_ref, right_ref, left_inc, right_inc):
+        def body(zz, _):
+            for x in range(3):
+                f_ref[x, zz] = left_ref[x, zz]
+                f_ref[x + 4, zz] = bw_ref[x + 1, zz]
+                f_ref[x + 8, zz] = right_ref[x + 1, zz]
+            f_ref[3, zz] = bw_ref[0, zz] + 2.0 * left_ref[3, zz]
+            f_ref[7, zz] = mask_right * (right_ref[0, zz] + 2.0 * bw_ref[4, zz])
+            return 0
+
+        lax.fori_loop(0, HALF, body, 0)
+        for i in range(POISSON + 1):
+            for x in range(3):
+                i_ref[i, x] = left_inc[i, x]
+                i_ref[i, x + 4] = inc_ref[i, x + 1]
+                i_ref[i, x + 8] = right_inc[i, x + 1]
+            i_ref[i, 3] = inc_ref[i, 0] + 2.0 * left_inc[i, 3]
+            i_ref[i, 7] = mask_right * (right_inc[i, 0] + 2.0 * inc_ref[i, 4])
+        for x in range(11):
+            f_ref[x, HALF] = swap(jnp.where(lower, i_ref[POISSON, x], f_ref[x, 0]))
+
+    @pl.when(odd == 0)
+    def _():
+        gather(bb_ref, ba_ref, ib_ref, ia_ref)
+
+    @pl.when(odd == 1)
+    def _():
+        gather(ba_ref, bb_ref, ia_ref, ib_ref)
+
+    def solve(x, _):
+        forward, backward = half_states(lambda t: f_ref[x, t])
+        arriving = [i_ref[i, x] for i in range(POISSON)]
+        swapped = [swap(entry) for entry in arriving]
+        onward = []
+        back = []
+        for i in range(POISSON):
+            carried = turned(HALF_TABLE, swapped, i)
+            onward.append(swap(jnp.where(lower, forward[i] + carried, arriving[i])))
+            back.append(swap(jnp.where(lower, arriving[i], backward[i] + carried)))
+
+        def ahead(zz, state):
+            state = cascade(state, f_ref[x, zz])
+            for i in range(POISSON):
+                u_ref[i, zz] = state[i]
+            return state
+
+        lax.fori_loop(0, HALF, ahead, tuple(onward), unroll=8)
+        end = cascade([u_ref[i, HALF - 1] for i in range(POISSON)], f_ref[x, HALF])
+        for i in range(POISSON):
+            u_ref[i, HALF] = end[i]
+
+        def mix(zz, state):
+            both = [f_ref[x, zz]] + [u_ref[i, zz] + state[i] for i in range(POISSON)]
+            for power in range(POISSON):
+                total = MIXES[power][0] * both[0]
+                for i in range(1, power + 2):
+                    total = total + MIXES[power][i] * both[i]
+                q_ref[power, x, zz] = total
+
+        mix(HALF, back)
+
+        def behind(t, state):
+            zz = HALF - 1 - t
+            state = cascade(state, f_ref[x, zz])
+            mix(zz, state)
+            return state
+
+        lax.fori_loop(0, HALF, behind, tuple(back), unroll=8)
+        return 0
+
+    lax.fori_loop(0, 11, solve, 0)
+    for power in (2, 1, 0):
+
+        def apply(zz, _, power=power):
+            edge = 2 - power
+            layers = {x: q_ref[power + 1, x, zz] for x in range(edge, 11 - edge)}
+            for x in range(edge + 1, 10 - edge if power else 8):
+                beside = 4.0 * (layers[x - 1] + layers[x + 1]) + (below(layers[x]) + above(layers[x]))
+                if x < 3:
+                    beside = mask_left * beside
+                if x > 6:
+                    beside = mask_right * beside
+                q_ref[power, x, zz] = q_ref[power, x, zz] + beside
+            return 0
+
+        lax.fori_loop(0, HALF + 1, apply, 0)
+
+    def correct(m, _):
+        for x in range(4):
+            pair = []
+            for zz in (2 * m, 2 * m + 1):
+                centre = q_ref[0, x + 3, zz]
+                pair.append(
+                    (
+                        v_ref[0, x, zz] - 2.0 * (q_ref[0, x + 4, zz] - centre),
+                        v_ref[1, x, zz] - (above(centre) - centre),
+                        v_ref[2, x, zz] - (q_ref[0, x + 3, zz + 1] - centre),
+                    )
+                )
+            for component in range(3):
+                first, second = pair[0][component], pair[1][component]
+                early = jnp.where(lower, first, swap(second))
+                late = jnp.where(lower, swap(first), second)
+                for tile in range(2):
+                    row = (component * 64 + 2 * m) * 32 + tile * 4 + x
+                    lanes = slice(tile * 128, tile * 128 + 128)
+                    solved_ref[pl.ds(row, 8, stride=8), :] = early[:, lanes]
+                    solved_ref[pl.ds(row + 1024, 8, stride=8), :] = late[:, lanes]
+        return 0
+
+    lax.fori_loop(0, 16, correct, 0)
+    couples = [(i, j) for i in range(4) for j in range(i, 4)]
+
+    def update(block, sums):
+        columns = []
+        for i in range(4):
+            rows = pl.ds(pl.multiple_of(block * 32 + 8 * i, 8), 8)
+            cells = factor_ref[rows, :] + (2.0 * shift) * solved_ref[rows, :]
+            nf_ref[rows, :] = cells
+            columns.append(cells)
+        return tuple(s + columns[i] * columns[j] for s, (i, j) in zip(sums, couples))
+
+    zero = jnp.zeros((8, 128), jnp.float32)
+    sums = lax.fori_loop(0, 192, update, (zero,) * len(couples), unroll=4)
+    t_ref[...] = jnp.zeros((32, 128), jnp.float32)
+    for total, (i, j) in zip(sums, couples):
+        t_ref[4 * i + j : 4 * i + j + 1, :] = jnp.sum(total, axis=0, keepdims=True)
+    lanes = lax.broadcasted_iota(jnp.int32, (1, 128), 1)
+    for sensor in range(4):
+        component = cells_ref[sensor, 0]
+        z = cells_ref[sensor, 1] - span * 64
+        x = cells_ref[sensor, 2] - stream * 4
+        y = cells_ref[sensor, 3]
+        held = (z >= 0) & (z < 64) & (x >= 0) & (x < 4)
+        z = jnp.clip(z, 0, 63)
+        x = jnp.clip(x, 0, 3)
+        tile = jnp.where(y >= 128, 1, 0)
+        lane = jnp.where(held, y - 128 * tile, -1)
+        for column in range(4):
+            row = (component * 64 + z) * 32 + column * 8 + tile * 4 + x
+            cells = solved_ref[pl.ds(row, 1), :]
+            at = 16 + 4 * sensor + column
+            t_ref[at : at + 1, :] = jnp.where(lanes == lane, cells, 0.0)
+    totals = jnp.sum(t_ref[...], axis=1, keepdims=True)
+    spread = lax.broadcasted_iota(jnp.int32, (32, 128), 1) == lax.broadcasted_iota(jnp.int32, (32, 128), 0)
+    sums_ref[...] = jnp.sum(jnp.where(spread, totals, 0.0), axis=0, keepdims=True)
+
+
+def gain_kernel(index_ref, sums_ref, gain_ref, solved_ref, out_ref, gram_ref, c_ref):
+    @pl.when(pl.program_id(0) == 0)
+    def _():
+        totals = jnp.sum(sums_ref[...], axis=0, keepdims=True)
+        lanes = lax.broadcasted_iota(jnp.int32, (1, 128), 1)
+        shift = shift_of(index_ref)
+        for i in range(4):
+            for j in range(4):
+                c_ref[i, j] = 2.0 * shift * jnp.sum(jnp.where(lanes == 16 + 4 * i + j, totals, 0.0))
+                at = 4 * min(i, j) + max(i, j)
+                gram_ref[i, j] = jnp.sum(jnp.where(lanes == at, totals, 0.0)) / 6291456.0
+
+    table = [[c_ref[i, j] for j in range(4)] for i in range(4)]
+
+    def body(block, _):
+        rows = [pl.ds(pl.multiple_of(block * 32 + 8 * j, 8), 8) for j in range(4)]
+        columns = [solved_ref[rows[j], :] for j in range(4)]
+        for i in range(4):
+            total = gain_ref[rows[i], :]
+            for j in range(4):
+                total = total + table[i][j] * columns[j]
+            out_ref[rows[i], :] = total
+        return 0
+
+    lax.fori_loop(0, out_ref.shape[0] // 32, body, 0, unroll=2)
+
+
+def call(kernel, outputs, scratch, operands, smalls, flops):
+    arrays = [jax.ShapeDtypeStruct(shape, jnp.float32) for shape in outputs]
+    places = [pl.BlockSpec(memory_space=pltpu.SMEM)] * smalls
+    places += [pl.BlockSpec(memory_space=pltpu.VMEM)] * (len(operands) - smalls)
+    moved = sum(4 * math.prod(shape) for shape in outputs) + sum(4 * math.prod(o.shape) for o in operands)
+    return pl.pallas_call(
+        kernel,
+        out_shape=arrays,
+        in_specs=places,
+        out_specs=[pl.BlockSpec(memory_space=pltpu.VMEM)] * len(outputs),
+        scratch_shapes=[pltpu.VMEM(shape, jnp.float32) for shape in scratch],
+        compiler_params=pltpu.CompilerParams(vmem_limit_bytes=56 << 20),
+        cost_estimate=pl.CostEstimate(flops=flops, bytes_accessed=moved, transcendentals=0),
+    )(*operands)
+
+
+def to_rows(cells):
+    head = cells.shape[:-2]
+    order = tuple(range(len(head)))
+    split = cells.reshape(*head, 4, 2, 128).transpose(*order, len(head) + 1, len(head), len(head) + 2)
+    return split.reshape(-1, 128)
+
+
+def from_rows(rows, head):
+    order = tuple(range(len(head)))
+    split = rows.reshape(*head, 2, 4, 128).transpose(*order, len(head) + 1, len(head), len(head) + 2)
+    return split.reshape(*head, 4, 256)
+
+
+def mixed(table, states):
+    table = np.asarray(table).astype(np.float32)
+    return jnp.stack(
+        [sum(float(table[i, k]) * states[k] for k in range(i + 1)) for i in range(POISSON)]
+    )
+
+
+def ring_states(states, own_even):
+    near = [(0, 1), (1, 0), (2, 3), (3, 2)]
+    far = [(1, 2), (2, 1), (3, 0), (0, 3)]
+    upper = jnp.arange(8)[None, None, :, None] >= 4
+    partner = lax.ppermute(states, "gz", near)
+    first = upper == own_even
+    nearer = jnp.where(first, partner, states)
+    farther = jnp.where(first, states, partner)
+    joined = nearer[:POISSON] + mixed(WHOLE_TABLE, farther[:POISSON])
+    other = lax.ppermute(jnp.concatenate([joined, states[POISSON:]]), "gz", far)
+    square = WHOLE_TABLE @ WHOLE_TABLE
+    cube = square @ WHOLE_TABLE
+    around = np.linalg.inv(np.eye(POISSON) - square @ square)
+    entering = jnp.where(
+        first[0],
+        other[:POISSON] + mixed(square, partner[:POISSON]),
+        partner[:POISSON] + mixed(WHOLE_TABLE, other[:POISSON]),
+    )
+    entering = entering + mixed(cube, states[:POISSON])
+    entering = mixed(around, entering)
+    ahead = jnp.where(own_even, partner[POISSON:], other[POISSON:])
+    return jnp.concatenate([entering, ahead])
+
+
+def fast_shards(factor, gain, base_flow, shift_index, sensor_cells):
+    swap_in = [(0, 1), (1, 0), (2, 3), (3, 2), (4, 5), (5, 4), (6, 7), (7, 6)]
+    swap_out = [(1, 2), (2, 1), (3, 4), (4, 3), (5, 6), (6, 5)]
+    send_round = [(1, 2), (2, 1), (5, 6), (6, 5), (3, 7), (4, 0)]
+    forward_round = [(7, 4), (0, 3)]
+    near = [(0, 1), (1, 0), (2, 3), (3, 2)]
+    far = [(1, 2), (2, 1), (3, 0), (0, 3)]
+    odd = lax.axis_index("gx") % 2
+    own_even = lax.axis_index("gz") % 2 == 0
+    factor_rows = to_rows(factor)
+    base_rows = to_rows(base_flow)
+    gain_rows = to_rows(gain)
+    cell = (8, 256)
+    own, a, b1, b2, z1, z2 = call(
+        pack_kernel,
+        [(3, 4, HALF, *cell), (312, *cell), (PART, *cell), (312 - PART, *cell), (26, *cell), (26, *cell)],
+        [], [factor_rows, base_rows], 0, 10**6,
+    )
+    b1_in = lax.ppermute(b1, "gx", send_round)
+    z1 = lax.ppermute(z1, "gz", near)
+    z2 = lax.ppermute(z2, "gz", far)
+    b2_in = lax.ppermute(b2, "gx", swap_out)
+    a_in = lax.ppermute(a, "gx", swap_in)
+    corners = len(CORNERS) + 3
+    ca, cb = call(corner_kernel, [(corners, *cell)] * 2, [], [z1, z2], 0, 10**5)
+    ca = lax.ppermute(ca, "gx", swap_in)
+    cb = lax.ppermute(cb, "gx", swap_out)
+    b3_in = lax.ppermute(b1_in, "gx", forward_round)
+    block = (10, 39, *cell)
+    velocity, sides, states = call(
+        velocity_kernel,
+        [(3, 4, HALF, *cell), (5, HALF, *cell), (POISSON + 1, 5, *cell)],
+        [(10, 80, 256)] + [block] * 5,
+        [shift_index, own, base_rows, a_in, b1_in, b3_in, b2_in, ca, cb, z1, z2], 1, 10**8,
+    )
+    side_b = lax.ppermute(lax.dynamic_slice_in_dim(sides, odd, 4, axis=0), "gx", swap_out)
+    side_a = lax.ppermute(lax.dynamic_slice_in_dim(sides, 1 - odd, 4, axis=0), "gx", swap_in)
+    entering = ring_states(states, own_even)
+    enter_b = lax.ppermute(lax.dynamic_slice_in_dim(entering, odd, 4, axis=1), "gx", swap_out)
+    enter_a = lax.ppermute(lax.dynamic_slice_in_dim(entering, 1 - odd, 4, axis=1), "gx", swap_in)
+    block = (11, HALF + 1, *cell)
+    new_rows, solved, sums = call(
+        pressure_kernel,
+        [factor_rows.shape, factor_rows.shape, (1, 128)],
+        [block, (POISSON + 1, 11, *cell), (POISSON, HALF + 1, *cell), (POISSON, *block), (32, 128)],
+        [shift_index, sensor_cells, velocity, sides, side_a, side_b, entering, enter_a, enter_b, factor_rows],
+        2, 10**8,
+    )
+    devices = lax.axis_size("gx") * lax.axis_size("gz")
+    shared = lax.all_to_all(
+        jnp.broadcast_to(sums[None], (devices, 1, 128)), ("gx", "gz"), split_axis=0, concat_axis=0, tiled=True
+    )
+    chunk = 768
+    whole = pl.BlockSpec(memory_space=pltpu.SMEM)
+    rows = pl.BlockSpec((chunk, 128), lambda i: (i, 0))
+    new_gain, gram = pl.pallas_call(
+        gain_kernel,
+        grid=(gain_rows.shape[0] // chunk,),
+        in_specs=[whole, pl.BlockSpec((devices, 128), lambda i: (0, 0)), rows, rows],
+        out_specs=[rows, whole],
+        out_shape=[
+            jax.ShapeDtypeStruct(gain_rows.shape, jnp.float32),
+            jax.ShapeDtypeStruct((4, 4), jnp.float32),
+        ],
+        scratch_shapes=[pltpu.SMEM((4, 4), jnp.float32)],
+    )(shift_index, shared.reshape(devices, 128), gain_rows, solved)
+    head = factor.shape[:3]
+    return (from_rows(new_rows, head), from_rows(new_gain, head), gram)
+
+
 def solution(mesh):
     placed = (
         P(None, "gz", None, "gx", None),
@@ -140,8 +857,9 @@
         P(),
         P(),
     )
+    fits = mesh.shape["gx"] == 8 and mesh.shape["gz"] == 4
     return jax.shard_map(
-        shards,
+        fast_shards if fits else shards,
         mesh=mesh,
         in_specs=placed,
         out_specs=(P(None, "gz", None, "gx", None), P(None, "gz", None, "gx", None), P()),

time: 427 us -> 188 us (0.44); the launches traced: 419 us -> 187 us
  waiting for transfers between devices: 144 us -> 34.1 us
  Pallas kernels: 0 us -> 88.6 us
  blocking collectives: 99.2 us -> 23.3 us
  matrix products: 47.1 us -> 0 us
  other arithmetic: 38.9 us -> 0.42 us
  starting transfers between devices: 70.2 us -> 33.3 us
  local copies, waits for them, and re-layouts: 16.5 us -> 6.02 us
    pallas_call x0 -> x5, Pallas kernels: none -> 88.6 us  [the longest x4 81.1 us: call(): pl.pallas_call(kernel, out_shape=arrays, in_specs=places, out_specs=[pl.B...]
    ppermute x26 -> x14, waiting for transfers between devices: 92.6 us -> 34.1 us  [the longest x1 16.1 us: fast_shards(): b1_in = lax.ppermute(b1, 'gx', send_round)]
    all_to_all x2 -> x0, waiting for transfers between devices: 51 us -> none  [turn_modes(): return lax.all_to_all(turned, 'gz', split_axis=0, concat_axis=1, tiled=True)]
    dot_general x5 -> x0, matrix products: 47.1 us -> none  [the longest x1 17.3 us: shards(): jnp.einsum('szxy,czjxy->scj', located.astype(jnp.float32), solved, precis...]
    psum x1 -> x0, blocking collectives: 42.1 us -> none  [shards(): gram_total, readout = lax.psum((gram_local, readout_local), ('gx', 'gz'))]
    all_to_all x2 -> x1, blocking collectives: 57.1 us -> 23.3 us  [fast_shards(): lax.all_to_all(jnp.broadcast_to(sums[None], (devices, 1, 128)), ('gx', 'g...]
    ppermute x26 -> x14, starting transfers between devices: 61.8 us -> 33.3 us  [the longest x1 7.46 us: fast_shards(): ca = lax.ppermute(ca, 'gx', swap_in)]
    div x6 -> x0, other arithmetic: 19.1 us -> none  [the longest x3 14.5 us: shards(): (source + viscosity * around_sum(padded) + base_field * padded[:, 1:-1, :...]
  transfers between devices with their start and end apart: 28 -> 14, of which waited for: 21 -> 7; matrix products, arithmetic and copies ran while one was open for 0% -> 0% of each run, Pallas kernels for 0% -> 1%
where the time goes in v1:
time: 188 us; the launch traced here: 187 us
  Pallas kernels  88.6 us (47%)
  waiting for transfers between devices  34.1 us (18%)
  starting transfers between devices  33.3 us (18%)
  blocking collectives  23.3 us (12%)
  local copies, waits for them, and re-layouts  6.02 us (3%)
    pallas_call x4, Pallas kernels, call(): pl.pallas_call(kernel, out_shape=arrays, in_specs=places, out_specs=[pl.B...  81.1 us
    all_to_all x1, blocking collectives, fast_shards(): lax.all_to_all(jnp.broadcast_to(sums[None], (devices, 1, 128)), ('gx', 'g...  23.3 us
    ppermute x1, waiting for transfers between devices, fast_shards(): b1_in = lax.ppermute(b1, 'gx', send_round)  16.1 us
    pallas_call x1, Pallas kernels, fast_shards(): pl.pallas_call(gain_kernel, grid=(gain_rows.shape[0] // chunk,), in_specs...  7.48 us
    ppermute x1, starting transfers between devices, fast_shards(): ca = lax.ppermute(ca, 'gx', swap_in)  7.46 us
    ppermute x1, waiting for transfers between devices, ring_states(): other = lax.ppermute(jnp.concatenate([joined, states[POISSON:]]), 'gz', far)  6 us
    ppermute x1, starting transfers between devices, ring_states(): other = lax.ppermute(jnp.concatenate([joined, states[POISSON:]]), 'gz', far)  5.51 us
    ppermute x1, starting transfers between devices, fast_shards(): lax.ppermute(lax.dynamic_slice_in_dim(sides, 1 - odd, 4, axis=0), 'gx', s...  4.55 us
  transfers between devices with their start and end apart: 14, of which 7 were waited for; matrix products, arithmetic and copies ran while one was open for 0% of the time, Pallas kernels for 1%

profile of v1, /device:TPU:0, one launch (start us, length us, event | category | flops | bytes accessed | tf_op | source)
XLA Modules:
  0.0 187.2 jit_solution(15200026926025234487)
XLA Ops:
  0.6 6.7 %shard_map.76 = (f32[3,4,32,8,256]{4,3,2,1,0:T(8,128)}, f32[312,8,256]{2,1,0:T(8,128)}, f32[152,8,256]{2,1,0:T(8,128)}, f32[160,8,256]{2,1,0:T(8,128)}, f32[26,8,256]{2,1,0:T(8,128)}, /*index=5*/f32[26,8,256]{2,1,0:T(8,128)}) custom-call(f32[6144,128]{1,0:T(8,128)} %bitcast.27, f32[512,128]{1,0:T(8,128)} %bitcast.30), custom_call_target="tpu_custom_call" | custom-call | flops 1000000 | bytes 12091392 | tf_op jit(solution)/shard_map/pallas_call | solution.py:727
  7.3 0.5 collective-permute-start
  7.8 1.3 collective-permute-start.1
  9.1 1.7 collective-permute-start.3
  10.8 16.1 %collective-permute-done.1.b1_ref = f32[152,8,256]{2,1,0:T(8,128)} collective-permute-done((f32[152,8,256]{2,1,0:T(8,128)}, f32[152,8,256]{2,1,0:T(8,128)}, u32[]{:S(2)}, u32[]{:S(2)}) %collective-permute-start.1) | collective-permute-done | bytes 1245216 | tf_op jit(solution)/shard_map/ppermute | solution.py:800
  26.9 3.8 %collective-permute-start.2 = (f32[152,8,256]{2,1,0:T(8,128)}, f32[152,8,256]{2,1,0:T(8,128)}, u32[]{:S(2)}, u32[]{:S(2)}) collective-permute-start(f32[152,8,256]{2,1,0:T(8,128)} %collective-permute-done.1.b1_ref), channel_id=1, source_target_pairs={{28,16},{0,12},{29,17},{1,13},{30,18},{2,14},{31,19},{3,15}} | collective-permute-start | bytes 3735560 | tf_op jit(solution)/shard_map/ppermute | solution.py:809
  30.7 1.6 collective-permute-start.4
  32.3 2.5 %collective-permute-start.5 = (f32[26,8,256]{2,1,0:T(8,128)}, f32[26,8,256]{2,1,0:T(8,128)S(1)}, u32[]{:S(2)}, u32[]{:S(2)}) collective-permute-start(f32[26,8,256]{2,1,0:T(8,128)} %get-tuple-element.24), channel_id=1, source_target_pairs={{1,2},{2,1},{3,0},{0,3},{5,6},{6,5},{7,4},{4,7},{9,10},{10,9},{11,... | collective-permute-start | bytes 638984 | tf_op jit(solution)/shard_map/ppermute | solution.py:802
  34.8 2.0 %collective-permute-done.4.z1_ref = f32[26,8,256]{2,1,0:T(8,128)S(1)} collective-permute-done((f32[26,8,256]{2,1,0:T(8,128)}, f32[26,8,256]{2,1,0:T(8,128)S(1)}, u32[]{:S(2)}, u32[]{:S(2)}) %collective-permute-start.4) | collective-permute-done | bytes 213024 | tf_op jit(solution)/shard_map/ppermute | solution.py:801
  36.8 0.0 copy-start.5
  36.8 4.4 %collective-permute-done.5.z2_ref = f32[26,8,256]{2,1,0:T(8,128)S(1)} collective-permute-done((f32[26,8,256]{2,1,0:T(8,128)}, f32[26,8,256]{2,1,0:T(8,128)S(1)}, u32[]{:S(2)}, u32[]{:S(2)}) %collective-permute-start.5) | collective-permute-done | bytes 213024 | tf_op jit(solution)/shard_map/ppermute | solution.py:802
  41.2 0.0 copy-done.5
  41.2 0.0 copy-start.6
  41.2 0.7 copy-done.6
  41.9 1.8 shard_map.77
  43.7 7.5 %collective-permute-start.6 = (f32[17,8,256]{2,1,0:T(8,128)}, f32[17,8,256]{2,1,0:T(8,128)S(1)}, u32[]{:S(2)}, u32[]{:S(2)}) collective-permute-start(f32[17,8,256]{2,1,0:T(8,128)} %get-tuple-element.25), channel_id=1, source_target_pairs={{0,4},{4,0},{8,12},{12,8},{16,20},{20,16},{24,28},{28,24},{1,5},{5... | collective-permute-start | bytes 417800 | tf_op jit(solution)/shard_map/ppermute | solution.py:807
  51.1 0.7 collective-permute-start.7
  52.5 0.0 collective-permute-done.6.ca_ref
  52.5 0.0 copy-start.9
  52.5 0.0 collective-permute-done.7.cb_ref
  52.5 0.0 copy-start.10
  52.5 0.0 collective-permute-done.3.b2_ref
  52.5 1.2 collective-permute-done.2.b3_ref
  53.7 0.0 collective-permute-done.a_ref
  53.7 0.0 copy-start
  53.7 0.0 copy-done.9
  53.7 0.0 copy-done.10
  53.7 1.5 copy-done
  55.2 45.7 %shard_map.78 = (f32[3,4,32,8,256]{4,3,2,1,0:T(8,128)}, f32[5,32,8,256]{3,2,1,0:T(8,128)}, f32[5,5,8,256]{3,2,1,0:T(8,128)}) custom-call(s32[1]{0:T(128)S(6)} %copy.22.index_ref, f32[3,4,32,8,256]{4,3,2,1,0:T(8,128)} %get-tuple-element.19.own_ref, f32[512,128]{1,0:T(8,128)} %bitcast.31, f32[312,8,256]{2,1,0:T(8,128)} %copy-done, ...), custom_call_target="tpu_custom_call" | custom-call | flops 100000000 | bytes 15130628 | tf_op jit(solution)/shard_map/pallas_call | solution.py:727
  100.9 0.0 copy-start.2
  100.9 1.7 constant_dynamic-slice_fusion.2
  102.6 4.6 %collective-permute-start.8 = (f32[4,32,8,256]{3,2,1,0:T(8,128)S(1)}, f32[4,32,8,256]{3,2,1,0:T(8,128)S(1)}, u32[]{:S(2)}, u32[]{:S(2)}) collective-permute-start(f32[4,32,8,256]{3,2,1,0:T(8,128)S(1)} %get-tuple-element.48), channel_id=1, source_target_pairs={{0,4},{4,0},{8,12},{12,8},{16,20},{20,16},{24,28},{28,24},{1,5},{5... | collective-permute-start | bytes 3145736 | tf_op jit(solution)/shard_map/ppermute | solution.py:818
  107.2 0.7 collective-permute-start.9
  107.9 0.0 copy-done.2
  107.9 2.3 %collective-permute-start.10 = (f32[5,5,8,256]{3,2,1,0:T(8,128)S(1)}, f32[5,5,8,256]{3,2,1,0:T(8,128)S(1)}, u32[]{:S(2)}, u32[]{:S(2)}) collective-permute-start(f32[5,5,8,256]{3,2,1,0:T(8,128)S(1)} %copy-done.2), channel_id=1, source_target_pairs={{0,1},{1,0},{2,3},{3,2},{4,5},{5,4},{6,7},{7,6},{8,9},{9,8},{10,11... | collective-permute-start | bytes 614408 | tf_op jit(solution)/shard_map/ppermute | solution.py:762
  110.2 3.7 %collective-permute-done.10 = f32[5,5,8,256]{3,2,1,0:T(8,128)S(1)} collective-permute-done((f32[5,5,8,256]{3,2,1,0:T(8,128)S(1)}, f32[5,5,8,256]{3,2,1,0:T(8,128)S(1)}, u32[]{:S(2)}, u32[]{:S(2)}) %collective-permute-start.10) | collective-permute-done | bytes 204832 | tf_op jit(solution)/shard_map/ppermute | solution.py:762
  113.9 0.1 broadcast_select_fusion
  114.1 0.1 fusion.2
  114.2 5.5 %collective-permute-start.11 = (f32[5,5,8,256]{3,2,1,0:T(8,128)S(1)}, f32[5,5,8,256]{3,2,1,0:T(8,128)S(1)}, u32[]{:S(2)}, u32[]{:S(2)}) collective-permute-start(f32[5,5,8,256]{3,2,1,0:T(8,128)S(1)} %pad_maximum_fusion), channel_id=1, source_target_pairs={{1,2},{2,1},{3,0},{0,3},{5,6},{6,5},{7,4},{4,7},{9,10},{10,9},{11,... | collective-permute-start | bytes 614408 | tf_op jit(solution)/shard_map/ppermute | solution.py:767
  119.7 6.0 %collective-permute-done.11 = f32[5,5,8,256]{3,2,1,0:T(8,128)S(1)} collective-permute-done((f32[5,5,8,256]{3,2,1,0:T(8,128)S(1)}, f32[5,5,8,256]{3,2,1,0:T(8,128)S(1)}, u32[]{:S(2)}, u32[]{:S(2)}) %collective-permute-start.11) | collective-permute-done | bytes 204832 | tf_op jit(solution)/shard_map/ppermute | solution.py:767
  125.7 0.1 fusion.1
  125.9 0.0 copy-start.1
  126.0 0.1 collective-permute-start.12
  126.1 0.7 collective-permute-start.13
  126.8 0.7 collective-permute-done.12.ia_ref
  127.4 0.0 copy-start.7
  127.4 0.0 collective-permute-done.13.ib_ref
  127.4 0.0 copy-start.8
  127.4 0.0 collective-permute-done.8.ba_ref
  127.4 0.0 copy-start.3
  127.4 0.0 collective-permute-done.9.bb_ref
  127.5 0.0 copy-start.4
  127.5 0.0 copy-done.1
  127.5 0.6 copy-done.7
  128.1 0.1 copy-done.8
  128.1 0.4 copy-done.3
  128.5 0.4 copy-done.4
  128.9 26.9 %shard_map.79 = (f32[6144,128]{1,0:T(8,128)}, f32[6144,128]{1,0:T(8,128)}, f32[1,128]{1,0:T(1,128)}) custom-call(s32[1]{0:T(128)S(6)} %copy.22.index_ref, s32[4,4]{1,0:T(4,128)} %cells_ref.1, f32[3,4,32,8,256]{4,3,2,1,0:T(8,128)} %get-tuple-element.27.v_ref, f32[5,32,8,256]{3,2,1,0:T(8,128)} %get-tuple-element.28.bw_ref, f32[4,32,8,256]{3,2,1,0:T(8,128)} %copy-done.3, ...), custom_call_target="tpu_custom_call" | custom-call | flops 100000000 | bytes 16523844 | tf_op jit(solution)/shard_map/pallas_call | solution.py:727
  155.8 0.7 broadcast_in_dim.31
  156.4 23.3 %all_to_all.5 = f32[32,1,128]{2,1,0:T(1,128)} all-to-all(f32[32,1,128]{2,1,0:T(1,128)S(1)} %broadcast_in_dim.31), channel_id=1, replica_groups=mesh['gx'=8,'gz'=4] {'gx','gz'}, dimensions={0} | all-to-all | bytes 32768 | tf_op jit(solution)/shard_map/all_to_all | solution.py:831
  179.7 7.5 %shard_map.80 = (f32[6144,128]{1,0:T(8,128)}, f32[4,4]{1,0:T(4,128)}) custom-call(s32[1]{0:T(128)S(6)} %copy.22.index_ref, f32[32,128]{1,0:T(8,128)} %bitcast.32, f32[6144,128]{1,0:T(8,128)} %bitcast.29, f32[6144,128]{1,0:T(8,128)} %get-tuple-element.32.solved_ref), custom_call_target="tpu_custom_call" | custom-call | tf_op jit(solution)/shard_map/pallas_call | solution.py:837
  (12 shorter events, 0.2 us)
Async XLA Ops:
  7.3 46.4 %collective-permute-start = (f32[312,8,256]{2,1,0:T(8,128)}, f32[312,8,256]{2,1,0:T(8,128)S(1)}, u32[]{:S(2)}, u32[]{:S(2)}) collective-permute-start(f32[312,8,256]{2,1,0:T(8,128)} %get-tuple-element.20), channel_id=1, source_target_pairs={{0,4},{4,0},{8,12},{12,8},{16,20},{20,16},{24,28},{28,24},{1,5},{5... | collective-permute-start | bytes 7667720 | tf_op jit(solution)/shard_map/ppermute | solution.py:804
  7.8 19.1 %collective-permute-start.1 = (f32[152,8,256]{2,1,0:T(8,128)}, f32[152,8,256]{2,1,0:T(8,128)}, u32[]{:S(2)}, u32[]{:S(2)}) collective-permute-start(f32[152,8,256]{2,1,0:T(8,128)} %get-tuple-element.21), channel_id=1, source_target_pairs={{4,8},{8,4},{20,24},{24,20},{12,28},{16,0},{5,9},{9,5},{21,25},{25... | collective-permute-start | bytes 3735560 | tf_op jit(solution)/shard_map/ppermute | solution.py:800
  9.1 43.4 %collective-permute-start.3 = (f32[160,8,256]{2,1,0:T(8,128)}, f32[160,8,256]{2,1,0:T(8,128)}, u32[]{:S(2)}, u32[]{:S(2)}) collective-permute-start(f32[160,8,256]{2,1,0:T(8,128)} %get-tuple-element.22), channel_id=1, source_target_pairs={{4,8},{8,4},{12,16},{16,12},{20,24},{24,20},{5,9},{9,5},{13,17},{1... | collective-permute-start | bytes 3932168 | tf_op jit(solution)/shard_map/ppermute | solution.py:803
  26.9 26.8 %collective-permute-start.2 = (f32[152,8,256]{2,1,0:T(8,128)}, f32[152,8,256]{2,1,0:T(8,128)}, u32[]{:S(2)}, u32[]{:S(2)}) collective-permute-start(f32[152,8,256]{2,1,0:T(8,128)} %collective-permute-done.1.b1_ref), channel_id=1, source_target_pairs={{28,16},{0,12},{29,17},{1,13},{30,18},{2,14},{31,19},{3,15}} | collective-permute-start | bytes 3735560 | tf_op jit(solution)/shard_map/ppermute | solution.py:809
  30.7 6.1 %collective-permute-start.4 = (f32[26,8,256]{2,1,0:T(8,128)}, f32[26,8,256]{2,1,0:T(8,128)S(1)}, u32[]{:S(2)}, u32[]{:S(2)}) collective-permute-start(f32[26,8,256]{2,1,0:T(8,128)} %get-tuple-element.23), channel_id=1, source_target_pairs={{0,1},{1,0},{2,3},{3,2},{4,5},{5,4},{6,7},{7,6},{8,9},{9,8},{10,11... | collective-permute-start | bytes 638984 | tf_op jit(solution)/shard_map/ppermute | solution.py:801
  32.3 8.9 %collective-permute-start.5 = (f32[26,8,256]{2,1,0:T(8,128)}, f32[26,8,256]{2,1,0:T(8,128)S(1)}, u32[]{:S(2)}, u32[]{:S(2)}) collective-permute-start(f32[26,8,256]{2,1,0:T(8,128)} %get-tuple-element.24), channel_id=1, source_target_pairs={{1,2},{2,1},{3,0},{0,3},{5,6},{6,5},{7,4},{4,7},{9,10},{10,9},{11,... | collective-permute-start | bytes 638984 | tf_op jit(solution)/shard_map/ppermute | solution.py:802
  36.8 4.4 %copy-start.5 = (f32[26,8,256]{2,1,0:T(8,128)}, f32[26,8,256]{2,1,0:T(8,128)S(1)}, u32[]{:S(2)}) copy-start(f32[26,8,256]{2,1,0:T(8,128)S(1)} %collective-permute-done.4.z1_ref) | copy-start | bytes 638980
  41.2 0.7 copy-start.6
  43.7 8.8 %collective-permute-start.6 = (f32[17,8,256]{2,1,0:T(8,128)}, f32[17,8,256]{2,1,0:T(8,128)S(1)}, u32[]{:S(2)}, u32[]{:S(2)}) collective-permute-start(f32[17,8,256]{2,1,0:T(8,128)} %get-tuple-element.25), channel_id=1, source_target_pairs={{0,4},{4,0},{8,12},{12,8},{16,20},{20,16},{24,28},{28,24},{1,5},{5... | collective-permute-start | bytes 417800 | tf_op jit(solution)/shard_map/ppermute | solution.py:807
  51.1 1.4 collective-permute-start.7
  52.5 1.2 copy-start.9
  52.5 1.2 copy-start.10
  53.7 1.5 copy-start
  100.9 7.0 %copy-start.2 = (f32[5,5,8,256]{3,2,1,0:T(8,128)S(1)}, f32[5,5,8,256]{3,2,1,0:T(8,128)}, u32[]{:S(2)}) copy-start(f32[5,5,8,256]{3,2,1,0:T(8,128)} %get-tuple-element.29) | copy-start | bytes 614404
  102.6 24.8 %collective-permute-start.8 = (f32[4,32,8,256]{3,2,1,0:T(8,128)S(1)}, f32[4,32,8,256]{3,2,1,0:T(8,128)S(1)}, u32[]{:S(2)}, u32[]{:S(2)}) collective-permute-start(f32[4,32,8,256]{3,2,1,0:T(8,128)S(1)} %get-tuple-element.48), channel_id=1, source_target_pairs={{0,4},{4,0},{8,12},{12,8},{16,20},{20,16},{24,28},{28,24},{1,5},{5... | collective-permute-start | bytes 3145736 | tf_op jit(solution)/shard_map/ppermute | solution.py:818
  107.2 20.3 %collective-permute-start.9 = (f32[4,32,8,256]{3,2,1,0:T(8,128)S(1)}, f32[4,32,8,256]{3,2,1,0:T(8,128)S(1)}, u32[]{:S(2)}, u32[]{:S(2)}) collective-permute-start(f32[4,32,8,256]{3,2,1,0:T(8,128)S(1)} %get-tuple-element.47), channel_id=1, source_target_pairs={{4,8},{8,4},{12,16},{16,12},{20,24},{24,20},{5,9},{9,5},{13,17},{1... | collective-permute-start | bytes 3145736 | tf_op jit(solution)/shard_map/ppermute | solution.py:817
  107.9 6.0 %collective-permute-start.10 = (f32[5,5,8,256]{3,2,1,0:T(8,128)S(1)}, f32[5,5,8,256]{3,2,1,0:T(8,128)S(1)}, u32[]{:S(2)}, u32[]{:S(2)}) collective-permute-start(f32[5,5,8,256]{3,2,1,0:T(8,128)S(1)} %copy-done.2), channel_id=1, source_target_pairs={{0,1},{1,0},{2,3},{3,2},{4,5},{5,4},{6,7},{7,6},{8,9},{9,8},{10,11... | collective-permute-start | bytes 614408 | tf_op jit(solution)/shard_map/ppermute | solution.py:762
  114.2 11.5 %collective-permute-start.11 = (f32[5,5,8,256]{3,2,1,0:T(8,128)S(1)}, f32[5,5,8,256]{3,2,1,0:T(8,128)S(1)}, u32[]{:S(2)}, u32[]{:S(2)}) collective-permute-start(f32[5,5,8,256]{3,2,1,0:T(8,128)S(1)} %pad_maximum_fusion), channel_id=1, source_target_pairs={{1,2},{2,1},{3,0},{0,3},{5,6},{6,5},{7,4},{4,7},{9,10},{10,9},{11,... | collective-permute-start | bytes 614408 | tf_op jit(solution)/shard_map/ppermute | solution.py:767
  125.9 1.6 copy-start.1
  126.0 1.5 collective-permute-start.12
  126.1 1.3 collective-permute-start.13
  127.4 0.7 copy-start.7
  127.4 0.7 copy-start.8
  127.4 1.1 copy-start.3
  127.5 1.4 copy-start.4

commit v2 on v1

--- a/solution.py
+++ b/solution.py
@@ -178,13 +178,25 @@
 
 
 def below(cells):
-    lanes = lax.broadcasted_iota(jnp.int32, (8, 256), 1)
-    return jnp.where(lanes > 0, pltpu.roll(cells, 1, 1), 0.0)
+    lanes = lax.broadcasted_iota(jnp.int32, (8, 128), 1)
+    low, high = pltpu.roll(cells[:, :128], 1, 1), pltpu.roll(cells[:, 128:], 1, 1)
+    return jnp.concatenate([jnp.where(lanes > 0, low, 0.0), jnp.where(lanes > 0, high, low)], axis=1)
 
 
 def above(cells):
-    lanes = lax.broadcasted_iota(jnp.int32, (8, 256), 1)
-    return jnp.where(lanes < 255, pltpu.roll(cells, 255, 1), 0.0)
+    lanes = lax.broadcasted_iota(jnp.int32, (8, 128), 1)
+    low, high = pltpu.roll(cells[:, :128], 127, 1), pltpu.roll(cells[:, 128:], 127, 1)
+    return jnp.concatenate([jnp.where(lanes < 127, low, high), jnp.where(lanes < 127, high, 0.0)], axis=1)
+
+
+def either_side(cells):
+    lanes = lax.broadcasted_iota(jnp.int32, (8, 128), 1)
+    low, high = cells[:, :128], cells[:, 128:]
+    low_up, high_up = pltpu.roll(low, 1, 1), pltpu.roll(high, 1, 1)
+    low_down, high_down = pltpu.roll(low, 127, 1), pltpu.roll(high, 127, 1)
+    first = jnp.where(lanes > 0, low_up, 0.0) + jnp.where(lanes < 127, low_down, high_down)
+    second = jnp.where(lanes > 0, high_up, low_up) + jnp.where(lanes < 127, high_down, 0.0)
+    return jnp.concatenate([first, second], axis=1)
 
 
 def shift_of(index_ref):
@@ -267,7 +279,7 @@
                     b2_ref[at - PART + zz] = cells
         return 0
 
-    lax.fori_loop(0, HALF, edges, 0)
+    lax.fori_loop(0, HALF, edges, 0, unroll=2)
     for layer in range(3):
         for group in range(8):
             for tile in range(2):
@@ -421,23 +433,29 @@
             r_ref[x, zz] = 1.0 + flow * (1.0 / viscosity)
         return 0
 
-    lax.fori_loop(0, 39, coefficients, 0)
+    lax.fori_loop(0, 39, coefficients, 0, unroll=3)
     zero = jnp.zeros((8, 256), jnp.float32)
     for x in (0, 1, 2, 7, 8, 9):
         for zz in (0, 1, 2, 3, 36, 37, 38):
             v0_ref[x, zz] = zero
 
+    def swept(source, zz, margin):
+        layers = {x: source[x, zz] for x in range(2 - margin, 8 + margin)}
+        result = {}
+        for x in range(3 - margin, 7 + margin):
+            centre = layers[x]
+            total = layers[x + 1] + either_side(centre)
+            total = total + (source[x, zz + 1] + source[x, zz - 1])
+            result[x] = v0_ref[x, zz] + a1_ref[x, zz] * (total + r_ref[x, zz] * layers[x - 1])
+        return result
+
     def sweep(source, target, margin):
         def body(zz, _):
-            layers = {x: source[x, zz] for x in range(2 - margin, 8 + margin)}
-            for x in range(3 - margin, 7 + margin):
-                centre = layers[x]
-                total = layers[x + 1] + (below(centre) + above(centre))
-                total = total + (source[x, zz + 1] + source[x, zz - 1])
-                target[x, zz] = v0_ref[x, zz] + a1_ref[x, zz] * (total + r_ref[x, zz] * layers[x - 1])
+            for x, cells in swept(source, zz, margin).items():
+                target[x, zz] = cells
             return 0
 
-        lax.fori_loop(3 - margin, 36 + margin, body, 0)
+        lax.fori_loop(3 - margin, 36 + margin, body, 0, unroll=6)
 
     for component in range(3):
 
@@ -446,7 +464,7 @@
                 v0_ref[x + 3, zz + 4] = own_ref[component, x, zz] * a1_ref[x + 3, zz + 4]
             return 0
 
-        lax.fori_loop(0, HALF, interior, 0)
+        lax.fori_loop(0, HALF, interior, 0, unroll=4)
 
         def before(cells, halo, k):
             if k % 2 == 0:
@@ -497,24 +515,25 @@
         each_x(sides)
         sweep(v0_ref, va_ref, 2)
         sweep(va_ref, vb_ref, 1)
-        sweep(vb_ref, va_ref, 0)
-
-        def diverge(zz, _, component=component):
+
+        def diverge(zz, before, component=component):
+            cells = [swept(vb_ref, zz + 4, 0)[x + 3] for x in range(4)]
             for x in range(4):
-                cells = va_ref[x + 3, zz + 4]
-                v_ref[component, x, zz] = cells
+                v_ref[component, x, zz] = cells[x]
                 if component == 0:
-                    inner = cells if x == 0 else cells - va_ref[x + 2, zz + 4]
-                    bw_ref[x, zz] = -2.0 * inner
+                    bw_ref[x, zz] = -2.0 * (cells[x] if x == 0 else cells[x] - cells[x - 1])
                 elif component == 1:
-                    bw_ref[x, zz] = bw_ref[x, zz] - (cells - below(cells))
+                    bw_ref[x, zz] = bw_ref[x, zz] - (cells[x] - below(cells[x]))
                 else:
-                    bw_ref[x, zz] = bw_ref[x, zz] - (cells - va_ref[x + 3, zz + 3])
+                    bw_ref[x, zz] = bw_ref[x, zz] - (cells[x] - before[x])
             if component == 0:
-                bw_ref[4, zz] = va_ref[6, zz + 4]
-            return 0
-
-        lax.fori_loop(0, HALF, diverge, 0)
+                bw_ref[4, zz] = cells[3]
+            return tuple(cells) if component == 2 else 0
+
+        start = 0
+        if component == 2:
+            start = tuple(swept(vb_ref, 3, 0)[x + 3] for x in range(4))
+        lax.fori_loop(0, HALF, diverge, start, unroll=4)
 
     def states(layer, _):
         forward, backward = half_states(lambda t: bw_ref[layer, t])
@@ -621,7 +640,7 @@
             edge = 2 - power
             layers = {x: q_ref[power + 1, x, zz] for x in range(edge, 11 - edge)}
             for x in range(edge + 1, 10 - edge if power else 8):
-                beside = 4.0 * (layers[x - 1] + layers[x + 1]) + (below(layers[x]) + above(layers[x]))
+                beside = 4.0 * (layers[x - 1] + layers[x + 1]) + either_side(layers[x])
                 if x < 3:
                     beside = mask_left * beside
                 if x > 6:
@@ -629,7 +648,7 @@
                 q_ref[power, x, zz] = q_ref[power, x, zz] + beside
             return 0
 
-        lax.fori_loop(0, HALF + 1, apply, 0)
+        lax.fori_loop(0, HALF + 1, apply, 0, unroll=3)
 
     def correct(m, _):
         for x in range(4):
@@ -654,7 +673,7 @@
                     solved_ref[pl.ds(row + 1024, 8, stride=8), :] = late[:, lanes]
         return 0
 
-    lax.fori_loop(0, 16, correct, 0)
+    lax.fori_loop(0, 16, correct, 0, unroll=2)
     couples = [(i, j) for i in range(4) for j in range(i, 4)]
 
     def update(block, sums):
@@ -730,7 +749,7 @@
         in_specs=places,
         out_specs=[pl.BlockSpec(memory_space=pltpu.VMEM)] * len(outputs),
         scratch_shapes=[pltpu.VMEM(shape, jnp.float32) for shape in scratch],
-        compiler_params=pltpu.CompilerParams(vmem_limit_bytes=56 << 20),
+        compiler_params=pltpu.CompilerParams(vmem_limit_bytes=26 << 20),
         cost_estimate=pl.CostEstimate(flops=flops, bytes_accessed=moved, transcendentals=0),
     )(*operands)
 

time: 188 us -> 150 us (0.80)
  Pallas kernels: 88.6 us -> 49.3 us
  waiting for transfers between devices: 34.1 us -> 36.1 us
    pallas_call x4, Pallas kernels: 81.1 us -> 41.8 us  [call(): pl.pallas_call(kernel, out_shape=arrays, in_specs=places, out_specs=[pl.B...]
    unnamed x23 -> x21, local copies, waits for them, and re-layouts: 3.6 us -> 7.05 us
where the time goes in v2:
time: 150 us
  Pallas kernels  49.3 us (33%)
  waiting for transfers between devices  36.1 us (24%)
  starting transfers between devices  32.2 us (21%)
  blocking collectives  22.9 us (15%)
  local copies, waits for them, and re-layouts  7.33 us (5%)
  between operations  1.51 us (1%)
    pallas_call x4, Pallas kernels, call(): pl.pallas_call(kernel, out_shape=arrays, in_specs=places, out_specs=[pl.B...  41.8 us
    all_to_all x1, blocking collectives, fast_shards(): lax.all_to_all(jnp.broadcast_to(sums[None], (devices, 1, 128)), ('gx', 'g...  22.9 us
    ppermute x1, waiting for transfers between devices, fast_shards(): b1_in = lax.ppermute(b1, 'gx', send_round)  15.9 us
    pallas_call x1, Pallas kernels, fast_shards(): pl.pallas_call(gain_kernel, grid=(gain_rows.shape[0] // chunk,), in_specs...  7.48 us
    ppermute x1, starting transfers between devices, fast_shards(): ca = lax.ppermute(ca, 'gx', swap_in)  7.37 us
    unnamed x21, local copies, waits for them, and re-layouts  7.05 us
    ppermute x1, waiting for transfers between devices, ring_states(): other = lax.ppermute(jnp.concatenate([joined, states[POISSON:]]), 'gz', far)  5.45 us
    ppermute x1, waiting for transfers between devices, ring_states(): partner = lax.ppermute(states, 'gz', near)  5.11 us
  transfers between devices with their start and end apart: 14, of which 7 were waited for; matrix products, arithmetic and copies ran while one was open for 0% of the time, Pallas kernels for 1%

profile of v2, /device:TPU:0, one launch (start us, length us, event | category | flops | bytes accessed | tf_op | source)
XLA Modules:
  0.0 149.7 jit_solution(10253487244022672165)
XLA Ops:
  0.6 0.0 copy-start
  0.6 1.9 %copy-done = f32[3,64,4,4,256]{4,3,2,1,0:T(4,128)S(1)} copy-done((f32[3,64,4,4,256]{4,3,2,1,0:T(4,128)S(1)}, f32[3,64,4,4,256]{4,3,2,1,0:T(4,128)}, u32[]{:S(2)}) %copy-start) | copy-done | bytes 3145752
  2.5 0.0 copy-start.3
  2.5 0.9 copy-done.3
  3.5 0.0 copy-start.4
  3.5 3.3 %shard_map.76 = (f32[3,4,32,8,256]{4,3,2,1,0:T(8,128)S(1)}, f32[312,8,256]{2,1,0:T(8,128)}, f32[152,8,256]{2,1,0:T(8,128)S(1)}, f32[160,8,256]{2,1,0:T(8,128)}, ...) custom-call(f32[6144,128]{1,0:T(8,128)S(1)} %bitcast.27, f32[512,128]{1,0:T(8,128)S(1)} %bitcast.29), custom_call_target="tpu_custom_call" | custom-call | flops 1000000 | bytes 12091392 | tf_op jit(solution)/shard_map/pallas_call | solution.py:746
  6.7 0.5 collective-permute-start
  7.2 1.3 collective-permute-start.1
  8.5 1.8 %collective-permute-start.3 = (f32[160,8,256]{2,1,0:T(8,128)}, f32[160,8,256]{2,1,0:T(8,128)}, u32[]{:S(2)}, u32[]{:S(2)}) collective-permute-start(f32[160,8,256]{2,1,0:T(8,128)} %get-tuple-element.22), channel_id=1, source_target_pairs={{4,8},{8,4},{12,16},{16,12},{20,24},{24,20},{5,9},{9,5},{13,17},{1... | collective-permute-start | bytes 3932168 | tf_op jit(solution)/shard_map/ppermute | solution.py:822
  10.2 15.9 %collective-permute-done.1.b1_ref = f32[152,8,256]{2,1,0:T(8,128)} collective-permute-done((f32[152,8,256]{2,1,0:T(8,128)S(1)}, f32[152,8,256]{2,1,0:T(8,128)}, u32[]{:S(2)}, u32[]{:S(2)}) %collective-permute-start.1) | collective-permute-done | bytes 1245216 | tf_op jit(solution)/shard_map/ppermute | solution.py:819
  26.1 3.6 %collective-permute-start.2 = (f32[152,8,256]{2,1,0:T(8,128)}, f32[152,8,256]{2,1,0:T(8,128)}, u32[]{:S(2)}, u32[]{:S(2)}) collective-permute-start(f32[152,8,256]{2,1,0:T(8,128)} %collective-permute-done.1.b1_ref), channel_id=1, source_target_pairs={{28,16},{0,12},{29,17},{1,13},{30,18},{2,14},{31,19},{3,15}} | collective-permute-start | bytes 3735560 | tf_op jit(solution)/shard_map/ppermute | solution.py:828
  29.7 1.6 %collective-permute-start.4 = (f32[26,8,256]{2,1,0:T(8,128)S(1)}, f32[26,8,256]{2,1,0:T(8,128)S(1)}, u32[]{:S(2)}, u32[]{:S(2)}) collective-permute-start(f32[26,8,256]{2,1,0:T(8,128)S(1)} %get-tuple-element.23), channel_id=1, source_target_pairs={{0,1},{1,0},{2,3},{3,2},{4,5},{5,4},{6,7},{7,6},{8,9},{9,8},{10,11... | collective-permute-start | bytes 638984 | tf_op jit(solution)/shard_map/ppermute | solution.py:820
  31.3 2.5 %collective-permute-start.5 = (f32[26,8,256]{2,1,0:T(8,128)S(1)}, f32[26,8,256]{2,1,0:T(8,128)S(1)}, u32[]{:S(2)}, u32[]{:S(2)}) collective-permute-start(f32[26,8,256]{2,1,0:T(8,128)S(1)} %get-tuple-element.24), channel_id=1, source_target_pairs={{1,2},{2,1},{3,0},{0,3},{5,6},{6,5},{7,4},{4,7},{9,10},{10,9},{11,... | collective-permute-start | bytes 638984 | tf_op jit(solution)/shard_map/ppermute | solution.py:821
  33.8 1.8 %collective-permute-done.4.z1_ref = f32[26,8,256]{2,1,0:T(8,128)S(1)} collective-permute-done((f32[26,8,256]{2,1,0:T(8,128)S(1)}, f32[26,8,256]{2,1,0:T(8,128)S(1)}, u32[]{:S(2)}, u32[]{:S(2)}) %collective-permute-start.4) | collective-permute-done | bytes 213024 | tf_op jit(solution)/shard_map/ppermute | solution.py:820
  35.6 4.4 %collective-permute-done.5.z2_ref = f32[26,8,256]{2,1,0:T(8,128)S(1)} collective-permute-done((f32[26,8,256]{2,1,0:T(8,128)S(1)}, f32[26,8,256]{2,1,0:T(8,128)S(1)}, u32[]{:S(2)}, u32[]{:S(2)}) %collective-permute-start.5) | collective-permute-done | bytes 213024 | tf_op jit(solution)/shard_map/ppermute | solution.py:821
  40.0 0.0 copy-start.7
  40.0 0.8 shard_map.77
  40.8 0.0 copy-done.7
  40.8 0.0 copy-start.5
  40.8 0.7 copy-done.5
  41.5 7.4 %collective-permute-start.6 = (f32[17,8,256]{2,1,0:T(8,128)}, f32[17,8,256]{2,1,0:T(8,128)S(1)}, u32[]{:S(2)}, u32[]{:S(2)}) collective-permute-start(f32[17,8,256]{2,1,0:T(8,128)} %get-tuple-element.25), channel_id=1, source_target_pairs={{0,4},{4,0},{8,12},{12,8},{16,20},{20,16},{24,28},{28,24},{1,5},{5... | collective-permute-start | bytes 417800 | tf_op jit(solution)/shard_map/ppermute | solution.py:826
  48.8 1.3 collective-permute-start.7
  50.8 0.0 collective-permute-done.6.ca_ref
  50.8 0.0 collective-permute-done.7.cb_ref
  50.9 0.0 collective-permute-done.3.b2_ref
  50.9 2.7 %collective-permute-done.2.b3_ref = f32[152,8,256]{2,1,0:T(8,128)} collective-permute-done((f32[152,8,256]{2,1,0:T(8,128)}, f32[152,8,256]{2,1,0:T(8,128)}, u32[]{:S(2)}, u32[]{:S(2)}) %collective-permute-start.2) | collective-permute-done | bytes 1245216 | tf_op jit(solution)/shard_map/ppermute | solution.py:828
  53.6 0.0 collective-permute-done.a_ref
  53.6 0.0 copy-done.4
  53.6 0.0 copy-start.6
  53.6 0.9 copy-done.6
  54.5 0.0 copy-start.8
  54.5 0.9 copy-done.8
  55.5 20.5 %shard_map.78 = (f32[3,4,32,8,256]{4,3,2,1,0:T(8,128)S(1)}, f32[5,32,8,256]{3,2,1,0:T(8,128)S(1)}, f32[5,5,8,256]{3,2,1,0:T(8,128)S(1)}) custom-call(s32[1]{0:T(128)S(6)} %copy.22.index_ref, f32[3,4,32,8,256]{4,3,2,1,0:T(8,128)S(1)} %get-tuple-element.19.own_ref, f32[512,128]{1,0:T(8,128)S(1)} %bitcast.30, f32[312,8,256]{2,1,0:T(8,128)} %collective-permute-done.a_ref, ...), custom_call_target="tpu_custom_call" | custom-call | flops 100000000 | bytes 15130628 | tf_op jit(solution)/shard_map/pallas_call | solution.py:746
  76.0 0.2 constant_dynamic-slice_fusion.2
  76.3 3.9 %collective-permute-start.8 = (f32[4,32,8,256]{3,2,1,0:T(8,128)S(1)}, f32[4,32,8,256]{3,2,1,0:T(8,128)S(1)}, u32[]{:S(2)}, u32[]{:S(2)}) collective-permute-start(f32[4,32,8,256]{3,2,1,0:T(8,128)S(1)} %get-tuple-element.48), channel_id=1, source_target_pairs={{0,4},{4,0},{8,12},{12,8},{16,20},{20,16},{24,28},{28,24},{1,5},{5... | collective-permute-start | bytes 3145736 | tf_op jit(solution)/shard_map/ppermute | solution.py:837
  80.2 0.7 collective-permute-start.9
  80.9 2.3 %collective-permute-start.10 = (f32[5,5,8,256]{3,2,1,0:T(8,128)S(1)}, f32[5,5,8,256]{3,2,1,0:T(8,128)S(1)}, u32[]{:S(2)}, u32[]{:S(2)}) collective-permute-start(f32[5,5,8,256]{3,2,1,0:T(8,128)S(1)} %get-tuple-element.29), channel_id=1, source_target_pairs={{0,1},{1,0},{2,3},{3,2},{4,5},{5,4},{6,7},{7,6},{8,9},{9,8},{10,11... | collective-permute-start | bytes 614408 | tf_op jit(solution)/shard_map/ppermute | solution.py:781
  83.2 0.0 copy-start.1
  83.2 0.0 copy-start.9
  83.2 5.1 %collective-permute-done.10 = f32[5,5,8,256]{3,2,1,0:T(8,128)S(1)} collective-permute-done((f32[5,5,8,256]{3,2,1,0:T(8,128)S(1)}, f32[5,5,8,256]{3,2,1,0:T(8,128)S(1)}, u32[]{:S(2)}, u32[]{:S(2)}) %collective-permute-start.10) | collective-permute-done | bytes 204832 | tf_op jit(solution)/shard_map/ppermute | solution.py:781
  88.3 0.1 broadcast_select_fusion
  88.4 0.1 fusion.2
  88.6 4.6 %collective-permute-start.11 = (f32[5,5,8,256]{3,2,1,0:T(8,128)S(1)}, f32[5,5,8,256]{3,2,1,0:T(8,128)S(1)}, u32[]{:S(2)}, u32[]{:S(2)}) collective-permute-start(f32[5,5,8,256]{3,2,1,0:T(8,128)S(1)} %pad_maximum_fusion), channel_id=1, source_target_pairs={{1,2},{2,1},{3,0},{0,3},{5,6},{6,5},{7,4},{4,7},{9,10},{10,9},{11,... | collective-permute-start | bytes 614408 | tf_op jit(solution)/shard_map/ppermute | solution.py:786
  93.2 5.4 %collective-permute-done.11 = f32[5,5,8,256]{3,2,1,0:T(8,128)S(1)} collective-permute-done((f32[5,5,8,256]{3,2,1,0:T(8,128)S(1)}, f32[5,5,8,256]{3,2,1,0:T(8,128)S(1)}, u32[]{:S(2)}, u32[]{:S(2)}) %collective-permute-start.11) | collective-permute-done | bytes 204832 | tf_op jit(solution)/shard_map/ppermute | solution.py:786
  98.7 0.1 fusion.1
  98.9 0.1 collective-permute-start.12
  99.0 0.7 collective-permute-start.13
  99.7 0.7 collective-permute-done.12.ia_ref
  100.4 0.0 collective-permute-done.13.ib_ref
  100.4 0.0 collective-permute-done.8.ba_ref
  100.4 0.0 collective-permute-done.9.bb_ref
  100.4 0.0 copy-done.1
  100.4 0.0 copy-done.9
  100.4 17.2 %shard_map.79 = (f32[6144,128]{1,0:T(8,128)}, f32[6144,128]{1,0:T(8,128)S(1)}, f32[1,128]{1,0:T(1,128)S(1)}) custom-call(s32[1]{0:T(128)S(6)} %copy.22.index_ref, s32[4,4]{1,0:T(4,128)S(1)} %copy-done.9, f32[3,4,32,8,256]{4,3,2,1,0:T(8,128)S(1)} %get-tuple-element.27.v_ref, f32[5,32,8,256]{3,2,1,0:T(8,128)S(1)} %get-tuple-element.28.bw_ref, ...), custom_call_target="tpu_custom_call" | custom-call | flops 100000000 | bytes 16523844 | tf_op jit(solution)/shard_map/pallas_call | solution.py:746
  117.6 0.0 copy-start.2
  117.6 1.6 %copy-done.2 = f32[6144,128]{1,0:T(8,128)} copy-done((f32[6144,128]{1,0:T(8,128)}, f32[6144,128]{1,0:T(8,128)S(1)}, u32[]{:S(2)}) %copy-start.2) | copy-done | bytes 3145752
  119.3 22.9 %all_to_all.5 = f32[32,1,128]{2,1,0:T(1,128)} all-to-all(f32[32,1,128]{2,1,0:T(1,128)S(1)} %broadcast_in_dim.31), channel_id=1, replica_groups=mesh['gx'=8,'gz'=4] {'gx','gz'}, dimensions={0} | all-to-all | bytes 32768 | tf_op jit(solution)/shard_map/all_to_all | solution.py:850
  142.2 7.5 %shard_map.80 = (f32[6144,128]{1,0:T(8,128)}, f32[4,4]{1,0:T(4,128)}) custom-call(s32[1]{0:T(128)S(6)} %copy.22.index_ref, f32[32,128]{1,0:T(8,128)} %bitcast.33, f32[6144,128]{1,0:T(8,128)} %bitcast.32, f32[6144,128]{1,0:T(8,128)} %copy-done.2), custom_call_target="tpu_custom_call" | custom-call | tf_op jit(solution)/shard_map/pallas_call | solution.py:856
  (13 shorter events, 0.2 us)
Async XLA Ops:
  0.6 1.9 %copy-start = (f32[3,64,4,4,256]{4,3,2,1,0:T(4,128)S(1)}, f32[3,64,4,4,256]{4,3,2,1,0:T(4,128)}, u32[]{:S(2)}) copy-start(f32[3,64,4,4,256]{4,3,2,1,0:T(4,128)} %param.5) | copy-start | bytes 9437188
  2.5 0.9 copy-start.3
  3.5 50.1 %copy-start.4 = (f32[64,4,256]{2,1,0:T(4,128)S(1)}, f32[64,4,256]{2,1,0:T(4,128)}, u32[]{:S(2)}) copy-start(f32[64,4,256]{2,1,0:T(4,128)} %param.7) | copy-start | bytes 786436
  6.7 46.9 %collective-permute-start = (f32[312,8,256]{2,1,0:T(8,128)}, f32[312,8,256]{2,1,0:T(8,128)}, u32[]{:S(2)}, u32[]{:S(2)}) collective-permute-start(f32[312,8,256]{2,1,0:T(8,128)} %get-tuple-element.20), channel_id=1, source_target_pairs={{0,4},{4,0},{8,12},{12,8},{16,20},{20,16},{24,28},{28,24},{1,5},{5... | collective-permute-start | bytes 7667720 | tf_op jit(solution)/shard_map/ppermute | solution.py:823
  7.2 18.9 %collective-permute-start.1 = (f32[152,8,256]{2,1,0:T(8,128)S(1)}, f32[152,8,256]{2,1,0:T(8,128)}, u32[]{:S(2)}, u32[]{:S(2)}) collective-permute-start(f32[152,8,256]{2,1,0:T(8,128)S(1)} %get-tuple-element.21), channel_id=1, source_target_pairs={{4,8},{8,4},{20,24},{24,20},{12,28},{16,0},{5,9},{9,5},{21,25},{25... | collective-permute-start | bytes 3735560 | tf_op jit(solution)/shard_map/ppermute | solution.py:819
  8.5 42.4 %collective-permute-start.3 = (f32[160,8,256]{2,1,0:T(8,128)}, f32[160,8,256]{2,1,0:T(8,128)}, u32[]{:S(2)}, u32[]{:S(2)}) collective-permute-start(f32[160,8,256]{2,1,0:T(8,128)} %get-tuple-element.22), channel_id=1, source_target_pairs={{4,8},{8,4},{12,16},{16,12},{20,24},{24,20},{5,9},{9,5},{13,17},{1... | collective-permute-start | bytes 3932168 | tf_op jit(solution)/shard_map/ppermute | solution.py:822
  26.1 27.5 %collective-permute-start.2 = (f32[152,8,256]{2,1,0:T(8,128)}, f32[152,8,256]{2,1,0:T(8,128)}, u32[]{:S(2)}, u32[]{:S(2)}) collective-permute-start(f32[152,8,256]{2,1,0:T(8,128)} %collective-permute-done.1.b1_ref), channel_id=1, source_target_pairs={{28,16},{0,12},{29,17},{1,13},{30,18},{2,14},{31,19},{3,15}} | collective-permute-start | bytes 3735560 | tf_op jit(solution)/shard_map/ppermute | solution.py:828
  29.7 5.8 %collective-permute-start.4 = (f32[26,8,256]{2,1,0:T(8,128)S(1)}, f32[26,8,256]{2,1,0:T(8,128)S(1)}, u32[]{:S(2)}, u32[]{:S(2)}) collective-permute-start(f32[26,8,256]{2,1,0:T(8,128)S(1)} %get-tuple-element.23), channel_id=1, source_target_pairs={{0,1},{1,0},{2,3},{3,2},{4,5},{5,4},{6,7},{7,6},{8,9},{9,8},{10,11... | collective-permute-start | bytes 638984 | tf_op jit(solution)/shard_map/ppermute | solution.py:820
  31.3 8.7 %collective-permute-start.5 = (f32[26,8,256]{2,1,0:T(8,128)S(1)}, f32[26,8,256]{2,1,0:T(8,128)S(1)}, u32[]{:S(2)}, u32[]{:S(2)}) collective-permute-start(f32[26,8,256]{2,1,0:T(8,128)S(1)} %get-tuple-element.24), channel_id=1, source_target_pairs={{1,2},{2,1},{3,0},{0,3},{5,6},{6,5},{7,4},{4,7},{9,10},{10,9},{11,... | collective-permute-start | bytes 638984 | tf_op jit(solution)/shard_map/ppermute | solution.py:821
  40.0 0.8 copy-start.7
  40.8 0.7 copy-start.5
  41.5 9.4 %collective-permute-start.6 = (f32[17,8,256]{2,1,0:T(8,128)}, f32[17,8,256]{2,1,0:T(8,128)S(1)}, u32[]{:S(2)}, u32[]{:S(2)}) collective-permute-start(f32[17,8,256]{2,1,0:T(8,128)} %get-tuple-element.25), channel_id=1, source_target_pairs={{0,4},{4,0},{8,12},{12,8},{16,20},{20,16},{24,28},{28,24},{1,5},{5... | collective-permute-start | bytes 417800 | tf_op jit(solution)/shard_map/ppermute | solution.py:826
  48.8 2.0 %collective-permute-start.7 = (f32[17,8,256]{2,1,0:T(8,128)}, f32[17,8,256]{2,1,0:T(8,128)}, u32[]{:S(2)}, u32[]{:S(2)}) collective-permute-start(f32[17,8,256]{2,1,0:T(8,128)} %get-tuple-element.26), channel_id=1, source_target_pairs={{4,8},{8,4},{12,16},{16,12},{20,24},{24,20},{5,9},{9,5},{13,17},{1... | collective-permute-start | bytes 417800 | tf_op jit(solution)/shard_map/ppermute | solution.py:827
  53.6 0.9 copy-start.6
  54.5 0.9 copy-start.8
  76.3 24.1 %collective-permute-start.8 = (f32[4,32,8,256]{3,2,1,0:T(8,128)S(1)}, f32[4,32,8,256]{3,2,1,0:T(8,128)S(1)}, u32[]{:S(2)}, u32[]{:S(2)}) collective-permute-start(f32[4,32,8,256]{3,2,1,0:T(8,128)S(1)} %get-tuple-element.48), channel_id=1, source_target_pairs={{0,4},{4,0},{8,12},{12,8},{16,20},{20,16},{24,28},{28,24},{1,5},{5... | collective-permute-start | bytes 3145736 | tf_op jit(solution)/shard_map/ppermute | solution.py:837
  80.2 20.2 %collective-permute-start.9 = (f32[4,32,8,256]{3,2,1,0:T(8,128)S(1)}, f32[4,32,8,256]{3,2,1,0:T(8,128)S(1)}, u32[]{:S(2)}, u32[]{:S(2)}) collective-permute-start(f32[4,32,8,256]{3,2,1,0:T(8,128)S(1)} %get-tuple-element.47), channel_id=1, source_target_pairs={{4,8},{8,4},{12,16},{16,12},{20,24},{24,20},{5,9},{9,5},{13,17},{1... | collective-permute-start | bytes 3145736 | tf_op jit(solution)/shard_map/ppermute | solution.py:836
  80.9 7.4 %collective-permute-start.10 = (f32[5,5,8,256]{3,2,1,0:T(8,128)S(1)}, f32[5,5,8,256]{3,2,1,0:T(8,128)S(1)}, u32[]{:S(2)}, u32[]{:S(2)}) collective-permute-start(f32[5,5,8,256]{3,2,1,0:T(8,128)S(1)} %get-tuple-element.29), channel_id=1, source_target_pairs={{0,1},{1,0},{2,3},{3,2},{4,5},{5,4},{6,7},{7,6},{8,9},{9,8},{10,11... | collective-permute-start | bytes 614408 | tf_op jit(solution)/shard_map/ppermute | solution.py:781
  83.2 17.2 %copy-start.1 = (f32[3,64,4,4,256]{4,3,2,1,0:T(4,128)S(1)}, f32[3,64,4,4,256]{4,3,2,1,0:T(4,128)}, u32[]{:S(2)}) copy-start(f32[3,64,4,4,256]{4,3,2,1,0:T(4,128)} %param.5) | copy-start | bytes 9437188
  83.2 17.2 %copy-start.9 = (s32[4,4]{1,0:T(4,128)S(1)}, s32[4,4]{1,0:T(4,128)}, u32[]{:S(2)}) copy-start(s32[4,4]{1,0:T(4,128)} %cells_ref.1) | copy-start | bytes 196
  88.6 10.1 %collective-permute-start.11 = (f32[5,5,8,256]{3,2,1,0:T(8,128)S(1)}, f32[5,5,8,256]{3,2,1,0:T(8,128)S(1)}, u32[]{:S(2)}, u32[]{:S(2)}) collective-permute-start(f32[5,5,8,256]{3,2,1,0:T(8,128)S(1)} %pad_maximum_fusion), channel_id=1, source_target_pairs={{1,2},{2,1},{3,0},{0,3},{5,6},{6,5},{7,4},{4,7},{9,10},{10,9},{11,... | collective-permute-start | bytes 614408 | tf_op jit(solution)/shard_map/ppermute | solution.py:786
  98.9 1.5 collective-permute-start.12
  99.0 1.4 collective-permute-start.13
  117.6 1.6 %copy-start.2 = (f32[6144,128]{1,0:T(8,128)}, f32[6144,128]{1,0:T(8,128)S(1)}, u32[]{:S(2)}) copy-start(f32[6144,128]{1,0:T(8,128)S(1)} %get-tuple-element.32.solved_ref) | copy-start | bytes 9437188

commit v3 on v2

--- a/solution.py
+++ b/solution.py
@@ -247,7 +247,15 @@
 CORNERS += [(2, 1, 0, 1), (2, 3, 0, 0)]
 
 
-def pack_kernel(factor_ref, base_ref, own_ref, a_ref, b1_ref, b2_ref, z1_ref, z2_ref):
+def pack_kernel(factor_hbm, base_ref, own_ref, a_ref, b1_ref, b2_ref, z1_ref, z2_ref, factor_ref, arrived):
+    share = factor_ref.shape[0] // 3
+    copies = []
+    for component in range(3):
+        rows = pl.ds(component * share, share)
+        copies.append(
+            pltpu.make_async_copy(factor_hbm.at[rows], factor_ref.at[rows], arrived.at[component])
+        )
+        copies[-1].start()
     odd = x_odd()
     even = 1 - odd
     low = lax.broadcasted_iota(jnp.int32, (8, 128), 0) < 4
@@ -265,7 +273,8 @@
                     own_ref[component, x, 2 * m + 1, :, lanes] = jnp.where(low, swap(first), second)
             return 0
 
-        lax.fori_loop(0, 16, load, 0)
+        copies[component].wait()
+        lax.fori_loop(0, 16, load, 0, unroll=2)
 
     def edges(zz, _):
         for component in range(3):
@@ -341,7 +350,7 @@
 
 def velocity_kernel(
     index_ref, own_ref, base_ref, a_ref, b1_ref, b3_ref, b2_ref, ca_ref, cb_ref, z1_ref, z2_ref,
-    v_ref, bw_ref, s_ref,
+    v_ref, bw_ref, s_ref, pa_ref, pb1_ref, pb2_ref,
     flow_ref, a1_ref, r_ref, v0_ref, va_ref, vb_ref,
 ):
     odd = x_odd()
@@ -535,6 +544,16 @@
             start = tuple(swept(vb_ref, 3, 0)[x + 3] for x in range(4))
         lax.fori_loop(0, HALF, diverge, start, unroll=4)
 
+    even = 1 - odd
+
+    def edges(zz, _):
+        for layer in range(4):
+            pa_ref[layer, zz] = bw_ref[layer + even, zz]
+            (pb1_ref if layer < 2 else pb2_ref)[layer % 2, zz] = bw_ref[layer + odd, zz]
+        return 0
+
+    lax.fori_loop(0, HALF, edges, 0, unroll=4)
+
     def states(layer, _):
         forward, backward = half_states(lambda t: bw_ref[layer, t])
         swapped_forward = [swap(entry) for entry in forward]
@@ -550,9 +569,9 @@
 
 
 def pressure_kernel(
-    index_ref, cells_ref, v_ref, bw_ref, ba_ref, bb_ref, inc_ref, ia_ref, ib_ref, factor_ref,
-    nf_ref, solved_ref, sums_ref,
-    f_ref, i_ref, u_ref, q_ref, t_ref,
+    index_ref, cells_ref, v_ref, bw_ref, ba_ref, b1_ref, b3_ref, b2_ref, inc_ref, ia_ref, ib_ref, factor_ref,
+    nf_hbm, solved_ref, sums_ref,
+    f_ref, i_ref, u_ref, q_ref, t_ref, nf_ref, sent,
 ):
     odd = x_odd()
     stream = lax.axis_index("gx")
@@ -563,17 +582,17 @@
     lower = lower_half()
     shift = shift_of(index_ref)
 
-    def gather(left_ref, right_ref, left_inc, right_inc):
+    def gather(left, right, left_inc, right_inc):
         def body(zz, _):
             for x in range(3):
-                f_ref[x, zz] = left_ref[x, zz]
+                f_ref[x, zz] = mask_left * left(x, zz)
                 f_ref[x + 4, zz] = bw_ref[x + 1, zz]
-                f_ref[x + 8, zz] = right_ref[x + 1, zz]
-            f_ref[3, zz] = bw_ref[0, zz] + 2.0 * left_ref[3, zz]
-            f_ref[7, zz] = mask_right * (right_ref[0, zz] + 2.0 * bw_ref[4, zz])
+                f_ref[x + 8, zz] = mask_right * right(x + 1, zz)
+            f_ref[3, zz] = bw_ref[0, zz] + (2.0 * mask_left) * left(3, zz)
+            f_ref[7, zz] = mask_right * (right(0, zz) + 2.0 * bw_ref[4, zz])
             return 0
 
-        lax.fori_loop(0, HALF, body, 0)
+        lax.fori_loop(0, HALF, body, 0, unroll=4)
         for i in range(POISSON + 1):
             for x in range(3):
                 i_ref[i, x] = left_inc[i, x]
@@ -584,13 +603,25 @@
         for x in range(11):
             f_ref[x, HALF] = swap(jnp.where(lower, i_ref[POISSON, x], f_ref[x, 0]))
 
-    @pl.when(odd == 0)
-    def _():
-        gather(bb_ref, ba_ref, ib_ref, ia_ref)
-
-    @pl.when(odd == 1)
-    def _():
-        gather(ba_ref, bb_ref, ia_ref, ib_ref)
+    def inside(layer, zz):
+        return ba_ref[layer, zz]
+
+    def direct(layer, zz):
+        return b1_ref[layer, zz] if layer < 2 else b2_ref[layer - 2, zz]
+
+    def relayed(layer, zz):
+        return b3_ref[layer, zz] if layer < 2 else b2_ref[layer - 2, zz]
+
+    middle = jnp.logical_or(stream == 3, stream == 4)
+    for parity in (0, 1):
+        for through, outside in ((False, direct), (True, relayed)):
+
+            @pl.when(jnp.logical_and(odd == parity, middle == through))
+            def _(parity=parity, outside=outside):
+                if parity == 0:
+                    gather(outside, inside, ib_ref, ia_ref)
+                else:
+                    gather(inside, outside, ia_ref, ib_ref)
 
     def solve(x, _):
         forward, backward = half_states(lambda t: f_ref[x, t])
@@ -685,8 +716,13 @@
             columns.append(cells)
         return tuple(s + columns[i] * columns[j] for s, (i, j) in zip(sums, couples))
 
-    zero = jnp.zeros((8, 128), jnp.float32)
-    sums = lax.fori_loop(0, 192, update, (zero,) * len(couples), unroll=4)
+    sums = (jnp.zeros((8, 128), jnp.float32),) * len(couples)
+    copies = []
+    for part in range(4):
+        sums = lax.fori_loop(part * 48, part * 48 + 48, update, sums, unroll=4)
+        rows = pl.ds(part * 1536, 1536)
+        copies.append(pltpu.make_async_copy(nf_ref.at[rows], nf_hbm.at[rows], sent.at[part]))
+        copies[-1].start()
     t_ref[...] = jnp.zeros((32, 128), jnp.float32)
     for total, (i, j) in zip(sums, couples):
         t_ref[4 * i + j : 4 * i + j + 1, :] = jnp.sum(total, axis=0, keepdims=True)
@@ -709,21 +745,21 @@
     totals = jnp.sum(t_ref[...], axis=1, keepdims=True)
     spread = lax.broadcasted_iota(jnp.int32, (32, 128), 1) == lax.broadcasted_iota(jnp.int32, (32, 128), 0)
     sums_ref[...] = jnp.sum(jnp.where(spread, totals, 0.0), axis=0, keepdims=True)
-
-
-def gain_kernel(index_ref, sums_ref, gain_ref, solved_ref, out_ref, gram_ref, c_ref):
-    @pl.when(pl.program_id(0) == 0)
-    def _():
-        totals = jnp.sum(sums_ref[...], axis=0, keepdims=True)
-        lanes = lax.broadcasted_iota(jnp.int32, (1, 128), 1)
-        shift = shift_of(index_ref)
-        for i in range(4):
-            for j in range(4):
-                c_ref[i, j] = 2.0 * shift * jnp.sum(jnp.where(lanes == 16 + 4 * i + j, totals, 0.0))
-                at = 4 * min(i, j) + max(i, j)
-                gram_ref[i, j] = jnp.sum(jnp.where(lanes == at, totals, 0.0)) / 6291456.0
-
-    table = [[c_ref[i, j] for j in range(4)] for i in range(4)]
+    for copy in copies:
+        copy.wait()
+
+
+def gain_kernel(index_ref, sums_ref, gain_ref, solved_ref, out_hbm, gram_ref, out_ref, sent):
+    totals = jnp.sum(sums_ref[...], axis=0, keepdims=True)
+    lanes = lax.broadcasted_iota(jnp.int32, (1, 128), 1)
+    shift = shift_of(index_ref)
+
+    def entry(at):
+        return jnp.sum(jnp.where(lanes == at, totals, 0.0), axis=1, keepdims=True)
+
+    table = [
+        [jnp.broadcast_to(2.0 * shift * entry(16 + 4 * i + j), (8, 128)) for j in range(4)] for i in range(4)
+    ]
 
     def body(block, _):
         rows = [pl.ds(pl.multiple_of(block * 32 + 8 * j, 8), 8) for j in range(4)]
@@ -735,20 +771,42 @@
             out_ref[rows[i], :] = total
         return 0
 
-    lax.fori_loop(0, out_ref.shape[0] // 32, body, 0, unroll=2)
-
-
-def call(kernel, outputs, scratch, operands, smalls, flops):
+    copies = []
+    for part in range(6):
+        lax.fori_loop(part * 32, part * 32 + 32, body, 0, unroll=4)
+        rows = pl.ds(part * 1024, 1024)
+        copies.append(pltpu.make_async_copy(out_ref.at[rows], out_hbm.at[rows], sent.at[part]))
+        copies[-1].start()
+    row = lax.broadcasted_iota(jnp.int32, (4, 4), 0)
+    column = lax.broadcasted_iota(jnp.int32, (4, 4), 1)
+    gram = jnp.zeros((4, 4), jnp.float32)
+    for i in range(4):
+        for j in range(4):
+            value = entry(4 * min(i, j) + max(i, j)) / 6291456.0
+            gram = gram + jnp.where((row == i) & (column == j), value, 0.0)
+    gram_ref[...] = gram
+    for copy in copies:
+        copy.wait()
+
+
+def call(kernel, outputs, scratch, operands, smalls, flops, far_in=(), far_out=(), signals=(), least=0):
     arrays = [jax.ShapeDtypeStruct(shape, jnp.float32) for shape in outputs]
     places = [pl.BlockSpec(memory_space=pltpu.SMEM)] * smalls
     places += [pl.BlockSpec(memory_space=pltpu.VMEM)] * (len(operands) - smalls)
+    results = [pl.BlockSpec(memory_space=pltpu.VMEM)] * len(outputs)
+    for place in far_in:
+        places[place] = pl.BlockSpec(memory_space=pltpu.HBM)
+    for place in far_out:
+        results[place] = pl.BlockSpec(memory_space=pltpu.HBM)
+    room = sum(4 * math.prod(shape) for shape in scratch) + (2 << 20)
     moved = sum(4 * math.prod(shape) for shape in outputs) + sum(4 * math.prod(o.shape) for o in operands)
     return pl.pallas_call(
         kernel,
         out_shape=arrays,
         in_specs=places,
-        out_specs=[pl.BlockSpec(memory_space=pltpu.VMEM)] * len(outputs),
-        scratch_shapes=[pltpu.VMEM(shape, jnp.float32) for shape in scratch],
+        out_specs=results,
+        scratch_shapes=[pltpu.VMEM(shape, jnp.float32) for shape in scratch]
+        + [pltpu.SemaphoreType.DMA((count,)) for count in signals],
         compiler_params=pltpu.CompilerParams(vmem_limit_bytes=26 << 20),
         cost_estimate=pl.CostEstimate(flops=flops, bytes_accessed=moved, transcendentals=0),
     )(*operands)
@@ -774,11 +832,8 @@
     )
 
 
-def ring_states(states, own_even):
-    near = [(0, 1), (1, 0), (2, 3), (3, 2)]
-    far = [(1, 2), (2, 1), (3, 0), (0, 3)]
+def ring_states(states, partner, own_even, far):
     upper = jnp.arange(8)[None, None, :, None] >= 4
-    partner = lax.ppermute(states, "gz", near)
     first = upper == own_even
     nearer = jnp.where(first, partner, states)
     farther = jnp.where(first, states, partner)
@@ -814,7 +869,7 @@
     own, a, b1, b2, z1, z2 = call(
         pack_kernel,
         [(3, 4, HALF, *cell), (312, *cell), (PART, *cell), (312 - PART, *cell), (26, *cell), (26, *cell)],
-        [], [factor_rows, base_rows], 0, 10**6,
+        [factor_rows.shape], [factor_rows, base_rows], 0, 10**6, far_in=(0,), signals=(3,),
     )
     b1_in = lax.ppermute(b1, "gx", send_round)
     z1 = lax.ppermute(z1, "gz", near)
@@ -825,45 +880,45 @@
     ca, cb = call(corner_kernel, [(corners, *cell)] * 2, [], [z1, z2], 0, 10**5)
     ca = lax.ppermute(ca, "gx", swap_in)
     cb = lax.ppermute(cb, "gx", swap_out)
+    b1_in, z1, z2 = lax.optimization_barrier((b1_in, z1, z2))
     b3_in = lax.ppermute(b1_in, "gx", forward_round)
     block = (10, 39, *cell)
-    velocity, sides, states = call(
+    velocity, sides, states, pa, pb1, pb2 = call(
         velocity_kernel,
-        [(3, 4, HALF, *cell), (5, HALF, *cell), (POISSON + 1, 5, *cell)],
+        [(3, 4, HALF, *cell), (5, HALF, *cell), (POISSON + 1, 5, *cell), (4, HALF, *cell)]
+        + [(2, HALF, *cell)] * 2,
         [(10, 80, 256)] + [block] * 5,
         [shift_index, own, base_rows, a_in, b1_in, b3_in, b2_in, ca, cb, z1, z2], 1, 10**8,
     )
-    side_b = lax.ppermute(lax.dynamic_slice_in_dim(sides, odd, 4, axis=0), "gx", swap_out)
-    side_a = lax.ppermute(lax.dynamic_slice_in_dim(sides, 1 - odd, 4, axis=0), "gx", swap_in)
-    entering = ring_states(states, own_even)
+    pb1_in = lax.ppermute(pb1, "gx", send_round)
+    pb2_in = lax.ppermute(pb2, "gx", swap_out)
+    partner = lax.ppermute(states, "gz", near)
+    pb1_in, partner = lax.optimization_barrier((pb1_in, partner))
+    pa_in = lax.ppermute(pa, "gx", swap_in)
+    pb3_in = lax.ppermute(pb1_in, "gx", forward_round)
+    entering = ring_states(states, partner, own_even, far)
     enter_b = lax.ppermute(lax.dynamic_slice_in_dim(entering, odd, 4, axis=1), "gx", swap_out)
     enter_a = lax.ppermute(lax.dynamic_slice_in_dim(entering, 1 - odd, 4, axis=1), "gx", swap_in)
     block = (11, HALF + 1, *cell)
     new_rows, solved, sums = call(
         pressure_kernel,
         [factor_rows.shape, factor_rows.shape, (1, 128)],
-        [block, (POISSON + 1, 11, *cell), (POISSON, HALF + 1, *cell), (POISSON, *block), (32, 128)],
-        [shift_index, sensor_cells, velocity, sides, side_a, side_b, entering, enter_a, enter_b, factor_rows],
-        2, 10**8,
+        [block, (POISSON + 1, 11, *cell), (POISSON, HALF + 1, *cell), (POISSON, *block), (32, 128)]
+        + [factor_rows.shape],
+        [shift_index, sensor_cells, velocity, sides, pa_in, pb1_in, pb3_in, pb2_in]
+        + [entering, enter_a, enter_b, factor_rows],
+        2, 10**8, far_out=(0,), signals=(4,),
     )
     devices = lax.axis_size("gx") * lax.axis_size("gz")
     shared = lax.all_to_all(
         jnp.broadcast_to(sums[None], (devices, 1, 128)), ("gx", "gz"), split_axis=0, concat_axis=0, tiled=True
     )
-    chunk = 768
-    whole = pl.BlockSpec(memory_space=pltpu.SMEM)
-    rows = pl.BlockSpec((chunk, 128), lambda i: (i, 0))
-    new_gain, gram = pl.pallas_call(
+    new_gain, gram = call(
         gain_kernel,
-        grid=(gain_rows.shape[0] // chunk,),
-        in_specs=[whole, pl.BlockSpec((devices, 128), lambda i: (0, 0)), rows, rows],
-        out_specs=[rows, whole],
-        out_shape=[
-            jax.ShapeDtypeStruct(gain_rows.shape, jnp.float32),
-            jax.ShapeDtypeStruct((4, 4), jnp.float32),
-        ],
-        scratch_shapes=[pltpu.SMEM((4, 4), jnp.float32)],
-    )(shift_index, shared.reshape(devices, 128), gain_rows, solved)
+        [gain_rows.shape, (4, 4)],
+        [gain_rows.shape], [shift_index, shared.reshape(devices, 128), gain_rows, solved], 1, 10**7,
+        far_out=(0,), signals=(6,),
+    )
     head = factor.shape[:3]
     return (from_rows(new_rows, head), from_rows(new_gain, head), gram)
 

time: 150 us -> 138 us (0.920)
  Pallas kernels: 49.3 us -> 39.8 us
  blocking collectives: 22.9 us -> 20.1 us
  waiting for transfers between devices: 36.1 us -> 38.8 us
  local copies, waits for them, and re-layouts: 7.33 us -> 5.73 us
    ppermute x1, waiting for transfers between devices: 2.73 us -> 20 us  [fast_shards(): b3_in = lax.ppermute(b1_in, 'gx', forward_round)]
    ppermute x1, waiting for transfers between devices: 15.9 us -> 2.88 us  [fast_shards(): b1_in = lax.ppermute(b1, 'gx', send_round)]
    pallas_call x5, Pallas kernels: 49.3 us -> 39.8 us  [call(): pl.pallas_call(kernel, out_shape=arrays, in_specs=places, out_specs=resul...]
    ppermute x1, starting transfers between devices: 7.37 us -> 4.12 us  [fast_shards(): ca = lax.ppermute(ca, 'gx', swap_in)]
    ppermute x1, waiting for transfers between devices: 4.41 us -> 7.59 us  [fast_shards(): z2 = lax.ppermute(z2, 'gz', far)]
    ppermute x1, starting transfers between devices: 0.07 us -> 3.02 us  [fast_shards(): lax.ppermute(lax.dynamic_slice_in_dim(entering, 1 - odd, 4, axis=1), 'gx'...]
    ppermute x1, waiting for transfers between devices: 5.45 us -> 2.6 us  [ring_states(): other = lax.ppermute(jnp.concatenate([joined, states[POISSON:]]), 'gz', far)]
    all_to_all x1, blocking collectives: 22.9 us -> 20.1 us  [fast_shards(): lax.all_to_all(jnp.broadcast_to(sums[None], (devices, 1, 128)), ('gx', 'g...]
  transfers between devices with their start and end apart: 14 -> 16, of which waited for: 7 -> 7; matrix products, arithmetic and copies ran while one was open for 0% -> 0% of each run, Pallas kernels for 1% -> 0%
where the time goes in v3:
time: 138 us
  Pallas kernels  39.8 us (29%)
  waiting for transfers between devices  38.8 us (28%)
  starting transfers between devices  31.6 us (23%)
  blocking collectives  20.1 us (15%)
  local copies, waits for them, and re-layouts  5.73 us (4%)
  between operations  1.59 us (1%)
    pallas_call x5, Pallas kernels, call(): pl.pallas_call(kernel, out_shape=arrays, in_specs=places, out_specs=resul...  39.8 us
    all_to_all x1, blocking collectives, fast_shards(): lax.all_to_all(jnp.broadcast_to(sums[None], (devices, 1, 128)), ('gx', 'g...  20.1 us
    ppermute x1, waiting for transfers between devices, fast_shards(): b3_in = lax.ppermute(b1_in, 'gx', forward_round)  20 us
    ppermute x1, waiting for transfers between devices, fast_shards(): z2 = lax.ppermute(z2, 'gz', far)  7.59 us
    unnamed x21, local copies, waits for them, and re-layouts  5.68 us
    ppermute x1, waiting for transfers between devices, fast_shards(): pb1_in = lax.ppermute(pb1, 'gx', send_round)  4.14 us
    ppermute x1, starting transfers between devices, fast_shards(): ca = lax.ppermute(ca, 'gx', swap_in)  4.12 us
    ppermute x1, starting transfers between devices, fast_shards(): pa_in = lax.ppermute(pa, 'gx', swap_in)  4.04 us
  transfers between devices with their start and end apart: 16, of which 7 were waited for; matrix products, arithmetic and copies ran while one was open for 0% of the time, Pallas kernels for 0%

profile of v3, /device:TPU:0, one launch (start us, length us, event | category | flops | bytes accessed | tf_op | source)
XLA Modules:
  0.0 138.1 jit_solution(2917868207694124548)
XLA Ops:
  0.6 0.0 copy-start
  0.6 1.9 %copy-done = f32[3,64,4,4,256]{4,3,2,1,0:T(4,128)S(1)} copy-done((f32[3,64,4,4,256]{4,3,2,1,0:T(4,128)S(1)}, f32[3,64,4,4,256]{4,3,2,1,0:T(4,128)}, u32[]{:S(2)}) %copy-start) | copy-done | bytes 3145752
  2.5 0.0 copy-start.5
  2.5 0.9 copy-done.5
  3.5 0.0 copy-start.6
  3.5 1.6 %shard_map.76 = (f32[3,4,32,8,256]{4,3,2,1,0:T(8,128)S(1)}, f32[312,8,256]{2,1,0:T(8,128)S(1)}, f32[152,8,256]{2,1,0:T(8,128)S(1)}, f32[160,8,256]{2,1,0:T(8,128...) custom-call(f32[6144,128]{1,0:T(8,128)S(1)} %bitcast.27, f32[512,128]{1,0:T(8,128)S(1)} %bitcast.30), custom_call_target="tpu_custom_call" | custom-call | flops 1000000 | bytes 12091392 | tf_op jit(solution)/shard_map/pallas_call | solution.py:803
  5.1 0.5 collective-permute-start
  5.6 1.3 collective-permute-start.1
  6.9 2.7 %collective-permute-start.2 = (f32[26,8,256]{2,1,0:T(8,128)S(1)}, f32[26,8,256]{2,1,0:T(8,128)S(1)}, u32[]{:S(2)}, u32[]{:S(2)}) collective-permute-start(f32[26,8,256]{2,1,0:T(8,128)S(1)} %get-tuple-element.30), channel_id=1, source_target_pairs={{0,1},{1,0},{2,3},{3,2},{4,5},{5,4},{6,7},{7,6},{8,9},{9,8},{10,11... | collective-permute-start | bytes 638984 | tf_op jit(solution)/shard_map/ppermute | solution.py:875
  9.5 2.5 %collective-permute-start.3 = (f32[26,8,256]{2,1,0:T(8,128)S(1)}, f32[26,8,256]{2,1,0:T(8,128)S(1)}, u32[]{:S(2)}, u32[]{:S(2)}) collective-permute-start(f32[26,8,256]{2,1,0:T(8,128)S(1)} %get-tuple-element.31), channel_id=1, source_target_pairs={{1,2},{2,1},{3,0},{0,3},{5,6},{6,5},{7,4},{4,7},{9,10},{10,9},{11,... | collective-permute-start | bytes 638984 | tf_op jit(solution)/shard_map/ppermute | solution.py:876
  12.0 0.7 collective-permute-start.5
  12.7 1.1 collective-permute-done.2.z1_ref
  13.9 7.6 %collective-permute-done.3.z2_ref = f32[26,8,256]{2,1,0:T(8,128)S(1)} collective-permute-done((f32[26,8,256]{2,1,0:T(8,128)S(1)}, f32[26,8,256]{2,1,0:T(8,128)S(1)}, u32[]{:S(2)}, u32[]{:S(2)}) %collective-permute-start.3) | collective-permute-done | bytes 213024 | tf_op jit(solution)/shard_map/ppermute | solution.py:876
  21.5 2.9 %collective-permute-done.1.b1_ref = f32[152,8,256]{2,1,0:T(8,128)S(1)} collective-permute-done((f32[152,8,256]{2,1,0:T(8,128)S(1)}, f32[152,8,256]{2,1,0:T(8,128)S(1)}, u32[]{:S(2)}, u32[]{:S(2)}) %collective-permute-start.1) | collective-permute-done | bytes 1245216 | tf_op jit(solution)/shard_map/ppermute | solution.py:874
  24.4 2.8 %collective-permute-start.4 = (f32[152,8,256]{2,1,0:T(8,128)S(1)}, f32[152,8,256]{2,1,0:T(8,128)S(1)}, u32[]{:S(2)}, u32[]{:S(2)}) collective-permute-start(f32[152,8,256]{2,1,0:T(8,128)S(1)} %collective-permute-done.1.b1_ref), channel_id=1, source_target_pairs={{28,16},{0,12},{29,17},{1,13},{30,18},{2,14},{31,19},{3,15}} | collective-permute-start | bytes 3735560 | tf_op jit(solution)/shard_map/ppermute | solution.py:884
  27.1 0.1 shard_map.77
  27.2 4.1 %collective-permute-start.6 = (f32[17,8,256]{2,1,0:T(8,128)S(1)}, f32[17,8,256]{2,1,0:T(8,128)S(1)}, u32[]{:S(2)}, u32[]{:S(2)}) collective-permute-start(f32[17,8,256]{2,1,0:T(8,128)S(1)} %get-tuple-element.34), channel_id=1, source_target_pairs={{0,4},{4,0},{8,12},{12,8},{16,20},{20,16},{24,28},{28,24},{1,5},{5... | collective-permute-start | bytes 417800 | tf_op jit(solution)/shard_map/ppermute | solution.py:881
  31.3 0.7 collective-permute-start.7
  32.6 0.0 collective-permute-done.6.ca_ref
  32.6 0.0 collective-permute-done.7.cb_ref
  32.7 0.0 collective-permute-done.5.b2_ref
  32.7 20.0 %collective-permute-done.4.b3_ref = f32[152,8,256]{2,1,0:T(8,128)S(1)} collective-permute-done((f32[152,8,256]{2,1,0:T(8,128)S(1)}, f32[152,8,256]{2,1,0:T(8,128)S(1)}, u32[]{:S(2)}, u32[]{:S(2)}) %collective-permute-start.4) | collective-permute-done | bytes 1245216 | tf_op jit(solution)/shard_map/ppermute | solution.py:884
  52.7 0.0 collective-permute-done.a_ref
  52.7 0.0 copy-done.6
  52.7 18.7 %shard_map.78 = (f32[3,4,32,8,256]{4,3,2,1,0:T(8,128)S(1)}, f32[5,32,8,256]{3,2,1,0:T(8,128)S(1)}, f32[5,5,8,256]{3,2,1,0:T(8,128)S(1)}, f32[4,32,8,256]{3,2,1,0...) custom-call(s32[1]{0:T(128)S(6)} %copy.22.index_ref, ...), custom_call_target="tpu_custom_call" | custom-call | flops 100000000 | bytes 17227780 | tf_op jit(solution)/shard_map/pallas_call | solution.py:803
  71.4 0.0 copy-start.3
  71.5 1.1 copy-done.3
  72.5 0.0 copy-start.8
  72.5 1.0 copy-done.8
  73.5 0.0 copy-start.9
  73.5 0.8 copy-done.9
  74.3 1.3 collective-permute-start.9
  75.6 1.6 %collective-permute-start.10 = (f32[5,5,8,256]{3,2,1,0:T(8,128)S(1)}, f32[5,5,8,256]{3,2,1,0:T(8,128)S(1)}, u32[]{:S(2)}, u32[]{:S(2)}) collective-permute-start(f32[5,5,8,256]{3,2,1,0:T(8,128)S(1)} %get-tuple-element.42), channel_id=1, source_target_pairs={{0,1},{1,0},{2,3},{3,2},{4,5},{5,4},{6,7},{7,6},{8,9},{9,8},{10,11... | collective-permute-start | bytes 614408 | tf_op jit(solution)/shard_map/ppermute | solution.py:895
  77.2 4.0 %collective-permute-start.8 = (f32[4,32,8,256]{3,2,1,0:T(8,128)}, f32[4,32,8,256]{3,2,1,0:T(8,128)S(1)}, u32[]{:S(2)}, u32[]{:S(2)}) collective-permute-start(f32[4,32,8,256]{3,2,1,0:T(8,128)} %copy-done.8), channel_id=1, source_target_pairs={{0,4},{4,0},{8,12},{12,8},{16,20},{20,16},{24,28},{28,24},{1,5},{5... | collective-permute-start | bytes 3145736 | tf_op jit(solution)/shard_map/ppermute | solution.py:897
  81.3 0.7 collective-permute-start.12
  82.0 0.0 copy-start.1
  82.0 0.0 copy-start.4
  82.0 0.0 copy-start.7
  82.0 0.0 collective-permute-done.10
  82.0 4.1 %collective-permute-done.9.b1_ref = f32[2,32,8,256]{3,2,1,0:T(8,128)} collective-permute-done((f32[2,32,8,256]{3,2,1,0:T(8,128)}, f32[2,32,8,256]{3,2,1,0:T(8,128)}, u32[]{:S(2)}, u32[]{:S(2)}) %collective-permute-start.9) | collective-permute-done | bytes 524320 | tf_op jit(solution)/shard_map/ppermute | solution.py:893
  86.2 0.1 broadcast_select_fusion
  86.3 0.1 fusion.2
  86.4 3.7 %collective-permute-start.13 = (f32[5,5,8,256]{3,2,1,0:T(8,128)S(1)}, f32[5,5,8,256]{3,2,1,0:T(8,128)S(1)}, u32[]{:S(2)}, u32[]{:S(2)}) collective-permute-start(f32[5,5,8,256]{3,2,1,0:T(8,128)S(1)} %pad_maximum_fusion), channel_id=1, source_target_pairs={{1,2},{2,1},{3,0},{0,3},{5,6},{6,5},{7,4},{4,7},{9,10},{10,9},{11,... | collective-permute-start | bytes 614408 | tf_op jit(solution)/shard_map/ppermute | solution.py:841
  90.1 1.4 %collective-permute-start.11 = (f32[2,32,8,256]{3,2,1,0:T(8,128)}, f32[2,32,8,256]{3,2,1,0:T(8,128)S(1)}, u32[]{:S(2)}, u32[]{:S(2)}) collective-permute-start(f32[2,32,8,256]{3,2,1,0:T(8,128)} %collective-permute-done.9.b1_ref), channel_id=1, source_target_pairs={{28,16},{0,12},{29,17},{1,13},{30,18},{2,14},{31,19},{3,15}} | collective-permute-start | bytes 1572872 | tf_op jit(solution)/shard_map/ppermute | solution.py:898
  91.5 2.6 %collective-permute-done.13 = f32[5,5,8,256]{3,2,1,0:T(8,128)S(1)} collective-permute-done((f32[5,5,8,256]{3,2,1,0:T(8,128)S(1)}, f32[5,5,8,256]{3,2,1,0:T(8,128)S(1)}, u32[]{:S(2)}, u32[]{:S(2)}) %collective-permute-start.13) | collective-permute-done | bytes 204832 | tf_op jit(solution)/shard_map/ppermute | solution.py:841
  94.2 0.1 fusion.1
  94.4 3.0 %collective-permute-start.14 = (f32[5,4,8,256]{3,2,1,0:T(8,128)S(1)}, f32[5,4,8,256]{3,2,1,0:T(8,128)S(1)}, u32[]{:S(2)}, u32[]{:S(2)}) collective-permute-start(f32[5,4,8,256]{3,2,1,0:T(8,128)S(1)} %get-tuple-element.64), channel_id=1, source_target_pairs={{0,4},{4,0},{8,12},{12,8},{16,20},{20,16},{24,28},{28,24},{1,5},{5... | collective-permute-start | bytes 491528 | tf_op jit(solution)/shard_map/ppermute | solution.py:901
  97.4 0.7 collective-permute-start.15
  98.1 0.0 collective-permute-done.12.b2_ref
  98.1 0.4 collective-permute-done.14.ia_ref
  98.4 0.0 collective-permute-done.15.ib_ref
  98.4 0.0 collective-permute-done.11.b3_ref
  98.5 0.0 collective-permute-done.8.ba_ref
  98.5 0.0 copy-done.1
  98.5 0.0 copy-done.4
  98.5 0.0 copy-done.7
  98.5 0.0 copy-start.2
  98.5 16.9 %shard_map.79 = (f32[6144,128]{1,0:T(8,128)}, f32[6144,128]{1,0:T(8,128)S(1)}, f32[1,128]{1,0:T(1,128)S(1)}) custom-call(s32[1]{0:T(128)S(6)} %copy.22.index_ref, s32[4,4]{1,0:T(4,128)S(1)} %copy-done.7, f32[3,4,32,8,256]{4,3,2,1,0:T(8,128)S(1)} %get-tuple-element.38.v_ref, f32[5,32,8,256]{3,2,1,0:T(8,128)S(1)} %copy-done.4, ...), custom_call_target="tpu_custom_call" | custom-call | flops 100000000 | bytes 17048132 | tf_op jit(solution)/shard_map/pallas_call | solution.py:803
  115.4 20.1 %all_to_all.5 = f32[32,1,128]{2,1,0:T(1,128)S(1)} all-to-all(f32[32,1,128]{2,1,0:T(1,128)S(1)} %broadcast_in_dim.31), channel_id=1, replica_groups=mesh['gx'=8,'gz'=4] {'gx','gz'}, dimensions={0} | all-to-all | bytes 32768 | tf_op jit(solution)/shard_map/all_to_all | solution.py:913
  135.5 0.0 copy-done.2
  135.5 2.6 %shard_map.80 = (f32[6144,128]{1,0:T(8,128)}, f32[4,4]{1,0:T(4,128)}) custom-call(s32[1]{0:T(128)S(6)} %copy.22.index_ref, f32[32,128]{1,0:T(8,128)S(1)} %bitcast.32, f32[6144,128]{1,0:T(8,128)S(1)} %bitcast.29, f32[6144,128]{1,0:T(8,128)S(1)} %get-tuple-element.48.solved_ref), custom_call_target="tpu_custom_call" | custom-call | flops 10000000 | bytes 9453636 | tf_op jit(solution)/shard_map/pallas_call | solution.py:803
  (13 shorter events, 0.2 us)
Async XLA Ops:
  0.6 1.9 %copy-start = (f32[3,64,4,4,256]{4,3,2,1,0:T(4,128)S(1)}, f32[3,64,4,4,256]{4,3,2,1,0:T(4,128)}, u32[]{:S(2)}) copy-start(f32[3,64,4,4,256]{4,3,2,1,0:T(4,128)} %param.5) | copy-start | bytes 9437188
  2.5 0.9 copy-start.5
  3.5 49.2 %copy-start.6 = (f32[64,4,256]{2,1,0:T(4,128)S(1)}, f32[64,4,256]{2,1,0:T(4,128)}, u32[]{:S(2)}) copy-start(f32[64,4,256]{2,1,0:T(4,128)} %param.7) | copy-start | bytes 786436
  5.1 47.6 %collective-permute-start = (f32[312,8,256]{2,1,0:T(8,128)S(1)}, f32[312,8,256]{2,1,0:T(8,128)S(1)}, u32[]{:S(2)}, u32[]{:S(2)}) collective-permute-start(f32[312,8,256]{2,1,0:T(8,128)S(1)} %get-tuple-element.28), channel_id=1, source_target_pairs={{0,4},{4,0},{8,12},{12,8},{16,20},{20,16},{24,28},{28,24},{1,5},{5... | collective-permute-start | bytes 7667720 | tf_op jit(solution)/shard_map/ppermute | solution.py:878
  5.6 18.8 %collective-permute-start.1 = (f32[152,8,256]{2,1,0:T(8,128)S(1)}, f32[152,8,256]{2,1,0:T(8,128)S(1)}, u32[]{:S(2)}, u32[]{:S(2)}) collective-permute-start(f32[152,8,256]{2,1,0:T(8,128)S(1)} %get-tuple-element.29), channel_id=1, source_target_pairs={{4,8},{8,4},{20,24},{24,20},{12,28},{16,0},{5,9},{9,5},{21,25},{25... | collective-permute-start | bytes 3735560 | tf_op jit(solution)/shard_map/ppermute | solution.py:874
  6.9 7.0 %collective-permute-start.2 = (f32[26,8,256]{2,1,0:T(8,128)S(1)}, f32[26,8,256]{2,1,0:T(8,128)S(1)}, u32[]{:S(2)}, u32[]{:S(2)}) collective-permute-start(f32[26,8,256]{2,1,0:T(8,128)S(1)} %get-tuple-element.30), channel_id=1, source_target_pairs={{0,1},{1,0},{2,3},{3,2},{4,5},{5,4},{6,7},{7,6},{8,9},{9,8},{10,11... | collective-permute-start | bytes 638984 | tf_op jit(solution)/shard_map/ppermute | solution.py:875
  9.5 12.0 %collective-permute-start.3 = (f32[26,8,256]{2,1,0:T(8,128)S(1)}, f32[26,8,256]{2,1,0:T(8,128)S(1)}, u32[]{:S(2)}, u32[]{:S(2)}) collective-permute-start(f32[26,8,256]{2,1,0:T(8,128)S(1)} %get-tuple-element.31), channel_id=1, source_target_pairs={{1,2},{2,1},{3,0},{0,3},{5,6},{6,5},{7,4},{4,7},{9,10},{10,9},{11,... | collective-permute-start | bytes 638984 | tf_op jit(solution)/shard_map/ppermute | solution.py:876
  12.0 20.6 %collective-permute-start.5 = (f32[160,8,256]{2,1,0:T(8,128)S(1)}, f32[160,8,256]{2,1,0:T(8,128)S(1)}, u32[]{:S(2)}, u32[]{:S(2)}) collective-permute-start(f32[160,8,256]{2,1,0:T(8,128)S(1)} %get-tuple-element.33), channel_id=1, source_target_pairs={{4,8},{8,4},{12,16},{16,12},{20,24},{24,20},{5,9},{9,5},{13,17},{1... | collective-permute-start | bytes 3932168 | tf_op jit(solution)/shard_map/ppermute | solution.py:877
  24.4 28.3 %collective-permute-start.4 = (f32[152,8,256]{2,1,0:T(8,128)S(1)}, f32[152,8,256]{2,1,0:T(8,128)S(1)}, u32[]{:S(2)}, u32[]{:S(2)}) collective-permute-start(f32[152,8,256]{2,1,0:T(8,128)S(1)} %collective-permute-done.1.b1_ref), channel_id=1, source_target_pairs={{28,16},{0,12},{29,17},{1,13},{30,18},{2,14},{31,19},{3,15}} | collective-permute-start | bytes 3735560 | tf_op jit(solution)/shard_map/ppermute | solution.py:884
  27.2 5.4 %collective-permute-start.6 = (f32[17,8,256]{2,1,0:T(8,128)S(1)}, f32[17,8,256]{2,1,0:T(8,128)S(1)}, u32[]{:S(2)}, u32[]{:S(2)}) collective-permute-start(f32[17,8,256]{2,1,0:T(8,128)S(1)} %get-tuple-element.34), channel_id=1, source_target_pairs={{0,4},{4,0},{8,12},{12,8},{16,20},{20,16},{24,28},{28,24},{1,5},{5... | collective-permute-start | bytes 417800 | tf_op jit(solution)/shard_map/ppermute | solution.py:881
  31.3 1.3 collective-permute-start.7
  71.4 1.1 copy-start.3
  72.5 1.0 copy-start.8
  73.5 0.8 copy-start.9
  74.3 11.9 %collective-permute-start.9 = (f32[2,32,8,256]{3,2,1,0:T(8,128)}, f32[2,32,8,256]{3,2,1,0:T(8,128)}, u32[]{:S(2)}, u32[]{:S(2)}) collective-permute-start(f32[2,32,8,256]{3,2,1,0:T(8,128)} %get-tuple-element.41), channel_id=1, source_target_pairs={{4,8},{8,4},{20,24},{24,20},{12,28},{16,0},{5,9},{9,5},{21,25},{25... | collective-permute-start | bytes 1572872 | tf_op jit(solution)/shard_map/ppermute | solution.py:893
  75.6 6.4 %collective-permute-start.10 = (f32[5,5,8,256]{3,2,1,0:T(8,128)S(1)}, f32[5,5,8,256]{3,2,1,0:T(8,128)S(1)}, u32[]{:S(2)}, u32[]{:S(2)}) collective-permute-start(f32[5,5,8,256]{3,2,1,0:T(8,128)S(1)} %get-tuple-element.42), channel_id=1, source_target_pairs={{0,1},{1,0},{2,3},{3,2},{4,5},{5,4},{6,7},{7,6},{8,9},{9,8},{10,11... | collective-permute-start | bytes 614408 | tf_op jit(solution)/shard_map/ppermute | solution.py:895
  77.2 21.2 %collective-permute-start.8 = (f32[4,32,8,256]{3,2,1,0:T(8,128)}, f32[4,32,8,256]{3,2,1,0:T(8,128)S(1)}, u32[]{:S(2)}, u32[]{:S(2)}) collective-permute-start(f32[4,32,8,256]{3,2,1,0:T(8,128)} %copy-done.8), channel_id=1, source_target_pairs={{0,4},{4,0},{8,12},{12,8},{16,20},{20,16},{24,28},{28,24},{1,5},{5... | collective-permute-start | bytes 3145736 | tf_op jit(solution)/shard_map/ppermute | solution.py:897
  81.3 16.8 %collective-permute-start.12 = (f32[2,32,8,256]{3,2,1,0:T(8,128)}, f32[2,32,8,256]{3,2,1,0:T(8,128)S(1)}, u32[]{:S(2)}, u32[]{:S(2)}) collective-permute-start(f32[2,32,8,256]{3,2,1,0:T(8,128)} %copy-done.9), channel_id=1, source_target_pairs={{4,8},{8,4},{12,16},{16,12},{20,24},{24,20},{5,9},{9,5},{13,17},{1... | collective-permute-start | bytes 1572872 | tf_op jit(solution)/shard_map/ppermute | solution.py:894
  82.0 16.5 %copy-start.1 = (f32[3,64,4,4,256]{4,3,2,1,0:T(4,128)S(1)}, f32[3,64,4,4,256]{4,3,2,1,0:T(4,128)}, u32[]{:S(2)}) copy-start(f32[3,64,4,4,256]{4,3,2,1,0:T(4,128)} %param.5) | copy-start | bytes 9437188
  82.0 16.5 %copy-start.4 = (f32[5,32,8,256]{3,2,1,0:T(8,128)S(1)}, f32[5,32,8,256]{3,2,1,0:T(8,128)}, u32[]{:S(2)}) copy-start(f32[5,32,8,256]{3,2,1,0:T(8,128)} %copy-done.3) | copy-start | bytes 3932164
  82.0 16.5 %copy-start.7 = (s32[4,4]{1,0:T(4,128)S(1)}, s32[4,4]{1,0:T(4,128)}, u32[]{:S(2)}) copy-start(s32[4,4]{1,0:T(4,128)} %cells_ref.1) | copy-start | bytes 196
  86.4 7.7 %collective-permute-start.13 = (f32[5,5,8,256]{3,2,1,0:T(8,128)S(1)}, f32[5,5,8,256]{3,2,1,0:T(8,128)S(1)}, u32[]{:S(2)}, u32[]{:S(2)}) collective-permute-start(f32[5,5,8,256]{3,2,1,0:T(8,128)S(1)} %pad_maximum_fusion), channel_id=1, source_target_pairs={{1,2},{2,1},{3,0},{0,3},{5,6},{6,5},{7,4},{4,7},{9,10},{10,9},{11,... | collective-permute-start | bytes 614408 | tf_op jit(solution)/shard_map/ppermute | solution.py:841
  90.1 8.4 %collective-permute-start.11 = (f32[2,32,8,256]{3,2,1,0:T(8,128)}, f32[2,32,8,256]{3,2,1,0:T(8,128)S(1)}, u32[]{:S(2)}, u32[]{:S(2)}) collective-permute-start(f32[2,32,8,256]{3,2,1,0:T(8,128)} %collective-permute-done.9.b1_ref), channel_id=1, source_target_pairs={{28,16},{0,12},{29,17},{1,13},{30,18},{2,14},{31,19},{3,15}} | collective-permute-start | bytes 1572872 | tf_op jit(solution)/shard_map/ppermute | solution.py:898
  94.4 4.0 %collective-permute-start.14 = (f32[5,4,8,256]{3,2,1,0:T(8,128)S(1)}, f32[5,4,8,256]{3,2,1,0:T(8,128)S(1)}, u32[]{:S(2)}, u32[]{:S(2)}) collective-permute-start(f32[5,4,8,256]{3,2,1,0:T(8,128)S(1)} %get-tuple-element.64), channel_id=1, source_target_pairs={{0,4},{4,0},{8,12},{12,8},{16,20},{20,16},{24,28},{28,24},{1,5},{5... | collective-permute-start | bytes 491528 | tf_op jit(solution)/shard_map/ppermute | solution.py:901
  97.4 1.0 collective-permute-start.15
  98.5 37.0 %copy-start.2 = (f32[3,64,4,4,256]{4,3,2,1,0:T(4,128)S(1)}, f32[3,64,4,4,256]{4,3,2,1,0:T(4,128)}, u32[]{:S(2)}) copy-start(f32[3,64,4,4,256]{4,3,2,1,0:T(4,128)} %param.6) | copy-start | bytes 9437188

commit v4 on v3

--- a/solution.py
+++ b/solution.py
@@ -230,7 +230,7 @@
         forward, backward = carry
         return cascade(forward, read(t)), cascade(backward, read(HALF - 1 - t))
 
-    return lax.fori_loop(0, HALF, body, ((zero,) * POISSON, (zero,) * POISSON), unroll=8)
+    return lax.fori_loop(0, HALF, body, ((zero,) * POISSON, (zero,) * POISSON), unroll=HALF)
 
 
 def turned(table, states, row):
@@ -448,23 +448,37 @@
         for zz in (0, 1, 2, 3, 36, 37, 38):
             v0_ref[x, zz] = zero
 
-    def swept(source, zz, margin):
-        layers = {x: source[x, zz] for x in range(2 - margin, 8 + margin)}
+    def swept(source, zz, margin, depth):
         result = {}
+        before = [source[2 - margin, zz + k] for k in range(depth)]
+        here = [source[3 - margin, zz + k - 1] for k in range(depth + 2)]
         for x in range(3 - margin, 7 + margin):
-            centre = layers[x]
-            total = layers[x + 1] + either_side(centre)
-            total = total + (source[x, zz + 1] + source[x, zz - 1])
-            result[x] = v0_ref[x, zz] + a1_ref[x, zz] * (total + r_ref[x, zz] * layers[x - 1])
+            if x < 6 + margin:
+                ahead = [source[x + 1, zz + k - 1] for k in range(depth + 2)]
+            else:
+                ahead = [None] + [source[x + 1, zz + k] for k in range(depth)]
+            result[x] = []
+            for k in range(depth):
+                total = ahead[k + 1] + either_side(here[k + 1])
+                total = total + (here[k] + here[k + 2])
+                result[x].append(
+                    v0_ref[x, zz + k] + a1_ref[x, zz + k] * (total + r_ref[x, zz + k] * before[k])
+                )
+            before, here = here[1 : depth + 1], ahead
         return result
 
     def sweep(source, target, margin):
-        def body(zz, _):
-            for x, cells in swept(source, zz, margin).items():
-                target[x, zz] = cells
+        depth = 4
+        first, extent = 3 - margin, 33 + 2 * margin
+
+        def body(t, _):
+            zz = first + jnp.minimum(t * depth, extent - depth)
+            for x, column in swept(source, zz, margin, depth).items():
+                for k, cells in enumerate(column):
+                    target[x, zz + k] = cells
             return 0
 
-        lax.fori_loop(3 - margin, 36 + margin, body, 0, unroll=6)
+        lax.fori_loop(0, -(-extent // depth), body, 0, unroll=2)
 
     for component in range(3):
 
@@ -525,24 +539,29 @@
         sweep(v0_ref, va_ref, 2)
         sweep(va_ref, vb_ref, 1)
 
-        def diverge(zz, before, component=component):
-            cells = [swept(vb_ref, zz + 4, 0)[x + 3] for x in range(4)]
-            for x in range(4):
-                v_ref[component, x, zz] = cells[x]
+        def diverge(t, before, component=component):
+            depth = 4
+            swept_cells = swept(vb_ref, 4 + t * depth, 0, depth)
+            for k in range(depth):
+                zz = t * depth + k
+                cells = [swept_cells[x + 3][k] for x in range(4)]
+                for x in range(4):
+                    v_ref[component, x, zz] = cells[x]
+                    if component == 0:
+                        bw_ref[x, zz] = -2.0 * (cells[x] if x == 0 else cells[x] - cells[x - 1])
+                    elif component == 1:
+                        bw_ref[x, zz] = bw_ref[x, zz] - (cells[x] - below(cells[x]))
+                    else:
+                        bw_ref[x, zz] = bw_ref[x, zz] - (cells[x] - before[x])
                 if component == 0:
-                    bw_ref[x, zz] = -2.0 * (cells[x] if x == 0 else cells[x] - cells[x - 1])
-                elif component == 1:
-                    bw_ref[x, zz] = bw_ref[x, zz] - (cells[x] - below(cells[x]))
-                else:
-                    bw_ref[x, zz] = bw_ref[x, zz] - (cells[x] - before[x])
-            if component == 0:
-                bw_ref[4, zz] = cells[3]
-            return tuple(cells) if component == 2 else 0
+                    bw_ref[4, zz] = cells[3]
+                before = tuple(cells) if component == 2 else 0
+            return before
 
         start = 0
         if component == 2:
-            start = tuple(swept(vb_ref, 3, 0)[x + 3] for x in range(4))
-        lax.fori_loop(0, HALF, diverge, start, unroll=4)
+            start = tuple(swept(vb_ref, 3, 0, 1)[x + 3][0] for x in range(4))
+        lax.fori_loop(0, HALF // 4, diverge, start, unroll=2)
 
     even = 1 - odd
 
@@ -679,7 +698,7 @@
                 q_ref[power, x, zz] = q_ref[power, x, zz] + beside
             return 0
 
-        lax.fori_loop(0, HALF + 1, apply, 0, unroll=3)
+        lax.fori_loop(0, HALF + 1, apply, 0, unroll=11)
 
     def correct(m, _):
         for x in range(4):

time: 138 us -> 134 us (0.971)
  Pallas kernels: 39.8 us -> 35.3 us
    pallas_call x5, Pallas kernels: 39.8 us -> 35.3 us  [call(): pl.pallas_call(kernel, out_shape=arrays, in_specs=places, out_specs=resul...]
where the time goes in v4:
time: 134 us
  waiting for transfers between devices  38.8 us (29%)
  Pallas kernels  35.3 us (26%)
  starting transfers between devices  31.6 us (24%)
  blocking collectives  20.1 us (15%)
  local copies, waits for them, and re-layouts  5.73 us (4%)
  between operations  1.59 us (1%)
    pallas_call x5, Pallas kernels, call(): pl.pallas_call(kernel, out_shape=arrays, in_specs=places, out_specs=resul...  35.3 us
    all_to_all x1, blocking collectives, fast_shards(): lax.all_to_all(jnp.broadcast_to(sums[None], (devices, 1, 128)), ('gx', 'g...  20.1 us
    ppermute x1, waiting for transfers between devices, fast_shards(): b3_in = lax.ppermute(b1_in, 'gx', forward_round)  20 us
    ppermute x1, waiting for transfers between devices, fast_shards(): z2 = lax.ppermute(z2, 'gz', far)  7.59 us
    unnamed x21, local copies, waits for them, and re-layouts  5.68 us
    ppermute x1, waiting for transfers between devices, fast_shards(): pb1_in = lax.ppermute(pb1, 'gx', send_round)  4.14 us
    ppermute x1, starting transfers between devices, fast_shards(): ca = lax.ppermute(ca, 'gx', swap_in)  4.12 us
    ppermute x1, starting transfers between devices, fast_shards(): pa_in = lax.ppermute(pa, 'gx', swap_in)  4.04 us
  transfers between devices with their start and end apart: 16, of which 7 were waited for; matrix products, arithmetic and copies ran while one was open for 0% of the time, Pallas kernels for 0%

profile of v4, /device:TPU:0, one launch (start us, length us, event | category | flops | bytes accessed | tf_op | source)
XLA Modules:
  0.0 133.5 jit_solution(378361430958570701)
XLA Ops:
  0.6 0.0 copy-start
  0.6 1.9 %copy-done = f32[3,64,4,4,256]{4,3,2,1,0:T(4,128)S(1)} copy-done((f32[3,64,4,4,256]{4,3,2,1,0:T(4,128)S(1)}, f32[3,64,4,4,256]{4,3,2,1,0:T(4,128)}, u32[]{:S(2)}) %copy-start) | copy-done | bytes 3145752
  2.5 0.0 copy-start.5
  2.5 0.9 copy-done.5
  3.5 0.0 copy-start.6
  3.5 1.6 %shard_map.76 = (f32[3,4,32,8,256]{4,3,2,1,0:T(8,128)S(1)}, f32[312,8,256]{2,1,0:T(8,128)S(1)}, f32[152,8,256]{2,1,0:T(8,128)S(1)}, f32[160,8,256]{2,1,0:T(8,128...) custom-call(f32[6144,128]{1,0:T(8,128)S(1)} %bitcast.27, f32[512,128]{1,0:T(8,128)S(1)} %bitcast.30), custom_call_target="tpu_custom_call" | custom-call | flops 1000000 | bytes 12091392 | tf_op jit(solution)/shard_map/pallas_call | solution.py:822
  5.1 0.5 collective-permute-start
  5.6 1.3 collective-permute-start.1
  6.9 2.7 %collective-permute-start.2 = (f32[26,8,256]{2,1,0:T(8,128)S(1)}, f32[26,8,256]{2,1,0:T(8,128)S(1)}, u32[]{:S(2)}, u32[]{:S(2)}) collective-permute-start(f32[26,8,256]{2,1,0:T(8,128)S(1)} %get-tuple-element.30), channel_id=1, source_target_pairs={{0,1},{1,0},{2,3},{3,2},{4,5},{5,4},{6,7},{7,6},{8,9},{9,8},{10,11... | collective-permute-start | bytes 638984 | tf_op jit(solution)/shard_map/ppermute | solution.py:894
  9.5 2.5 %collective-permute-start.3 = (f32[26,8,256]{2,1,0:T(8,128)S(1)}, f32[26,8,256]{2,1,0:T(8,128)S(1)}, u32[]{:S(2)}, u32[]{:S(2)}) collective-permute-start(f32[26,8,256]{2,1,0:T(8,128)S(1)} %get-tuple-element.31), channel_id=1, source_target_pairs={{1,2},{2,1},{3,0},{0,3},{5,6},{6,5},{7,4},{4,7},{9,10},{10,9},{11,... | collective-permute-start | bytes 638984 | tf_op jit(solution)/shard_map/ppermute | solution.py:895
  12.0 0.7 collective-permute-start.5
  12.7 1.1 collective-permute-done.2.z1_ref
  13.9 7.6 %collective-permute-done.3.z2_ref = f32[26,8,256]{2,1,0:T(8,128)S(1)} collective-permute-done((f32[26,8,256]{2,1,0:T(8,128)S(1)}, f32[26,8,256]{2,1,0:T(8,128)S(1)}, u32[]{:S(2)}, u32[]{:S(2)}) %collective-permute-start.3) | collective-permute-done | bytes 213024 | tf_op jit(solution)/shard_map/ppermute | solution.py:895
  21.5 2.9 %collective-permute-done.1.b1_ref = f32[152,8,256]{2,1,0:T(8,128)S(1)} collective-permute-done((f32[152,8,256]{2,1,0:T(8,128)S(1)}, f32[152,8,256]{2,1,0:T(8,128)S(1)}, u32[]{:S(2)}, u32[]{:S(2)}) %collective-permute-start.1) | collective-permute-done | bytes 1245216 | tf_op jit(solution)/shard_map/ppermute | solution.py:893
  24.4 2.8 %collective-permute-start.4 = (f32[152,8,256]{2,1,0:T(8,128)S(1)}, f32[152,8,256]{2,1,0:T(8,128)S(1)}, u32[]{:S(2)}, u32[]{:S(2)}) collective-permute-start(f32[152,8,256]{2,1,0:T(8,128)S(1)} %collective-permute-done.1.b1_ref), channel_id=1, source_target_pairs={{28,16},{0,12},{29,17},{1,13},{30,18},{2,14},{31,19},{3,15}} | collective-permute-start | bytes 3735560 | tf_op jit(solution)/shard_map/ppermute | solution.py:903
  27.1 0.1 shard_map.77
  27.2 4.1 %collective-permute-start.6 = (f32[17,8,256]{2,1,0:T(8,128)S(1)}, f32[17,8,256]{2,1,0:T(8,128)S(1)}, u32[]{:S(2)}, u32[]{:S(2)}) collective-permute-start(f32[17,8,256]{2,1,0:T(8,128)S(1)} %get-tuple-element.34), channel_id=1, source_target_pairs={{0,4},{4,0},{8,12},{12,8},{16,20},{20,16},{24,28},{28,24},{1,5},{5... | collective-permute-start | bytes 417800 | tf_op jit(solution)/shard_map/ppermute | solution.py:900
  31.3 0.7 collective-permute-start.7
  32.6 0.0 collective-permute-done.6.ca_ref
  32.6 0.0 collective-permute-done.7.cb_ref
  32.7 0.0 collective-permute-done.5.b2_ref
  32.7 20.0 %collective-permute-done.4.b3_ref = f32[152,8,256]{2,1,0:T(8,128)S(1)} collective-permute-done((f32[152,8,256]{2,1,0:T(8,128)S(1)}, f32[152,8,256]{2,1,0:T(8,128)S(1)}, u32[]{:S(2)}, u32[]{:S(2)}) %collective-permute-start.4) | collective-permute-done | bytes 1245216 | tf_op jit(solution)/shard_map/ppermute | solution.py:903
  52.7 0.0 collective-permute-done.a_ref
  52.7 0.0 copy-done.6
  52.7 16.3 %shard_map.78 = (f32[3,4,32,8,256]{4,3,2,1,0:T(8,128)S(1)}, f32[5,32,8,256]{3,2,1,0:T(8,128)S(1)}, f32[5,5,8,256]{3,2,1,0:T(8,128)S(1)}, f32[4,32,8,256]{3,2,1,0...) custom-call(s32[1]{0:T(128)S(6)} %copy.22.index_ref, ...), custom_call_target="tpu_custom_call" | custom-call | flops 100000000 | bytes 17227780 | tf_op jit(solution)/shard_map/pallas_call | solution.py:822
  69.0 0.0 copy-start.3
  69.0 1.1 copy-done.3
  70.1 0.0 copy-start.8
  70.1 1.0 copy-done.8
  71.0 0.0 copy-start.9
  71.0 0.8 copy-done.9
  71.8 1.3 collective-permute-start.9
  73.2 1.6 %collective-permute-start.10 = (f32[5,5,8,256]{3,2,1,0:T(8,128)S(1)}, f32[5,5,8,256]{3,2,1,0:T(8,128)S(1)}, u32[]{:S(2)}, u32[]{:S(2)}) collective-permute-start(f32[5,5,8,256]{3,2,1,0:T(8,128)S(1)} %get-tuple-element.42), channel_id=1, source_target_pairs={{0,1},{1,0},{2,3},{3,2},{4,5},{5,4},{6,7},{7,6},{8,9},{9,8},{10,11... | collective-permute-start | bytes 614408 | tf_op jit(solution)/shard_map/ppermute | solution.py:914
  74.8 4.0 %collective-permute-start.8 = (f32[4,32,8,256]{3,2,1,0:T(8,128)}, f32[4,32,8,256]{3,2,1,0:T(8,128)S(1)}, u32[]{:S(2)}, u32[]{:S(2)}) collective-permute-start(f32[4,32,8,256]{3,2,1,0:T(8,128)} %copy-done.8), channel_id=1, source_target_pairs={{0,4},{4,0},{8,12},{12,8},{16,20},{20,16},{24,28},{28,24},{1,5},{5... | collective-permute-start | bytes 3145736 | tf_op jit(solution)/shard_map/ppermute | solution.py:916
  78.8 0.7 collective-permute-start.12
  79.6 0.0 copy-start.1
  79.6 0.0 copy-start.4
  79.6 0.0 copy-start.7
  79.6 0.0 collective-permute-done.10
  79.6 4.1 %collective-permute-done.9.b1_ref = f32[2,32,8,256]{3,2,1,0:T(8,128)} collective-permute-done((f32[2,32,8,256]{3,2,1,0:T(8,128)}, f32[2,32,8,256]{3,2,1,0:T(8,128)}, u32[]{:S(2)}, u32[]{:S(2)}) %collective-permute-start.9) | collective-permute-done | bytes 524320 | tf_op jit(solution)/shard_map/ppermute | solution.py:912
  83.7 0.1 broadcast_select_fusion
  83.9 0.1 fusion.2
  84.0 3.7 %collective-permute-start.13 = (f32[5,5,8,256]{3,2,1,0:T(8,128)S(1)}, f32[5,5,8,256]{3,2,1,0:T(8,128)S(1)}, u32[]{:S(2)}, u32[]{:S(2)}) collective-permute-start(f32[5,5,8,256]{3,2,1,0:T(8,128)S(1)} %pad_maximum_fusion), channel_id=1, source_target_pairs={{1,2},{2,1},{3,0},{0,3},{5,6},{6,5},{7,4},{4,7},{9,10},{10,9},{11,... | collective-permute-start | bytes 614408 | tf_op jit(solution)/shard_map/ppermute | solution.py:860
  87.6 1.4 %collective-permute-start.11 = (f32[2,32,8,256]{3,2,1,0:T(8,128)}, f32[2,32,8,256]{3,2,1,0:T(8,128)S(1)}, u32[]{:S(2)}, u32[]{:S(2)}) collective-permute-start(f32[2,32,8,256]{3,2,1,0:T(8,128)} %collective-permute-done.9.b1_ref), channel_id=1, source_target_pairs={{28,16},{0,12},{29,17},{1,13},{30,18},{2,14},{31,19},{3,15}} | collective-permute-start | bytes 1572872 | tf_op jit(solution)/shard_map/ppermute | solution.py:917
  89.1 2.6 %collective-permute-done.13 = f32[5,5,8,256]{3,2,1,0:T(8,128)S(1)} collective-permute-done((f32[5,5,8,256]{3,2,1,0:T(8,128)S(1)}, f32[5,5,8,256]{3,2,1,0:T(8,128)S(1)}, u32[]{:S(2)}, u32[]{:S(2)}) %collective-permute-start.13) | collective-permute-done | bytes 204832 | tf_op jit(solution)/shard_map/ppermute | solution.py:860
  91.7 0.1 fusion.1
  91.9 3.0 %collective-permute-start.14 = (f32[5,4,8,256]{3,2,1,0:T(8,128)S(1)}, f32[5,4,8,256]{3,2,1,0:T(8,128)S(1)}, u32[]{:S(2)}, u32[]{:S(2)}) collective-permute-start(f32[5,4,8,256]{3,2,1,0:T(8,128)S(1)} %get-tuple-element.64), channel_id=1, source_target_pairs={{0,4},{4,0},{8,12},{12,8},{16,20},{20,16},{24,28},{28,24},{1,5},{5... | collective-permute-start | bytes 491528 | tf_op jit(solution)/shard_map/ppermute | solution.py:920
  95.0 0.7 collective-permute-start.15
  95.6 0.0 collective-permute-done.12.b2_ref
  95.6 0.4 collective-permute-done.14.ia_ref
  96.0 0.0 collective-permute-done.15.ib_ref
  96.0 0.0 collective-permute-done.11.b3_ref
  96.0 0.0 collective-permute-done.8.ba_ref
  96.0 0.0 copy-done.1
  96.0 0.0 copy-done.4
  96.1 0.0 copy-done.7
  96.1 0.0 copy-start.2
  96.1 14.8 %shard_map.79 = (f32[6144,128]{1,0:T(8,128)}, f32[6144,128]{1,0:T(8,128)S(1)}, f32[1,128]{1,0:T(1,128)S(1)}) custom-call(s32[1]{0:T(128)S(6)} %copy.22.index_ref, s32[4,4]{1,0:T(4,128)S(1)} %copy-done.7, f32[3,4,32,8,256]{4,3,2,1,0:T(8,128)S(1)} %get-tuple-element.38.v_ref, f32[5,32,8,256]{3,2,1,0:T(8,128)S(1)} %copy-done.4, ...), custom_call_target="tpu_custom_call" | custom-call | flops 100000000 | bytes 17048132 | tf_op jit(solution)/shard_map/pallas_call | solution.py:822
  110.9 20.1 %all_to_all.5 = f32[32,1,128]{2,1,0:T(1,128)S(1)} all-to-all(f32[32,1,128]{2,1,0:T(1,128)S(1)} %broadcast_in_dim.31), channel_id=1, replica_groups=mesh['gx'=8,'gz'=4] {'gx','gz'}, dimensions={0} | all-to-all | bytes 32768 | tf_op jit(solution)/shard_map/all_to_all | solution.py:932
  131.0 0.0 copy-done.2
  131.0 2.6 %shard_map.80 = (f32[6144,128]{1,0:T(8,128)}, f32[4,4]{1,0:T(4,128)}) custom-call(s32[1]{0:T(128)S(6)} %copy.22.index_ref, f32[32,128]{1,0:T(8,128)S(1)} %bitcast.32, f32[6144,128]{1,0:T(8,128)S(1)} %bitcast.29, f32[6144,128]{1,0:T(8,128)S(1)} %get-tuple-element.48.solved_ref), custom_call_target="tpu_custom_call" | custom-call | flops 10000000 | bytes 9453636 | tf_op jit(solution)/shard_map/pallas_call | solution.py:822
  (13 shorter events, 0.2 us)
Async XLA Ops:
  0.6 1.9 %copy-start = (f32[3,64,4,4,256]{4,3,2,1,0:T(4,128)S(1)}, f32[3,64,4,4,256]{4,3,2,1,0:T(4,128)}, u32[]{:S(2)}) copy-start(f32[3,64,4,4,256]{4,3,2,1,0:T(4,128)} %param.5) | copy-start | bytes 9437188
  2.5 0.9 copy-start.5
  3.5 49.2 %copy-start.6 = (f32[64,4,256]{2,1,0:T(4,128)S(1)}, f32[64,4,256]{2,1,0:T(4,128)}, u32[]{:S(2)}) copy-start(f32[64,4,256]{2,1,0:T(4,128)} %param.7) | copy-start | bytes 786436
  5.1 47.6 %collective-permute-start = (f32[312,8,256]{2,1,0:T(8,128)S(1)}, f32[312,8,256]{2,1,0:T(8,128)S(1)}, u32[]{:S(2)}, u32[]{:S(2)}) collective-permute-start(f32[312,8,256]{2,1,0:T(8,128)S(1)} %get-tuple-element.28), channel_id=1, source_target_pairs={{0,4},{4,0},{8,12},{12,8},{16,20},{20,16},{24,28},{28,24},{1,5},{5... | collective-permute-start | bytes 7667720 | tf_op jit(solution)/shard_map/ppermute | solution.py:897
  5.6 18.8 %collective-permute-start.1 = (f32[152,8,256]{2,1,0:T(8,128)S(1)}, f32[152,8,256]{2,1,0:T(8,128)S(1)}, u32[]{:S(2)}, u32[]{:S(2)}) collective-permute-start(f32[152,8,256]{2,1,0:T(8,128)S(1)} %get-tuple-element.29), channel_id=1, source_target_pairs={{4,8},{8,4},{20,24},{24,20},{12,28},{16,0},{5,9},{9,5},{21,25},{25... | collective-permute-start | bytes 3735560 | tf_op jit(solution)/shard_map/ppermute | solution.py:893
  6.9 7.0 %collective-permute-start.2 = (f32[26,8,256]{2,1,0:T(8,128)S(1)}, f32[26,8,256]{2,1,0:T(8,128)S(1)}, u32[]{:S(2)}, u32[]{:S(2)}) collective-permute-start(f32[26,8,256]{2,1,0:T(8,128)S(1)} %get-tuple-element.30), channel_id=1, source_target_pairs={{0,1},{1,0},{2,3},{3,2},{4,5},{5,4},{6,7},{7,6},{8,9},{9,8},{10,11... | collective-permute-start | bytes 638984 | tf_op jit(solution)/shard_map/ppermute | solution.py:894
  9.5 12.0 %collective-permute-start.3 = (f32[26,8,256]{2,1,0:T(8,128)S(1)}, f32[26,8,256]{2,1,0:T(8,128)S(1)}, u32[]{:S(2)}, u32[]{:S(2)}) collective-permute-start(f32[26,8,256]{2,1,0:T(8,128)S(1)} %get-tuple-element.31), channel_id=1, source_target_pairs={{1,2},{2,1},{3,0},{0,3},{5,6},{6,5},{7,4},{4,7},{9,10},{10,9},{11,... | collective-permute-start | bytes 638984 | tf_op jit(solution)/shard_map/ppermute | solution.py:895
  12.0 20.6 %collective-permute-start.5 = (f32[160,8,256]{2,1,0:T(8,128)S(1)}, f32[160,8,256]{2,1,0:T(8,128)S(1)}, u32[]{:S(2)}, u32[]{:S(2)}) collective-permute-start(f32[160,8,256]{2,1,0:T(8,128)S(1)} %get-tuple-element.33), channel_id=1, source_target_pairs={{4,8},{8,4},{12,16},{16,12},{20,24},{24,20},{5,9},{9,5},{13,17},{1... | collective-permute-start | bytes 3932168 | tf_op jit(solution)/shard_map/ppermute | solution.py:896
  24.4 28.3 %collective-permute-start.4 = (f32[152,8,256]{2,1,0:T(8,128)S(1)}, f32[152,8,256]{2,1,0:T(8,128)S(1)}, u32[]{:S(2)}, u32[]{:S(2)}) collective-permute-start(f32[152,8,256]{2,1,0:T(8,128)S(1)} %collective-permute-done.1.b1_ref), channel_id=1, source_target_pairs={{28,16},{0,12},{29,17},{1,13},{30,18},{2,14},{31,19},{3,15}} | collective-permute-start | bytes 3735560 | tf_op jit(solution)/shard_map/ppermute | solution.py:903
  27.2 5.4 %collective-permute-start.6 = (f32[17,8,256]{2,1,0:T(8,128)S(1)}, f32[17,8,256]{2,1,0:T(8,128)S(1)}, u32[]{:S(2)}, u32[]{:S(2)}) collective-permute-start(f32[17,8,256]{2,1,0:T(8,128)S(1)} %get-tuple-element.34), channel_id=1, source_target_pairs={{0,4},{4,0},{8,12},{12,8},{16,20},{20,16},{24,28},{28,24},{1,5},{5... | collective-permute-start | bytes 417800 | tf_op jit(solution)/shard_map/ppermute | solution.py:900
  31.3 1.3 collective-permute-start.7
  69.0 1.1 copy-start.3
  70.1 1.0 copy-start.8
  71.0 0.8 copy-start.9
  71.8 11.9 %collective-permute-start.9 = (f32[2,32,8,256]{3,2,1,0:T(8,128)}, f32[2,32,8,256]{3,2,1,0:T(8,128)}, u32[]{:S(2)}, u32[]{:S(2)}) collective-permute-start(f32[2,32,8,256]{3,2,1,0:T(8,128)} %get-tuple-element.41), channel_id=1, source_target_pairs={{4,8},{8,4},{20,24},{24,20},{12,28},{16,0},{5,9},{9,5},{21,25},{25... | collective-permute-start | bytes 1572872 | tf_op jit(solution)/shard_map/ppermute | solution.py:912
  73.2 6.4 %collective-permute-start.10 = (f32[5,5,8,256]{3,2,1,0:T(8,128)S(1)}, f32[5,5,8,256]{3,2,1,0:T(8,128)S(1)}, u32[]{:S(2)}, u32[]{:S(2)}) collective-permute-start(f32[5,5,8,256]{3,2,1,0:T(8,128)S(1)} %get-tuple-element.42), channel_id=1, source_target_pairs={{0,1},{1,0},{2,3},{3,2},{4,5},{5,4},{6,7},{7,6},{8,9},{9,8},{10,11... | collective-permute-start | bytes 614408 | tf_op jit(solution)/shard_map/ppermute | solution.py:914
  74.8 21.2 %collective-permute-start.8 = (f32[4,32,8,256]{3,2,1,0:T(8,128)}, f32[4,32,8,256]{3,2,1,0:T(8,128)S(1)}, u32[]{:S(2)}, u32[]{:S(2)}) collective-permute-start(f32[4,32,8,256]{3,2,1,0:T(8,128)} %copy-done.8), channel_id=1, source_target_pairs={{0,4},{4,0},{8,12},{12,8},{16,20},{20,16},{24,28},{28,24},{1,5},{5... | collective-permute-start | bytes 3145736 | tf_op jit(solution)/shard_map/ppermute | solution.py:916
  78.8 16.8 %collective-permute-start.12 = (f32[2,32,8,256]{3,2,1,0:T(8,128)}, f32[2,32,8,256]{3,2,1,0:T(8,128)S(1)}, u32[]{:S(2)}, u32[]{:S(2)}) collective-permute-start(f32[2,32,8,256]{3,2,1,0:T(8,128)} %copy-done.9), channel_id=1, source_target_pairs={{4,8},{8,4},{12,16},{16,12},{20,24},{24,20},{5,9},{9,5},{13,17},{1... | collective-permute-start | bytes 1572872 | tf_op jit(solution)/shard_map/ppermute | solution.py:913
  79.6 16.5 %copy-start.1 = (f32[3,64,4,4,256]{4,3,2,1,0:T(4,128)S(1)}, f32[3,64,4,4,256]{4,3,2,1,0:T(4,128)}, u32[]{:S(2)}) copy-start(f32[3,64,4,4,256]{4,3,2,1,0:T(4,128)} %param.5) | copy-start | bytes 9437188
  79.6 16.5 %copy-start.4 = (f32[5,32,8,256]{3,2,1,0:T(8,128)S(1)}, f32[5,32,8,256]{3,2,1,0:T(8,128)}, u32[]{:S(2)}) copy-start(f32[5,32,8,256]{3,2,1,0:T(8,128)} %copy-done.3) | copy-start | bytes 3932164
  79.6 16.5 %copy-start.7 = (s32[4,4]{1,0:T(4,128)S(1)}, s32[4,4]{1,0:T(4,128)}, u32[]{:S(2)}) copy-start(s32[4,4]{1,0:T(4,128)} %cells_ref.1) | copy-start | bytes 196
  84.0 7.7 %collective-permute-start.13 = (f32[5,5,8,256]{3,2,1,0:T(8,128)S(1)}, f32[5,5,8,256]{3,2,1,0:T(8,128)S(1)}, u32[]{:S(2)}, u32[]{:S(2)}) collective-permute-start(f32[5,5,8,256]{3,2,1,0:T(8,128)S(1)} %pad_maximum_fusion), channel_id=1, source_target_pairs={{1,2},{2,1},{3,0},{0,3},{5,6},{6,5},{7,4},{4,7},{9,10},{10,9},{11,... | collective-permute-start | bytes 614408 | tf_op jit(solution)/shard_map/ppermute | solution.py:860
  87.6 8.4 %collective-permute-start.11 = (f32[2,32,8,256]{3,2,1,0:T(8,128)}, f32[2,32,8,256]{3,2,1,0:T(8,128)S(1)}, u32[]{:S(2)}, u32[]{:S(2)}) collective-permute-start(f32[2,32,8,256]{3,2,1,0:T(8,128)} %collective-permute-done.9.b1_ref), channel_id=1, source_target_pairs={{28,16},{0,12},{29,17},{1,13},{30,18},{2,14},{31,19},{3,15}} | collective-permute-start | bytes 1572872 | tf_op jit(solution)/shard_map/ppermute | solution.py:917
  91.9 4.0 %collective-permute-start.14 = (f32[5,4,8,256]{3,2,1,0:T(8,128)S(1)}, f32[5,4,8,256]{3,2,1,0:T(8,128)S(1)}, u32[]{:S(2)}, u32[]{:S(2)}) collective-permute-start(f32[5,4,8,256]{3,2,1,0:T(8,128)S(1)} %get-tuple-element.64), channel_id=1, source_target_pairs={{0,4},{4,0},{8,12},{12,8},{16,20},{20,16},{24,28},{28,24},{1,5},{5... | collective-permute-start | bytes 491528 | tf_op jit(solution)/shard_map/ppermute | solution.py:920
  95.0 1.0 collective-permute-start.15
  96.1 34.9 %copy-start.2 = (f32[3,64,4,4,256]{4,3,2,1,0:T(4,128)S(1)}, f32[3,64,4,4,256]{4,3,2,1,0:T(4,128)}, u32[]{:S(2)}) copy-start(f32[3,64,4,4,256]{4,3,2,1,0:T(4,128)} %param.6) | copy-start | bytes 9437188

commit v5 on v3

--- a/solution.py
+++ b/solution.py
@@ -1,3 +1,4 @@
+import functools
 import math
 
 import jax
@@ -230,7 +231,7 @@
         forward, backward = carry
         return cascade(forward, read(t)), cascade(backward, read(HALF - 1 - t))
 
-    return lax.fori_loop(0, HALF, body, ((zero,) * POISSON, (zero,) * POISSON), unroll=8)
+    return lax.fori_loop(0, HALF, body, ((zero,) * POISSON, (zero,) * POISSON), unroll=HALF)
 
 
 def turned(table, states, row):
@@ -348,11 +349,25 @@
         fill(z1_ref, z2_ref)
 
 
-def velocity_kernel(
-    index_ref, own_ref, base_ref, a_ref, b1_ref, b3_ref, b2_ref, ca_ref, cb_ref, z1_ref, z2_ref,
-    v_ref, bw_ref, s_ref, pa_ref, pb1_ref, pb2_ref,
-    flow_ref, a1_ref, r_ref, v0_ref, va_ref, vb_ref,
-):
+KNOWN = {("early", 0): (3, 9), ("early", 1): (0, 6), ("late", 0): (0, 5), ("late", 1): (4, 9)}
+SWEPT = {
+    ("early", 0): ((4, 8), (5, 7), (6, 6)),
+    ("early", 1): ((1, 5), (2, 4), (3, 3)),
+    ("late", 0): ((1, 3), (2, 4), (3, 5)),
+    ("late", 1): ((6, 8), (5, 7), (4, 6)),
+}
+HANDED = (((4, 5), (5, 6), 6), ((4, 5), (3, 4), 3))
+
+
+def velocity_kernel(stage, *refs):
+    early = stage == "early"
+    if early:
+        index_ref, own_ref, base_ref, a_ref, c_ref, z1_ref, z2_ref, *refs = refs
+        h1_ref, h2_ref, h3_ref, *refs = refs
+    else:
+        index_ref, own_ref, base_ref, b1_ref, b3_ref, b2_ref, c_ref, z1_ref, z2_ref, *refs = refs
+        h1_ref, h2_ref, h3_ref, v_ref, bw_ref, s_ref, pa_ref, pb1_ref, pb2_ref, *refs = refs
+    flow_ref, a1_ref, r_ref, v0_ref, va_ref, vb_ref = refs
     odd = x_odd()
     stream = lax.axis_index("gx")
     last = lax.axis_size("gx") - 1
@@ -362,6 +377,7 @@
     rightward = z_even()
     lower = lower_half()
     shift = shift_of(index_ref)
+    zero = jnp.zeros((8, 256), jnp.float32)
 
     def each_z(step):
         @pl.when(rightward)
@@ -384,125 +400,137 @@
         return pick
 
     def each_x(step):
-        @pl.when(jnp.logical_and(odd == 0, relayed))
+        if early:
+            step(inside)
+            return
+
+        @pl.when(relayed)
         def _():
-            step(outside(b3_ref), cb_ref, inside, ca_ref)
-
-        @pl.when(jnp.logical_and(odd == 0, jnp.logical_not(relayed)))
+            step(outside(b3_ref))
+
+        @pl.when(jnp.logical_not(relayed))
         def _():
-            step(outside(b1_ref), cb_ref, inside, ca_ref)
-
-        @pl.when(jnp.logical_and(odd == 1, relayed))
-        def _():
-            step(inside, ca_ref, outside(b3_ref), cb_ref)
-
-        @pl.when(jnp.logical_and(odd == 1, jnp.logical_not(relayed)))
-        def _():
-            step(inside, ca_ref, outside(b1_ref), cb_ref)
-
-    for x in range(4):
-        for group in range(8):
-            for tile in range(2):
-                lanes = slice(tile * 128, tile * 128 + 128)
-                flow_ref[x + 3, 8 + 8 * group : 16 + 8 * group, lanes] = base_ref[
-                    pl.ds(group * 64 + tile * 4 + x, 8, stride=8), :
-                ]
-
-    def flow_span(behind_ref, ahead_ref):
-        for x in range(4):
-            for k in range(4):
-                at = 24 + k // 2
-                row = (k % 2) * 4 + x
-                flow_ref[x + 3, 7 - k, :] = behind_ref[at, row, :]
-                flow_ref[x + 3, 72 + k, :] = ahead_ref[at, row, :]
-
-    each_z(flow_span)
-
-    def flow_stream(left, left_corner, right, right_corner):
-        for dx in (1, 2, 3):
-            for place, layer, read, corner in (
-                (3 - dx, 3 - dx, left, left_corner),
-                (6 + dx, dx - 1, right, right_corner),
-            ):
+            step(outside(b1_ref))
+
+    def before(cells, halo, k):
+        if k % 2 == 0:
+            return jnp.where(lower, halo, swap(cells))
+        return swap(jnp.where(lower, cells, halo))
+
+    def after(cells, halo, k):
+        if k % 2 == 0:
+            return swap(jnp.where(lower, halo, cells))
+        return jnp.where(lower, swap(cells), halo)
+
+    def run(parity):
+        low, high = KNOWN[stage, parity]
+        own_layers = [x for x in range(4) if low <= x + 3 <= high]
+        if low < 3:
+            halo = [(dx, 3 - dx, 3 - dx) for dx in (1, 2, 3)]
+        else:
+            halo = [(dx, 6 + dx, dx - 1) for dx in (1, 2, 3)]
+
+        for x in own_layers:
+            for group in range(8):
+                for tile in range(2):
+                    lanes = slice(tile * 128, tile * 128 + 128)
+                    flow_ref[x + 3, 8 + 8 * group : 16 + 8 * group, lanes] = base_ref[
+                        pl.ds(group * 64 + tile * 4 + x, 8, stride=8), :
+                    ]
+
+        def flow_span(behind_ref, ahead_ref):
+            for x in own_layers:
+                for k in range(4):
+                    at = 24 + k // 2
+                    row = (k % 2) * 4 + x
+                    flow_ref[x + 3, 7 - k, :] = behind_ref[at, row, :]
+                    flow_ref[x + 3, 72 + k, :] = ahead_ref[at, row, :]
+
+        each_z(flow_span)
+
+        def flow_stream(pick):
+            for dx, place, layer in halo:
                 for group in range(8):
-                    flow_ref[place, 8 + 8 * group : 16 + 8 * group, :] = read(layer * 8)(group)
+                    flow_ref[place, 8 + 8 * group : 16 + 8 * group, :] = pick(layer * 8)(group)
                 for k in range(4):
-                    flow_ref[place, 7 - k, :] = corner[len(CORNERS) + dx - 1, k, :]
-                    flow_ref[place, 72 + k, :] = corner[len(CORNERS) + dx - 1, 4 + k, :]
-
-    each_x(flow_stream)
-
-    def coefficients(zz, _):
-        for x in range(10):
-            first = jnp.broadcast_to(flow_ref[x, pl.ds(zz + 4, 1), :], (8, 256))
-            second = jnp.broadcast_to(flow_ref[x, pl.ds(zz + 36, 1), :], (8, 256))
-            flow = jnp.where(lower, first, second)
-            scale = viscosity * (mask_left if x < 3 else mask_right if x > 6 else 1.0)
-            a1_ref[x, zz] = scale / (shift + 6.0 * viscosity + flow)
-            r_ref[x, zz] = 1.0 + flow * (1.0 / viscosity)
-        return 0
-
-    lax.fori_loop(0, 39, coefficients, 0, unroll=3)
-    zero = jnp.zeros((8, 256), jnp.float32)
-    for x in (0, 1, 2, 7, 8, 9):
-        for zz in (0, 1, 2, 3, 36, 37, 38):
-            v0_ref[x, zz] = zero
-
-    def swept(source, zz, margin):
-        layers = {x: source[x, zz] for x in range(2 - margin, 8 + margin)}
-        result = {}
-        for x in range(3 - margin, 7 + margin):
-            centre = layers[x]
-            total = layers[x + 1] + either_side(centre)
-            total = total + (source[x, zz + 1] + source[x, zz - 1])
-            result[x] = v0_ref[x, zz] + a1_ref[x, zz] * (total + r_ref[x, zz] * layers[x - 1])
-        return result
-
-    def sweep(source, target, margin):
-        def body(zz, _):
-            for x, cells in swept(source, zz, margin).items():
-                target[x, zz] = cells
+                    flow_ref[place, 7 - k, :] = c_ref[len(CORNERS) + dx - 1, k, :]
+                    flow_ref[place, 72 + k, :] = c_ref[len(CORNERS) + dx - 1, 4 + k, :]
+
+        each_x(flow_stream)
+
+        def coefficients(zz, _):
+            for x in range(low, high + 1):
+                first = jnp.broadcast_to(flow_ref[x, pl.ds(zz + 4, 1), :], (8, 256))
+                second = jnp.broadcast_to(flow_ref[x, pl.ds(zz + 36, 1), :], (8, 256))
+                flow = jnp.where(lower, first, second)
+                scale = viscosity * (mask_left if x < 3 else mask_right if x > 6 else 1.0)
+                a1_ref[x, zz] = scale / (shift + 6.0 * viscosity + flow)
+                r_ref[x, zz] = 1.0 + flow * (1.0 / viscosity)
             return 0
 
-        lax.fori_loop(3 - margin, 36 + margin, body, 0, unroll=6)
-
-    for component in range(3):
-
-        def interior(zz, _, component=component):
-            for x in range(4):
-                v0_ref[x + 3, zz + 4] = own_ref[component, x, zz] * a1_ref[x + 3, zz + 4]
-            return 0
-
-        lax.fori_loop(0, HALF, interior, 0, unroll=4)
-
-        def before(cells, halo, k):
-            if k % 2 == 0:
-                return jnp.where(lower, halo, swap(cells))
-            return swap(jnp.where(lower, cells, halo))
-
-        def after(cells, halo, k):
-            if k % 2 == 0:
-                return swap(jnp.where(lower, halo, cells))
-            return jnp.where(lower, swap(cells), halo)
-
-        def span(behind_ref, ahead_ref, component=component):
-            for x in range(4):
-                at = (component * 4 + x) * 2
-                for k in range(4):
-                    cells = before(own_ref[component, x, 31 - k], behind_ref[at + k // 2], k)
-                    v0_ref[x + 3, 3 - k] = cells * a1_ref[x + 3, 3 - k]
-                for k in range(3):
-                    cells = after(own_ref[component, x, k], ahead_ref[at + k // 2], k)
-                    v0_ref[x + 3, 36 + k] = cells * a1_ref[x + 3, 36 + k]
-
-        each_z(span)
-
-        def sides(left, left_corner, right, right_corner, component=component):
-            for dx in (1, 2, 3):
-                for place, layer, pick, corner in (
-                    (3 - dx, 3 - dx, left, left_corner),
-                    (6 + dx, dx - 1, right, right_corner),
-                ):
+        lax.fori_loop(0, 39, coefficients, 0, unroll=3)
+        for _, place, _ in halo:
+            for zz in (0, 1, 2, 3, 36, 37, 38):
+                v0_ref[place, zz] = zero
+
+        def swept(source, span, zz, depth):
+            result = {}
+            first, final = span
+            behind = [source(first - 1, zz + k) for k in range(depth)]
+            here = [source(first, zz + k - 1) for k in range(depth + 2)]
+            for x in range(first, final + 1):
+                if x < final:
+                    ahead = [source(x + 1, zz + k - 1) for k in range(depth + 2)]
+                else:
+                    ahead = [None] + [source(x + 1, zz + k) for k in range(depth)]
+                result[x] = []
+                for k in range(depth):
+                    total = ahead[k + 1] + either_side(here[k + 1])
+                    total = total + (here[k] + here[k + 2])
+                    total = total + r_ref[x, zz + k] * behind[k]
+                    result[x].append(v0_ref[x, zz + k] + a1_ref[x, zz + k] * total)
+                behind, here = here[1 : depth + 1], ahead
+            return result
+
+        def sweep(source, target, level, margin, hand):
+            depth = 4
+            first, extent = 3 - margin, 33 + 2 * margin
+
+            def body(t, _):
+                zz = first + jnp.minimum(t * depth, extent - depth)
+                for x, column in swept(source, SWEPT[stage, parity][level], zz, depth).items():
+                    for k, cells in enumerate(column):
+                        if target is not None:
+                            target[x, zz + k] = cells
+                        hand(x, zz + k, cells)
+                return 0
+
+            lax.fori_loop(0, -(-extent // depth), body, 0, unroll=2)
+
+        handed_first, handed_second, handed_third = HANDED[parity]
+        for component in range(3):
+
+            def interior(zz, _, component=component):
+                for x in own_layers:
+                    v0_ref[x + 3, zz + 4] = own_ref[component, x, zz] * a1_ref[x + 3, zz + 4]
+                return 0
+
+            lax.fori_loop(0, HALF, interior, 0, unroll=4)
+
+            def span(behind_ref, ahead_ref, component=component):
+                for x in own_layers:
+                    at = (component * 4 + x) * 2
+                    for k in range(4):
+                        cells = before(own_ref[component, x, 31 - k], behind_ref[at + k // 2], k)
+                        v0_ref[x + 3, 3 - k] = cells * a1_ref[x + 3, 3 - k]
+                    for k in range(3):
+                        cells = after(own_ref[component, x, k], ahead_ref[at + k // 2], k)
+                        v0_ref[x + 3, 36 + k] = cells * a1_ref[x + 3, 36 + k]
+
+            each_z(span)
+
+            def sides(pick, component=component):
+                for dx, place, layer in halo:
                     read = pick(FACTOR_AT + (component * 3 + layer) * HALF)
 
                     def body(zz, _, read=read, place=place):
@@ -515,35 +543,73 @@
                             continue
                         for k in (2 * pair, 2 * pair + 1):
                             if side == 0:
-                                cells = before(read(31 - k), corner[entry], k)
+                                cells = before(read(31 - k), c_ref[entry], k)
                                 v0_ref[place, 3 - k] = cells * a1_ref[place, 3 - k]
                             else:
-                                cells = after(read(k), corner[entry], k)
+                                cells = after(read(k), c_ref[entry], k)
                                 v0_ref[place, 36 + k] = cells * a1_ref[place, 36 + k]
 
-        each_x(sides)
-        sweep(v0_ref, va_ref, 2)
-        sweep(va_ref, vb_ref, 1)
-
-        def diverge(zz, before, component=component):
-            cells = [swept(vb_ref, zz + 4, 0)[x + 3] for x in range(4)]
-            for x in range(4):
-                v_ref[component, x, zz] = cells[x]
-                if component == 0:
-                    bw_ref[x, zz] = -2.0 * (cells[x] if x == 0 else cells[x] - cells[x - 1])
-                elif component == 1:
-                    bw_ref[x, zz] = bw_ref[x, zz] - (cells[x] - below(cells[x]))
-                else:
-                    bw_ref[x, zz] = bw_ref[x, zz] - (cells[x] - before[x])
-            if component == 0:
-                bw_ref[4, zz] = cells[3]
-            return tuple(cells) if component == 2 else 0
-
-        start = 0
-        if component == 2:
-            start = tuple(swept(vb_ref, 3, 0)[x + 3] for x in range(4))
-        lax.fori_loop(0, HALF, diverge, start, unroll=4)
-
+            each_x(sides)
+
+            def hand_first(x, zz, cells, component=component):
+                if early and x in handed_first:
+                    h1_ref[component, handed_first.index(x), zz] = cells
+
+            def hand_second(x, zz, cells, component=component):
+                if early and x in handed_second:
+                    h2_ref[component, handed_second.index(x), zz] = cells
+
+            def hand_third(x, zz, cells, component=component):
+                h3_ref[component, zz - 3] = cells
+
+            def from_first(x, zz, component=component):
+                if not early and x in handed_first:
+                    return h1_ref[component, handed_first.index(x), zz]
+                return va_ref[x, zz]
+
+            def from_second(x, zz, component=component):
+                if not early and x in handed_second:
+                    return h2_ref[component, handed_second.index(x), zz]
+                return vb_ref[x, zz]
+
+            sweep(lambda x, zz: v0_ref[x, zz], va_ref, 0, 2, hand_first)
+            sweep(from_first, vb_ref, 1, 1, hand_second)
+            if early:
+                sweep(from_second, None, 2, 0, hand_third)
+                continue
+
+            def finished(zz, depth, component=component):
+                found = swept(from_second, SWEPT[stage, parity][2], zz + 4, depth)
+                found[handed_third] = [h3_ref[component, zz + 1 + k] for k in range(depth)]
+                return [[found[x + 3][k] for x in range(4)] for k in range(depth)]
+
+            def diverge(t, past, component=component):
+                for k, cells in enumerate(finished(4 * t, 4)):
+                    zz = 4 * t + k
+                    for x in range(4):
+                        v_ref[component, x, zz] = cells[x]
+                        if component == 0:
+                            bw_ref[x, zz] = -2.0 * (cells[x] if x == 0 else cells[x] - cells[x - 1])
+                        elif component == 1:
+                            bw_ref[x, zz] = bw_ref[x, zz] - (cells[x] - below(cells[x]))
+                        else:
+                            bw_ref[x, zz] = bw_ref[x, zz] - (cells[x] - past[x])
+                    if component == 0:
+                        bw_ref[4, zz] = cells[3]
+                    past = tuple(cells) if component == 2 else 0
+                return past
+
+            start = tuple(finished(-1, 1)[0]) if component == 2 else 0
+            lax.fori_loop(0, HALF // 4, diverge, start, unroll=2)
+
+    for parity in (0, 1):
+
+        @pl.when(odd == parity)
+        def _(parity=parity):
+            run(parity)
+
+    if early:
+        return
     even = 1 - odd
 
     def edges(zz, _):
@@ -679,7 +745,7 @@
                 q_ref[power, x, zz] = q_ref[power, x, zz] + beside
             return 0
 
-        lax.fori_loop(0, HALF + 1, apply, 0, unroll=3)
+        lax.fori_loop(0, HALF + 1, apply, 0, unroll=11)
 
     def correct(m, _):
         for x in range(4):
@@ -807,7 +873,7 @@
         out_specs=results,
         scratch_shapes=[pltpu.VMEM(shape, jnp.float32) for shape in scratch]
         + [pltpu.SemaphoreType.DMA((count,)) for count in signals],
-        compiler_params=pltpu.CompilerParams(vmem_limit_bytes=26 << 20),
+        compiler_params=pltpu.CompilerParams(vmem_limit_bytes=(24 if len(scratch) > 1 else 12 if scratch else 4) << 20),
         cost_estimate=pl.CostEstimate(flops=flops, bytes_accessed=moved, transcendentals=0),
     )(*operands)
 
@@ -883,12 +949,18 @@
     b1_in, z1, z2 = lax.optimization_barrier((b1_in, z1, z2))
     b3_in = lax.ppermute(b1_in, "gx", forward_round)
     block = (10, 39, *cell)
+    scratch = [(10, 80, 256)] + [block] * 5
+    handed = call(
+        functools.partial(velocity_kernel, "early"),
+        [(3, 2, 39, *cell), (3, 2, 39, *cell), (3, HALF + 1, *cell)],
+        scratch, [shift_index, own, base_rows, a_in, ca, z1, z2], 1, 10**8,
+    )
     velocity, sides, states, pa, pb1, pb2 = call(
-        velocity_kernel,
+        functools.partial(velocity_kernel, "late"),
         [(3, 4, HALF, *cell), (5, HALF, *cell), (POISSON + 1, 5, *cell), (4, HALF, *cell)]
         + [(2, HALF, *cell)] * 2,
-        [(10, 80, 256)] + [block] * 5,
-        [shift_index, own, base_rows, a_in, b1_in, b3_in, b2_in, ca, cb, z1, z2], 1, 10**8,
+        scratch,
+        [shift_index, own, base_rows, b1_in, b3_in, b2_in, cb, z1, z2, *handed], 1, 10**8,
     )
     pb1_in = lax.ppermute(pb1, "gx", send_round)
     pb2_in = lax.ppermute(pb2, "gx", swap_out)

time: 138 us -> 129 us (0.935)
  waiting for transfers between devices: 38.8 us -> 29.5 us
    ppermute x1, waiting for transfers between devices: 20 us -> 10.7 us  [fast_shards(): b3_in = lax.ppermute(b1_in, 'gx', forward_round)]
    pallas_call x5 -> x6, Pallas kernels: 39.8 us -> 39.4 us  [call(): pl.pallas_call(kernel, out_shape=arrays, in_specs=places, out_specs=resul...]
  transfers between devices with their start and end apart: 16 -> 16, of which waited for: 7 -> 7; matrix products, arithmetic and copies ran while one was open for 0% -> 0% of each run, Pallas kernels for 0% -> 7%
where the time goes in v5:
time: 129 us; the launch traced here: 128 us
  Pallas kernels  39.4 us (31%)
  starting transfers between devices  31.6 us (24%)
  waiting for transfers between devices  29.5 us (23%)
  blocking collectives  20.1 us (16%)
  local copies, waits for them, and re-layouts  5.73 us (4%)
  between operations  1.61 us (1%)
    pallas_call x6, Pallas kernels, call(): pl.pallas_call(kernel, out_shape=arrays, in_specs=places, out_specs=resul...  39.4 us
    all_to_all x1, blocking collectives, fast_shards(): lax.all_to_all(jnp.broadcast_to(sums[None], (devices, 1, 128)), ('gx', 'g...  20.1 us
    ppermute x1, waiting for transfers between devices, fast_shards(): b3_in = lax.ppermute(b1_in, 'gx', forward_round)  10.7 us
    ppermute x1, waiting for transfers between devices, fast_shards(): z2 = lax.ppermute(z2, 'gz', far)  7.59 us
    unnamed x21, local copies, waits for them, and re-layouts  5.68 us
    ppermute x1, waiting for transfers between devices, fast_shards(): pb1_in = lax.ppermute(pb1, 'gx', send_round)  4.14 us
    ppermute x1, starting transfers between devices, fast_shards(): ca = lax.ppermute(ca, 'gx', swap_in)  4.12 us
    ppermute x1, starting transfers between devices, fast_shards(): pa_in = lax.ppermute(pa, 'gx', swap_in)  4.04 us
  transfers between devices with their start and end apart: 16, of which 7 were waited for; matrix products, arithmetic and copies ran while one was open for 0% of the time, Pallas kernels for 7%

profile of v5, /device:TPU:0, one launch (start us, length us, event | category | flops | bytes accessed | tf_op | source)
XLA Modules:
  0.0 128.4 jit_solution(6079469567798116113)
XLA Ops:
  0.6 0.0 copy-start
  0.6 1.9 %copy-done = f32[3,64,4,4,256]{4,3,2,1,0:T(4,128)S(1)} copy-done((f32[3,64,4,4,256]{4,3,2,1,0:T(4,128)S(1)}, f32[3,64,4,4,256]{4,3,2,1,0:T(4,128)}, u32[]{:S(2)}) %copy-start) | copy-done | bytes 3145752
  2.5 0.0 copy-start.3
  2.5 0.9 copy-done.3
  3.5 0.0 copy-start.4
  3.5 1.6 %shard_map.76 = (f32[3,4,32,8,256]{4,3,2,1,0:T(8,128)S(1)}, f32[312,8,256]{2,1,0:T(8,128)S(1)}, f32[152,8,256]{2,1,0:T(8,128)S(1)}, f32[160,8,256]{2,1,0:T(8,128...) custom-call(f32[6144,128]{1,0:T(8,128)S(1)} %bitcast.27, f32[512,128]{1,0:T(8,128)S(1)} %bitcast.30), custom_call_target="tpu_custom_call" | custom-call | flops 1000000 | bytes 12091392 | tf_op jit(solution)/shard_map/pallas_call | solution.py:869
  5.1 0.5 collective-permute-start.6
  5.6 1.3 collective-permute-start
  6.9 2.7 %collective-permute-start.1 = (f32[26,8,256]{2,1,0:T(8,128)S(1)}, f32[26,8,256]{2,1,0:T(8,128)S(1)}, u32[]{:S(2)}, u32[]{:S(2)}) collective-permute-start(f32[26,8,256]{2,1,0:T(8,128)S(1)} %get-tuple-element.32), channel_id=1, source_target_pairs={{0,1},{1,0},{2,3},{3,2},{4,5},{5,4},{6,7},{7,6},{8,9},{9,8},{10,11... | collective-permute-start | bytes 638984 | tf_op jit(solution)/shard_map/ppermute | solution.py:941
  9.5 2.5 %collective-permute-start.2 = (f32[26,8,256]{2,1,0:T(8,128)S(1)}, f32[26,8,256]{2,1,0:T(8,128)S(1)}, u32[]{:S(2)}, u32[]{:S(2)}) collective-permute-start(f32[26,8,256]{2,1,0:T(8,128)S(1)} %get-tuple-element.33), channel_id=1, source_target_pairs={{1,2},{2,1},{3,0},{0,3},{5,6},{6,5},{7,4},{4,7},{9,10},{10,9},{11,... | collective-permute-start | bytes 638984 | tf_op jit(solution)/shard_map/ppermute | solution.py:942
  12.0 0.7 collective-permute-start.4
  12.7 1.1 collective-permute-done.1.z1_ref.refs_5_.refs_7_
  13.9 7.6 %collective-permute-done.2.z2_ref.refs_6_.refs_8_ = f32[26,8,256]{2,1,0:T(8,128)S(1)} collective-permute-done((f32[26,8,256]{2,1,0:T(8,128)S(1)}, f32[26,8,256]{2,1,0:T(8,128)S(1)}, u32[]{:S(2)}, u32[]{:S(2)}) %collective-permute-start.2) | collective-permute-done | bytes 213024 | tf_op jit(solution)/shard_map/ppermute | solution.py:942
  21.5 2.9 %collective-permute-done.refs_3_ = f32[152,8,256]{2,1,0:T(8,128)S(1)} collective-permute-done((f32[152,8,256]{2,1,0:T(8,128)S(1)}, f32[152,8,256]{2,1,0:T(8,128)S(1)}, u32[]{:S(2)}, u32[]{:S(2)}) %collective-permute-start) | collective-permute-done | bytes 1245216 | tf_op jit(solution)/shard_map/ppermute | solution.py:940
  24.4 2.8 %collective-permute-start.3 = (f32[152,8,256]{2,1,0:T(8,128)S(1)}, f32[152,8,256]{2,1,0:T(8,128)S(1)}, u32[]{:S(2)}, u32[]{:S(2)}) collective-permute-start(f32[152,8,256]{2,1,0:T(8,128)S(1)} %collective-permute-done.refs_3_), channel_id=1, source_target_pairs={{28,16},{0,12},{29,17},{1,13},{30,18},{2,14},{31,19},{3,15}} | collective-permute-start | bytes 3735560 | tf_op jit(solution)/shard_map/ppermute | solution.py:950
  27.1 0.1 shard_map.77
  27.2 4.1 %collective-permute-start.7 = (f32[17,8,256]{2,1,0:T(8,128)S(1)}, f32[17,8,256]{2,1,0:T(8,128)S(1)}, u32[]{:S(2)}, u32[]{:S(2)}) collective-permute-start(f32[17,8,256]{2,1,0:T(8,128)S(1)} %get-tuple-element.40), channel_id=1, source_target_pairs={{0,4},{4,0},{8,12},{12,8},{16,20},{20,16},{24,28},{28,24},{1,5},{5... | collective-permute-start | bytes 417800 | tf_op jit(solution)/shard_map/ppermute | solution.py:947
  31.3 0.7 collective-permute-start.5
  32.6 0.0 collective-permute-done.7.refs_4_
  32.6 0.0 collective-permute-done.6.refs_3_
  32.7 0.0 copy-done.4
  32.7 9.3 %shard_map.78 = (f32[3,2,39,8,256]{4,3,2,1,0:T(8,128)S(1)}, f32[3,2,39,8,256]{4,3,2,1,0:T(8,128)S(1)}, f32[3,33,8,256]{3,2,1,0:T(8,128)S(1)}) custom-call(s32[1]{0:T(128)S(6)} %copy.22.refs_0_.index_ref, f32[3,4,32,8,256]{4,3,2,1,0:T(8,128)S(1)} %get-tuple-element.30.refs_1_, f32[512,128]{1,0:T(8,128)S(1)} %bitcast.31, ...), custom_call_target="tpu_custom_call" | custom-call | flops 100000000 | bytes 11173892 | tf_op jit(solution)/shard_map/pallas_call | solution.py:869
  42.0 0.0 collective-permute-done.5.refs_6_
  42.0 0.0 collective-permute-done.4.refs_5_
  42.0 10.7 %collective-permute-done.3.refs_4_ = f32[152,8,256]{2,1,0:T(8,128)S(1)} collective-permute-done((f32[152,8,256]{2,1,0:T(8,128)S(1)}, f32[152,8,256]{2,1,0:T(8,128)S(1)}, u32[]{:S(2)}, u32[]{:S(2)}) %collective-permute-start.3) | collective-permute-done | bytes 1245216 | tf_op jit(solution)/shard_map/ppermute | solution.py:950
  52.7 11.1 %shard_map.79 = (f32[3,4,32,8,256]{4,3,2,1,0:T(8,128)S(1)}, f32[5,32,8,256]{3,2,1,0:T(8,128)S(1)}, f32[5,5,8,256]{3,2,1,0:T(8,128)S(1)}, f32[4,32,8,256]{3,2,1,0...) custom-call(s32[1]{0:T(128)S(6)} %copy.22.refs_0_.index_ref, ...), custom_call_target="tpu_custom_call" | custom-call | flops 100000000 | bytes 19177476 | tf_op jit(solution)/shard_map/pallas_call | solution.py:869
  63.8 0.0 copy-start.5
  63.8 1.1 copy-done.5
  64.9 0.0 copy-start.8
  64.9 1.0 copy-done.8
  65.9 0.0 copy-start.9
  65.9 0.8 copy-done.9
  66.7 1.3 collective-permute-start.9
  68.0 1.6 %collective-permute-start.10 = (f32[5,5,8,256]{3,2,1,0:T(8,128)S(1)}, f32[5,5,8,256]{3,2,1,0:T(8,128)S(1)}, u32[]{:S(2)}, u32[]{:S(2)}) collective-permute-start(f32[5,5,8,256]{3,2,1,0:T(8,128)S(1)} %get-tuple-element.48), channel_id=1, source_target_pairs={{0,1},{1,0},{2,3},{3,2},{4,5},{5,4},{6,7},{7,6},{8,9},{9,8},{10,11... | collective-permute-start | bytes 614408 | tf_op jit(solution)/shard_map/ppermute | solution.py:967
  69.6 4.0 %collective-permute-start.8 = (f32[4,32,8,256]{3,2,1,0:T(8,128)}, f32[4,32,8,256]{3,2,1,0:T(8,128)S(1)}, u32[]{:S(2)}, u32[]{:S(2)}) collective-permute-start(f32[4,32,8,256]{3,2,1,0:T(8,128)} %copy-done.8), channel_id=1, source_target_pairs={{0,4},{4,0},{8,12},{12,8},{16,20},{20,16},{24,28},{28,24},{1,5},{5... | collective-permute-start | bytes 3145736 | tf_op jit(solution)/shard_map/ppermute | solution.py:969
  73.7 0.7 collective-permute-start.12
  74.4 0.0 copy-start.1
  74.4 0.0 copy-start.6
  74.4 0.0 copy-start.7
  74.4 0.0 collective-permute-done.10
  74.4 4.1 %collective-permute-done.9.b1_ref = f32[2,32,8,256]{3,2,1,0:T(8,128)} collective-permute-done((f32[2,32,8,256]{3,2,1,0:T(8,128)}, f32[2,32,8,256]{3,2,1,0:T(8,128)}, u32[]{:S(2)}, u32[]{:S(2)}) %collective-permute-start.9) | collective-permute-done | bytes 524320 | tf_op jit(solution)/shard_map/ppermute | solution.py:965
  78.6 0.1 broadcast_select_fusion
  78.7 0.1 fusion.2
  78.8 3.7 %collective-permute-start.13 = (f32[5,5,8,256]{3,2,1,0:T(8,128)S(1)}, f32[5,5,8,256]{3,2,1,0:T(8,128)S(1)}, u32[]{:S(2)}, u32[]{:S(2)}) collective-permute-start(f32[5,5,8,256]{3,2,1,0:T(8,128)S(1)} %pad_maximum_fusion), channel_id=1, source_target_pairs={{1,2},{2,1},{3,0},{0,3},{5,6},{6,5},{7,4},{4,7},{9,10},{10,9},{11,... | collective-permute-start | bytes 614408 | tf_op jit(solution)/shard_map/ppermute | solution.py:907
  82.5 1.4 %collective-permute-start.11 = (f32[2,32,8,256]{3,2,1,0:T(8,128)}, f32[2,32,8,256]{3,2,1,0:T(8,128)S(1)}, u32[]{:S(2)}, u32[]{:S(2)}) collective-permute-start(f32[2,32,8,256]{3,2,1,0:T(8,128)} %collective-permute-done.9.b1_ref), channel_id=1, source_target_pairs={{28,16},{0,12},{29,17},{1,13},{30,18},{2,14},{31,19},{3,15}} | collective-permute-start | bytes 1572872 | tf_op jit(solution)/shard_map/ppermute | solution.py:970
  83.9 2.6 %collective-permute-done.13 = f32[5,5,8,256]{3,2,1,0:T(8,128)S(1)} collective-permute-done((f32[5,5,8,256]{3,2,1,0:T(8,128)S(1)}, f32[5,5,8,256]{3,2,1,0:T(8,128)S(1)}, u32[]{:S(2)}, u32[]{:S(2)}) %collective-permute-start.13) | collective-permute-done | bytes 204832 | tf_op jit(solution)/shard_map/ppermute | solution.py:907
  86.5 0.1 fusion.1
  86.8 3.0 %collective-permute-start.14 = (f32[5,4,8,256]{3,2,1,0:T(8,128)S(1)}, f32[5,4,8,256]{3,2,1,0:T(8,128)S(1)}, u32[]{:S(2)}, u32[]{:S(2)}) collective-permute-start(f32[5,4,8,256]{3,2,1,0:T(8,128)S(1)} %get-tuple-element.70), channel_id=1, source_target_pairs={{0,4},{4,0},{8,12},{12,8},{16,20},{20,16},{24,28},{28,24},{1,5},{5... | collective-permute-start | bytes 491528 | tf_op jit(solution)/shard_map/ppermute | solution.py:973
  89.8 0.7 collective-permute-start.15
  90.5 0.0 collective-permute-done.12.b2_ref
  90.5 0.4 collective-permute-done.14.ia_ref
  90.8 0.0 collective-permute-done.15.ib_ref
  90.8 0.0 collective-permute-done.11.b3_ref
  90.9 0.0 collective-permute-done.8.ba_ref
  90.9 0.0 copy-done.1
  90.9 0.0 copy-done.6
  90.9 0.0 copy-done.7
  90.9 0.0 copy-start.2
  90.9 14.8 %shard_map.80 = (f32[6144,128]{1,0:T(8,128)}, f32[6144,128]{1,0:T(8,128)S(1)}, f32[1,128]{1,0:T(1,128)S(1)}) custom-call(s32[1]{0:T(128)S(6)} %copy.22.refs_0_.index_ref, s32[4,4]{1,0:T(4,128)S(1)} %copy-done.7, f32[3,4,32,8,256]{4,3,2,1,0:T(8,128)S(1)} %get-tuple-element.44.v_ref, f32[5,32,8,256]{3,2,1,0:T(8,128)S(1)} %copy-done.6, ...), custom_call_target="tpu_custom_call" | custom-call | flops 100000000 | bytes 17048132 | tf_op jit(solution)/shard_map/pallas_call | solution.py:869
  105.7 20.1 %all_to_all.5 = f32[32,1,128]{2,1,0:T(1,128)S(1)} all-to-all(f32[32,1,128]{2,1,0:T(1,128)S(1)} %broadcast_in_dim.31), channel_id=1, replica_groups=mesh['gx'=8,'gz'=4] {'gx','gz'}, dimensions={0} | all-to-all | bytes 32768 | tf_op jit(solution)/shard_map/all_to_all | solution.py:985
  125.8 0.0 copy-done.2
  125.8 2.6 %shard_map.81 = (f32[6144,128]{1,0:T(8,128)}, f32[4,4]{1,0:T(4,128)}) custom-call(s32[1]{0:T(128)S(6)} %copy.22.refs_0_.index_ref, f32[32,128]{1,0:T(8,128)S(1)} %bitcast.33, f32[6144,128]{1,0:T(8,128)S(1)} %bitcast.29, f32[6144,128]{1,0:T(8,128)S(1)} %get-tuple-element.54.solved_ref), custom_call_target="tpu_custom_call" | custom-call | flops 10000000 | bytes 9453636 | tf_op jit(solution)/shard_map/pallas_call | solution.py:869
  (13 shorter events, 0.2 us)
Async XLA Ops:
  0.6 1.9 %copy-start = (f32[3,64,4,4,256]{4,3,2,1,0:T(4,128)S(1)}, f32[3,64,4,4,256]{4,3,2,1,0:T(4,128)}, u32[]{:S(2)}) copy-start(f32[3,64,4,4,256]{4,3,2,1,0:T(4,128)} %param.5) | copy-start | bytes 9437188
  2.5 0.9 copy-start.3
  3.5 29.2 %copy-start.4 = (f32[64,4,256]{2,1,0:T(4,128)S(1)}, f32[64,4,256]{2,1,0:T(4,128)}, u32[]{:S(2)}) copy-start(f32[64,4,256]{2,1,0:T(4,128)} %param.7) | copy-start | bytes 786436
  5.1 27.6 %collective-permute-start.6 = (f32[312,8,256]{2,1,0:T(8,128)S(1)}, f32[312,8,256]{2,1,0:T(8,128)S(1)}, u32[]{:S(2)}, u32[]{:S(2)}) collective-permute-start(f32[312,8,256]{2,1,0:T(8,128)S(1)} %get-tuple-element.39), channel_id=1, source_target_pairs={{0,4},{4,0},{8,12},{12,8},{16,20},{20,16},{24,28},{28,24},{1,5},{5... | collective-permute-start | bytes 7667720 | tf_op jit(solution)/shard_map/ppermute | solution.py:944
  5.6 18.8 %collective-permute-start = (f32[152,8,256]{2,1,0:T(8,128)S(1)}, f32[152,8,256]{2,1,0:T(8,128)S(1)}, u32[]{:S(2)}, u32[]{:S(2)}) collective-permute-start(f32[152,8,256]{2,1,0:T(8,128)S(1)} %get-tuple-element.31), channel_id=1, source_target_pairs={{4,8},{8,4},{20,24},{24,20},{12,28},{16,0},{5,9},{9,5},{21,25},{25... | collective-permute-start | bytes 3735560 | tf_op jit(solution)/shard_map/ppermute | solution.py:940
  6.9 7.0 %collective-permute-start.1 = (f32[26,8,256]{2,1,0:T(8,128)S(1)}, f32[26,8,256]{2,1,0:T(8,128)S(1)}, u32[]{:S(2)}, u32[]{:S(2)}) collective-permute-start(f32[26,8,256]{2,1,0:T(8,128)S(1)} %get-tuple-element.32), channel_id=1, source_target_pairs={{0,1},{1,0},{2,3},{3,2},{4,5},{5,4},{6,7},{7,6},{8,9},{9,8},{10,11... | collective-permute-start | bytes 638984 | tf_op jit(solution)/shard_map/ppermute | solution.py:941
  9.5 12.0 %collective-permute-start.2 = (f32[26,8,256]{2,1,0:T(8,128)S(1)}, f32[26,8,256]{2,1,0:T(8,128)S(1)}, u32[]{:S(2)}, u32[]{:S(2)}) collective-permute-start(f32[26,8,256]{2,1,0:T(8,128)S(1)} %get-tuple-element.33), channel_id=1, source_target_pairs={{1,2},{2,1},{3,0},{0,3},{5,6},{6,5},{7,4},{4,7},{9,10},{10,9},{11,... | collective-permute-start | bytes 638984 | tf_op jit(solution)/shard_map/ppermute | solution.py:942
  12.0 30.0 %collective-permute-start.4 = (f32[160,8,256]{2,1,0:T(8,128)S(1)}, f32[160,8,256]{2,1,0:T(8,128)S(1)}, u32[]{:S(2)}, u32[]{:S(2)}) collective-permute-start(f32[160,8,256]{2,1,0:T(8,128)S(1)} %get-tuple-element.35), channel_id=1, source_target_pairs={{4,8},{8,4},{12,16},{16,12},{20,24},{24,20},{5,9},{9,5},{13,17},{1... | collective-permute-start | bytes 3932168 | tf_op jit(solution)/shard_map/ppermute | solution.py:943
  24.4 28.3 %collective-permute-start.3 = (f32[152,8,256]{2,1,0:T(8,128)S(1)}, f32[152,8,256]{2,1,0:T(8,128)S(1)}, u32[]{:S(2)}, u32[]{:S(2)}) collective-permute-start(f32[152,8,256]{2,1,0:T(8,128)S(1)} %collective-permute-done.refs_3_), channel_id=1, source_target_pairs={{28,16},{0,12},{29,17},{1,13},{30,18},{2,14},{31,19},{3,15}} | collective-permute-start | bytes 3735560 | tf_op jit(solution)/shard_map/ppermute | solution.py:950
  27.2 5.4 %collective-permute-start.7 = (f32[17,8,256]{2,1,0:T(8,128)S(1)}, f32[17,8,256]{2,1,0:T(8,128)S(1)}, u32[]{:S(2)}, u32[]{:S(2)}) collective-permute-start(f32[17,8,256]{2,1,0:T(8,128)S(1)} %get-tuple-element.40), channel_id=1, source_target_pairs={{0,4},{4,0},{8,12},{12,8},{16,20},{20,16},{24,28},{28,24},{1,5},{5... | collective-permute-start | bytes 417800 | tf_op jit(solution)/shard_map/ppermute | solution.py:947
  31.3 10.7 %collective-permute-start.5 = (f32[17,8,256]{2,1,0:T(8,128)S(1)}, f32[17,8,256]{2,1,0:T(8,128)S(1)}, u32[]{:S(2)}, u32[]{:S(2)}) collective-permute-start(f32[17,8,256]{2,1,0:T(8,128)S(1)} %get-tuple-element.36), channel_id=1, source_target_pairs={{4,8},{8,4},{12,16},{16,12},{20,24},{24,20},{5,9},{9,5},{13,17},{1... | collective-permute-start | bytes 417800 | tf_op jit(solution)/shard_map/ppermute | solution.py:948
  63.8 1.1 copy-start.5
  64.9 1.0 copy-start.8
  65.9 0.8 copy-start.9
  66.7 11.9 %collective-permute-start.9 = (f32[2,32,8,256]{3,2,1,0:T(8,128)}, f32[2,32,8,256]{3,2,1,0:T(8,128)}, u32[]{:S(2)}, u32[]{:S(2)}) collective-permute-start(f32[2,32,8,256]{3,2,1,0:T(8,128)} %get-tuple-element.47), channel_id=1, source_target_pairs={{4,8},{8,4},{20,24},{24,20},{12,28},{16,0},{5,9},{9,5},{21,25},{25... | collective-permute-start | bytes 1572872 | tf_op jit(solution)/shard_map/ppermute | solution.py:965
  68.0 6.4 %collective-permute-start.10 = (f32[5,5,8,256]{3,2,1,0:T(8,128)S(1)}, f32[5,5,8,256]{3,2,1,0:T(8,128)S(1)}, u32[]{:S(2)}, u32[]{:S(2)}) collective-permute-start(f32[5,5,8,256]{3,2,1,0:T(8,128)S(1)} %get-tuple-element.48), channel_id=1, source_target_pairs={{0,1},{1,0},{2,3},{3,2},{4,5},{5,4},{6,7},{7,6},{8,9},{9,8},{10,11... | collective-permute-start | bytes 614408 | tf_op jit(solution)/shard_map/ppermute | solution.py:967
  69.6 21.2 %collective-permute-start.8 = (f32[4,32,8,256]{3,2,1,0:T(8,128)}, f32[4,32,8,256]{3,2,1,0:T(8,128)S(1)}, u32[]{:S(2)}, u32[]{:S(2)}) collective-permute-start(f32[4,32,8,256]{3,2,1,0:T(8,128)} %copy-done.8), channel_id=1, source_target_pairs={{0,4},{4,0},{8,12},{12,8},{16,20},{20,16},{24,28},{28,24},{1,5},{5... | collective-permute-start | bytes 3145736 | tf_op jit(solution)/shard_map/ppermute | solution.py:969
  73.7 16.8 %collective-permute-start.12 = (f32[2,32,8,256]{3,2,1,0:T(8,128)}, f32[2,32,8,256]{3,2,1,0:T(8,128)S(1)}, u32[]{:S(2)}, u32[]{:S(2)}) collective-permute-start(f32[2,32,8,256]{3,2,1,0:T(8,128)} %copy-done.9), channel_id=1, source_target_pairs={{4,8},{8,4},{12,16},{16,12},{20,24},{24,20},{5,9},{9,5},{13,17},{1... | collective-permute-start | bytes 1572872 | tf_op jit(solution)/shard_map/ppermute | solution.py:966
  74.4 16.5 %copy-start.1 = (f32[3,64,4,4,256]{4,3,2,1,0:T(4,128)S(1)}, f32[3,64,4,4,256]{4,3,2,1,0:T(4,128)}, u32[]{:S(2)}) copy-start(f32[3,64,4,4,256]{4,3,2,1,0:T(4,128)} %param.5) | copy-start | bytes 9437188
  74.4 16.5 %copy-start.6 = (f32[5,32,8,256]{3,2,1,0:T(8,128)S(1)}, f32[5,32,8,256]{3,2,1,0:T(8,128)}, u32[]{:S(2)}) copy-start(f32[5,32,8,256]{3,2,1,0:T(8,128)} %copy-done.5) | copy-start | bytes 3932164
  74.4 16.5 %copy-start.7 = (s32[4,4]{1,0:T(4,128)S(1)}, s32[4,4]{1,0:T(4,128)}, u32[]{:S(2)}) copy-start(s32[4,4]{1,0:T(4,128)} %cells_ref.1) | copy-start | bytes 196
  78.8 7.7 %collective-permute-start.13 = (f32[5,5,8,256]{3,2,1,0:T(8,128)S(1)}, f32[5,5,8,256]{3,2,1,0:T(8,128)S(1)}, u32[]{:S(2)}, u32[]{:S(2)}) collective-permute-start(f32[5,5,8,256]{3,2,1,0:T(8,128)S(1)} %pad_maximum_fusion), channel_id=1, source_target_pairs={{1,2},{2,1},{3,0},{0,3},{5,6},{6,5},{7,4},{4,7},{9,10},{10,9},{11,... | collective-permute-start | bytes 614408 | tf_op jit(solution)/shard_map/ppermute | solution.py:907
  82.5 8.4 %collective-permute-start.11 = (f32[2,32,8,256]{3,2,1,0:T(8,128)}, f32[2,32,8,256]{3,2,1,0:T(8,128)S(1)}, u32[]{:S(2)}, u32[]{:S(2)}) collective-permute-start(f32[2,32,8,256]{3,2,1,0:T(8,128)} %collective-permute-done.9.b1_ref), channel_id=1, source_target_pairs={{28,16},{0,12},{29,17},{1,13},{30,18},{2,14},{31,19},{3,15}} | collective-permute-start | bytes 1572872 | tf_op jit(solution)/shard_map/ppermute | solution.py:970
  86.8 4.0 %collective-permute-start.14 = (f32[5,4,8,256]{3,2,1,0:T(8,128)S(1)}, f32[5,4,8,256]{3,2,1,0:T(8,128)S(1)}, u32[]{:S(2)}, u32[]{:S(2)}) collective-permute-start(f32[5,4,8,256]{3,2,1,0:T(8,128)S(1)} %get-tuple-element.70), channel_id=1, source_target_pairs={{0,4},{4,0},{8,12},{12,8},{16,20},{20,16},{24,28},{28,24},{1,5},{5... | collective-permute-start | bytes 491528 | tf_op jit(solution)/shard_map/ppermute | solution.py:973
  89.8 1.0 collective-permute-start.15
  90.9 34.9 %copy-start.2 = (f32[3,64,4,4,256]{4,3,2,1,0:T(4,128)S(1)}, f32[3,64,4,4,256]{4,3,2,1,0:T(4,128)}, u32[]{:S(2)}) copy-start(f32[3,64,4,4,256]{4,3,2,1,0:T(4,128)} %param.6) | copy-start | bytes 9437188

commit v6 on v5

--- a/solution.py
+++ b/solution.py
@@ -164,10 +164,13 @@
         )
         middle = kernel[0] - 2.0 * np.sum(sides)
         mixes.append([float(series[power - 1] * entry) for entry in [middle, *sides]])
-    return float(ratio), half.tolist(), whole, mixes
-
-
-RATIO, HALF_TABLE, WHOLE_TABLE, MIXES = recurrence_tables(12.0, chebyshev_weights)
+    square = whole @ whole
+    around = np.linalg.inv(np.eye(order) - square @ square)
+    wholes = [table.tolist() for table in (whole, square, square @ whole, around)]
+    return float(ratio), half.tolist(), wholes, mixes
+
+
+RATIO, HALF_TABLE, WHOLE_TABLES, MIXES = recurrence_tables(12.0, chebyshev_weights)
 
 
 def lower_half():
@@ -464,14 +467,14 @@
                 second = jnp.broadcast_to(flow_ref[x, pl.ds(zz + 36, 1), :], (8, 256))
                 flow = jnp.where(lower, first, second)
                 scale = viscosity * (mask_left if x < 3 else mask_right if x > 6 else 1.0)
-                a1_ref[x, zz] = scale / (shift + 6.0 * viscosity + flow)
-                r_ref[x, zz] = 1.0 + flow * (1.0 / viscosity)
+                a1_ref[x - low, zz] = scale / (shift + 6.0 * viscosity + flow)
+                r_ref[x - low, zz] = 1.0 + flow * (1.0 / viscosity)
             return 0
 
         lax.fori_loop(0, 39, coefficients, 0, unroll=3)
         for _, place, _ in halo:
             for zz in (0, 1, 2, 3, 36, 37, 38):
-                v0_ref[place, zz] = zero
+                v0_ref[place - low, zz] = zero
 
         def swept(source, span, zz, depth):
             result = {}
@@ -487,8 +490,8 @@
                 for k in range(depth):
                     total = ahead[k + 1] + either_side(here[k + 1])
                     total = total + (here[k] + here[k + 2])
-                    total = total + r_ref[x, zz + k] * behind[k]
-                    result[x].append(v0_ref[x, zz + k] + a1_ref[x, zz + k] * total)
+                    total = total + r_ref[x - low, zz + k] * behind[k]
+                    result[x].append(v0_ref[x - low, zz + k] + a1_ref[x - low, zz + k] * total)
                 behind, here = here[1 : depth + 1], ahead
             return result
 
@@ -501,7 +504,7 @@
                 for x, column in swept(source, SWEPT[stage, parity][level], zz, depth).items():
                     for k, cells in enumerate(column):
                         if target is not None:
-                            target[x, zz + k] = cells
+                            target[x - low, zz + k] = cells
                         hand(x, zz + k, cells)
                 return 0
 
@@ -512,7 +515,7 @@
 
             def interior(zz, _, component=component):
                 for x in own_layers:
-                    v0_ref[x + 3, zz + 4] = own_ref[component, x, zz] * a1_ref[x + 3, zz + 4]
+                    v0_ref[x + 3 - low, zz + 4] = own_ref[component, x, zz] * a1_ref[x + 3 - low, zz + 4]
                 return 0
 
             lax.fori_loop(0, HALF, interior, 0, unroll=4)
@@ -522,10 +525,10 @@
                     at = (component * 4 + x) * 2
                     for k in range(4):
                         cells = before(own_ref[component, x, 31 - k], behind_ref[at + k // 2], k)
-                        v0_ref[x + 3, 3 - k] = cells * a1_ref[x + 3, 3 - k]
+                        v0_ref[x + 3 - low, 3 - k] = cells * a1_ref[x + 3 - low, 3 - k]
                     for k in range(3):
                         cells = after(own_ref[component, x, k], ahead_ref[at + k // 2], k)
-                        v0_ref[x + 3, 36 + k] = cells * a1_ref[x + 3, 36 + k]
+                        v0_ref[x + 3 - low, 36 + k] = cells * a1_ref[x + 3 - low, 36 + k]
 
             each_z(span)
 
@@ -534,7 +537,7 @@
                     read = pick(FACTOR_AT + (component * 3 + layer) * HALF)
 
                     def body(zz, _, read=read, place=place):
-                        v0_ref[place, zz + 4] = read(zz) * a1_ref[place, zz + 4]
+                        v0_ref[place - low, zz + 4] = read(zz) * a1_ref[place - low, zz + 4]
                         return 0
 
                     lax.fori_loop(0, HALF, body, 0, unroll=4)
@@ -544,10 +547,10 @@
                         for k in (2 * pair, 2 * pair + 1):
                             if side == 0:
                                 cells = before(read(31 - k), c_ref[entry], k)
-                                v0_ref[place, 3 - k] = cells * a1_ref[place, 3 - k]
+                                v0_ref[place - low, 3 - k] = cells * a1_ref[place - low, 3 - k]
                             else:
                                 cells = after(read(k), c_ref[entry], k)
-                                v0_ref[place, 36 + k] = cells * a1_ref[place, 36 + k]
+                                v0_ref[place - low, 36 + k] = cells * a1_ref[place - low, 36 + k]
 
             each_x(sides)
 
@@ -565,14 +568,14 @@
             def from_first(x, zz, component=component):
                 if not early and x in handed_first:
                     return h1_ref[component, handed_first.index(x), zz]
-                return va_ref[x, zz]
+                return va_ref[x - low, zz]
 
             def from_second(x, zz, component=component):
                 if not early and x in handed_second:
                     return h2_ref[component, handed_second.index(x), zz]
-                return vb_ref[x, zz]
-
-            sweep(lambda x, zz: v0_ref[x, zz], va_ref, 0, 2, hand_first)
+                return vb_ref[x - low, zz]
+
+            sweep(lambda x, zz: v0_ref[x - low, zz], va_ref, 0, 2, hand_first)
             sweep(from_first, vb_ref, 1, 1, hand_second)
             if early:
                 sweep(from_second, None, 2, 0, hand_third)
@@ -610,11 +613,10 @@
 
     if early:
         return
-    even = 1 - odd
 
     def edges(zz, _):
         for layer in range(4):
-            pa_ref[layer, zz] = bw_ref[layer + even, zz]
+            pa_ref[layer, zz] = bw_ref[layer + 1 - odd, zz]
             (pb1_ref if layer < 2 else pb2_ref)[layer % 2, zz] = bw_ref[layer + odd, zz]
         return 0
 
@@ -661,13 +663,19 @@
         lax.fori_loop(0, HALF, body, 0, unroll=4)
         for i in range(POISSON + 1):
             for x in range(3):
-                i_ref[i, x] = left_inc[i, x]
+                i_ref[i, x] = left_inc(i, x)
                 i_ref[i, x + 4] = inc_ref[i, x + 1]
-                i_ref[i, x + 8] = right_inc[i, x + 1]
-            i_ref[i, 3] = inc_ref[i, 0] + 2.0 * left_inc[i, 3]
-            i_ref[i, 7] = mask_right * (right_inc[i, 0] + 2.0 * inc_ref[i, 4])
+                i_ref[i, x + 8] = right_inc(i, x + 1)
+            i_ref[i, 3] = inc_ref[i, 0] + 2.0 * left_inc(i, 3)
+            i_ref[i, 7] = mask_right * (right_inc(i, 0) + 2.0 * inc_ref[i, 4])
         for x in range(11):
             f_ref[x, HALF] = swap(jnp.where(lower, i_ref[POISSON, x], f_ref[x, 0]))
+
+    def enter_inside(i, layer):
+        return ia_ref[i, layer]
+
+    def enter_outside(i, layer):
+        return ib_ref[i, layer]
 
     def inside(layer, zz):
         return ba_ref[layer, zz]
@@ -685,9 +693,9 @@
             @pl.when(jnp.logical_and(odd == parity, middle == through))
             def _(parity=parity, outside=outside):
                 if parity == 0:
-                    gather(outside, inside, ib_ref, ia_ref)
+                    gather(outside, inside, enter_outside, enter_inside)
                 else:
-                    gather(inside, outside, ia_ref, ib_ref)
+                    gather(inside, outside, enter_inside, enter_outside)
 
     def solve(x, _):
         forward, backward = half_states(lambda t: f_ref[x, t])
@@ -855,7 +863,47 @@
         copy.wait()
 
 
-def call(kernel, outputs, scratch, operands, smalls, flops, far_in=(), far_out=(), signals=(), least=0):
+def ring_sides():
+    upper = lax.broadcasted_iota(jnp.int32, (8, 256), 0) // 4
+    return upper == 1 - lax.rem(lax.axis_index("gz"), 2)
+
+
+def joining_kernel(states_ref, partner_ref, joined_ref):
+    first = ring_sides()
+    for layer in range(5):
+        own = [states_ref[i, layer] for i in range(POISSON)]
+        near = [partner_ref[i, layer] for i in range(POISSON)]
+        farther = [jnp.where(first, o, n) for o, n in zip(own, near)]
+        for i in range(POISSON):
+            nearer = jnp.where(first, near[i], own[i])
+            joined_ref[i, layer] = nearer + turned(WHOLE_TABLES[0], farther, i)
+        joined_ref[POISSON, layer] = states_ref[POISSON, layer]
+
+
+def entering_kernel(states_ref, partner_ref, other_ref, inc_ref, a_ref, b_ref):
+    first = ring_sides()
+    odd = x_odd()
+    even = 1 - odd
+    rightward = z_even()
+    once, twice, thrice, around = WHOLE_TABLES
+    for layer in range(5):
+        own = [states_ref[i, layer] for i in range(POISSON)]
+        near = [partner_ref[i, layer] for i in range(POISSON)]
+        far = [other_ref[i, layer] for i in range(POISSON)]
+        entering = []
+        for i in range(POISSON):
+            cells = jnp.where(first, far[i] + turned(twice, near, i), near[i] + turned(once, far, i))
+            entering.append(cells + turned(thrice, own, i))
+        for i in range(POISSON):
+            inc_ref[i, layer] = turned(around, entering, i)
+        inc_ref[POISSON, layer] = jnp.where(rightward, partner_ref[POISSON, layer], other_ref[POISSON, layer])
+    for layer in range(4):
+        for i in range(POISSON + 1):
+            a_ref[i, layer] = inc_ref[i, layer + even]
+            b_ref[i, layer] = inc_ref[i, layer + odd]
+
+
+def call(kernel, outputs, scratch, operands, smalls, flops, room, far_in=(), far_out=(), signals=(), least=0):
     arrays = [jax.ShapeDtypeStruct(shape, jnp.float32) for shape in outputs]
     places = [pl.BlockSpec(memory_space=pltpu.SMEM)] * smalls
     places += [pl.BlockSpec(memory_space=pltpu.VMEM)] * (len(operands) - smalls)
@@ -864,7 +912,6 @@
         places[place] = pl.BlockSpec(memory_space=pltpu.HBM)
     for place in far_out:
         results[place] = pl.BlockSpec(memory_space=pltpu.HBM)
-    room = sum(4 * math.prod(shape) for shape in scratch) + (2 << 20)
     moved = sum(4 * math.prod(shape) for shape in outputs) + sum(4 * math.prod(o.shape) for o in operands)
     return pl.pallas_call(
         kernel,
@@ -873,7 +920,7 @@
         out_specs=results,
         scratch_shapes=[pltpu.VMEM(shape, jnp.float32) for shape in scratch]
         + [pltpu.SemaphoreType.DMA((count,)) for count in signals],
-        compiler_params=pltpu.CompilerParams(vmem_limit_bytes=(24 if len(scratch) > 1 else 12 if scratch else 4) << 20),
+        compiler_params=pltpu.CompilerParams(vmem_limit_bytes=room << 20),
         cost_estimate=pl.CostEstimate(flops=flops, bytes_accessed=moved, transcendentals=0),
     )(*operands)
 
@@ -889,34 +936,6 @@
     order = tuple(range(len(head)))
     split = rows.reshape(*head, 2, 4, 128).transpose(*order, len(head) + 1, len(head), len(head) + 2)
     return split.reshape(*head, 4, 256)
-
-
-def mixed(table, states):
-    table = np.asarray(table).astype(np.float32)
-    return jnp.stack(
-        [sum(float(table[i, k]) * states[k] for k in range(i + 1)) for i in range(POISSON)]
-    )
-
-
-def ring_states(states, partner, own_even, far):
-    upper = jnp.arange(8)[None, None, :, None] >= 4
-    first = upper == own_even
-    nearer = jnp.where(first, partner, states)
-    farther = jnp.where(first, states, partner)
-    joined = nearer[:POISSON] + mixed(WHOLE_TABLE, farther[:POISSON])
-    other = lax.ppermute(jnp.concatenate([joined, states[POISSON:]]), "gz", far)
-    square = WHOLE_TABLE @ WHOLE_TABLE
-    cube = square @ WHOLE_TABLE
-    around = np.linalg.inv(np.eye(POISSON) - square @ square)
-    entering = jnp.where(
-        first[0],
-        other[:POISSON] + mixed(square, partner[:POISSON]),
-        partner[:POISSON] + mixed(WHOLE_TABLE, other[:POISSON]),
-    )
-    entering = entering + mixed(cube, states[:POISSON])
-    entering = mixed(around, entering)
-    ahead = jnp.where(own_even, partner[POISSON:], other[POISSON:])
-    return jnp.concatenate([entering, ahead])
 
 
 def fast_shards(factor, gain, base_flow, shift_index, sensor_cells):
@@ -926,8 +945,6 @@
     forward_round = [(7, 4), (0, 3)]
     near = [(0, 1), (1, 0), (2, 3), (3, 2)]
     far = [(1, 2), (2, 1), (3, 0), (0, 3)]
-    odd = lax.axis_index("gx") % 2
-    own_even = lax.axis_index("gz") % 2 == 0
     factor_rows = to_rows(factor)
     base_rows = to_rows(base_flow)
     gain_rows = to_rows(gain)
@@ -935,7 +952,7 @@
     own, a, b1, b2, z1, z2 = call(
         pack_kernel,
         [(3, 4, HALF, *cell), (312, *cell), (PART, *cell), (312 - PART, *cell), (26, *cell), (26, *cell)],
-        [factor_rows.shape], [factor_rows, base_rows], 0, 10**6, far_in=(0,), signals=(3,),
+        [factor_rows.shape], [factor_rows, base_rows], 0, 10**6, 16, far_in=(0,), signals=(3,),
     )
     b1_in = lax.ppermute(b1, "gx", send_round)
     z1 = lax.ppermute(z1, "gz", near)
@@ -943,34 +960,40 @@
     b2_in = lax.ppermute(b2, "gx", swap_out)
     a_in = lax.ppermute(a, "gx", swap_in)
     corners = len(CORNERS) + 3
-    ca, cb = call(corner_kernel, [(corners, *cell)] * 2, [], [z1, z2], 0, 10**5)
+    ca, cb = call(corner_kernel, [(corners, *cell)] * 2, [], [z1, z2], 0, 10**5, 4)
     ca = lax.ppermute(ca, "gx", swap_in)
     cb = lax.ppermute(cb, "gx", swap_out)
     b1_in, z1, z2 = lax.optimization_barrier((b1_in, z1, z2))
     b3_in = lax.ppermute(b1_in, "gx", forward_round)
-    block = (10, 39, *cell)
+    block = (7, 39, *cell)
     scratch = [(10, 80, 256)] + [block] * 5
     handed = call(
         functools.partial(velocity_kernel, "early"),
         [(3, 2, 39, *cell), (3, 2, 39, *cell), (3, HALF + 1, *cell)],
-        scratch, [shift_index, own, base_rows, a_in, ca, z1, z2], 1, 10**8,
+        scratch, [shift_index, own, base_rows, a_in, ca, z1, z2], 1, 10**8, 34,
     )
     velocity, sides, states, pa, pb1, pb2 = call(
         functools.partial(velocity_kernel, "late"),
         [(3, 4, HALF, *cell), (5, HALF, *cell), (POISSON + 1, 5, *cell), (4, HALF, *cell)]
         + [(2, HALF, *cell)] * 2,
         scratch,
-        [shift_index, own, base_rows, b1_in, b3_in, b2_in, cb, z1, z2, *handed], 1, 10**8,
+        [shift_index, own, base_rows, b1_in, b3_in, b2_in, cb, z1, z2, *handed], 1, 10**8, 34,
     )
     pb1_in = lax.ppermute(pb1, "gx", send_round)
     pb2_in = lax.ppermute(pb2, "gx", swap_out)
     partner = lax.ppermute(states, "gz", near)
-    pb1_in, partner = lax.optimization_barrier((pb1_in, partner))
+    (joined,) = call(joining_kernel, [states.shape], [], [states, partner], 0, 10**5, 4)
+    other = lax.ppermute(joined, "gz", far)
+    pb1_in, _ = lax.optimization_barrier((pb1_in, partner))
+    pb3_in = lax.ppermute(pb1_in, "gx", forward_round)
     pa_in = lax.ppermute(pa, "gx", swap_in)
-    pb3_in = lax.ppermute(pb1_in, "gx", forward_round)
-    entering = ring_states(states, partner, own_even, far)
-    enter_b = lax.ppermute(lax.dynamic_slice_in_dim(entering, odd, 4, axis=1), "gx", swap_out)
-    enter_a = lax.ppermute(lax.dynamic_slice_in_dim(entering, 1 - odd, 4, axis=1), "gx", swap_in)
+    entering, enter_a, enter_b = call(
+        entering_kernel,
+        [states.shape, (POISSON + 1, 4, *cell), (POISSON + 1, 4, *cell)],
+        [], [states, partner, other], 0, 10**5, 4,
+    )
+    enter_b = lax.ppermute(enter_b, "gx", swap_out)
+    enter_a = lax.ppermute(enter_a, "gx", swap_in)
     block = (11, HALF + 1, *cell)
     new_rows, solved, sums = call(
         pressure_kernel,
@@ -979,7 +1002,7 @@
         + [factor_rows.shape],
         [shift_index, sensor_cells, velocity, sides, pa_in, pb1_in, pb3_in, pb2_in]
         + [entering, enter_a, enter_b, factor_rows],
-        2, 10**8, far_out=(0,), signals=(4,),
+        2, 10**8, 38, far_out=(0,), signals=(4,),
     )
     devices = lax.axis_size("gx") * lax.axis_size("gz")
     shared = lax.all_to_all(
@@ -988,7 +1011,7 @@
     new_gain, gram = call(
         gain_kernel,
         [gain_rows.shape, (4, 4)],
-        [gain_rows.shape], [shift_index, shared.reshape(devices, 128), gain_rows, solved], 1, 10**7,
+        [gain_rows.shape], [shift_index, shared.reshape(devices, 128), gain_rows, solved], 1, 10**7, 14,
         far_out=(0,), signals=(6,),
     )
     head = factor.shape[:3]

time: 129 us -> 127 us (0.984)
  waiting for transfers between devices: 29.5 us -> 32.6 us
  local copies, waits for them, and re-layouts: 5.73 us -> 2.86 us
    ppermute x1, waiting for transfers between devices: 0.01 us -> 4.63 us  [fast_shards(): partner = lax.ppermute(states, 'gz', near)]
    ppermute x1, waiting for transfers between devices: 4.14 us -> 0.01 us  [fast_shards(): pb1_in = lax.ppermute(pb1, 'gx', send_round)]
    ppermute x3, waiting for transfers between devices: 2.96 us -> 6.14 us  [the longest x1 5.44 us: fast_shards(): other = lax.ppermute(joined, 'gz', far)]
    ppermute x3, starting transfers between devices: 7.34 us -> 4.4 us  [the longest x1 3.66 us: fast_shards(): other = lax.ppermute(joined, 'gz', far)]
    unnamed x21 -> x12, local copies, waits for them, and re-layouts: 5.68 us -> 2.85 us
    ppermute x1, starting transfers between devices: 1.42 us -> 3.43 us  [fast_shards(): pb3_in = lax.ppermute(pb1_in, 'gx', forward_round)]
    pallas_call x6 -> x8, Pallas kernels: 39.4 us -> 39.1 us  [call(): pl.pallas_call(kernel, out_shape=arrays, in_specs=places, out_specs=resul...]
  transfers between devices with their start and end apart: 16 -> 16, of which waited for: 7 -> 7; matrix products, arithmetic and copies ran while one was open for 0% -> 0% of each run, Pallas kernels for 7% -> 8%
where the time goes in v6:
time: 127 us
  Pallas kernels  39.1 us (31%)
  waiting for transfers between devices  32.6 us (26%)
  starting transfers between devices  31 us (24%)
  blocking collectives  20 us (16%)
  local copies, waits for them, and re-layouts  2.86 us (2%)
  between operations  1.5 us (1%)
    pallas_call x8, Pallas kernels, call(): pl.pallas_call(kernel, out_shape=arrays, in_specs=places, out_specs=resul...  39.1 us
    all_to_all x1, blocking collectives, fast_shards(): lax.all_to_all(jnp.broadcast_to(sums[None], (devices, 1, 128)), ('gx', 'g...  20 us
    ppermute x1, waiting for transfers between devices, fast_shards(): b3_in = lax.ppermute(b1_in, 'gx', forward_round)  10.2 us
    ppermute x1, waiting for transfers between devices, fast_shards(): z2 = lax.ppermute(z2, 'gz', far)  7.59 us
    ppermute x1, waiting for transfers between devices, fast_shards(): other = lax.ppermute(joined, 'gz', far)  5.44 us
    ppermute x1, waiting for transfers between devices, fast_shards(): partner = lax.ppermute(states, 'gz', near)  4.63 us
    ppermute x1, starting transfers between devices, fast_shards(): ca = lax.ppermute(ca, 'gx', swap_in)  4.12 us
    ppermute x1, starting transfers between devices, fast_shards(): pa_in = lax.ppermute(pa, 'gx', swap_in)  3.8 us
  transfers between devices with their start and end apart: 16, of which 7 were waited for; matrix products, arithmetic and copies ran while one was open for 0% of the time, Pallas kernels for 8%

profile of v6, /device:TPU:0, one launch (start us, length us, event | category | flops | bytes accessed | tf_op | source)
XLA Modules:
  0.0 127.1 jit_solution(7402464226512925777)
XLA Ops:
  0.6 0.0 copy-start
  0.6 1.9 %copy-done = f32[3,64,4,4,256]{4,3,2,1,0:T(4,128)S(1)} copy-done((f32[3,64,4,4,256]{4,3,2,1,0:T(4,128)S(1)}, f32[3,64,4,4,256]{4,3,2,1,0:T(4,128)}, u32[]{:S(2)}) %copy-start) | copy-done | bytes 3145752
  2.5 0.0 copy-start.3
  2.5 0.9 copy-done.3
  3.5 0.0 copy-start.4
  3.5 1.5 %shard_map.76 = (f32[3,4,32,8,256]{4,3,2,1,0:T(8,128)S(1)}, f32[312,8,256]{2,1,0:T(8,128)S(1)}, f32[152,8,256]{2,1,0:T(8,128)S(1)}, f32[160,8,256]{2,1,0:T(8,128...) custom-call(f32[6144,128]{1,0:T(8,128)S(1)} %bitcast.27, f32[512,128]{1,0:T(8,128)S(1)} %bitcast.30), custom_call_target="tpu_custom_call" | custom-call | flops 1000000 | bytes 12091392 | tf_op jit(solution)/shard_map/pallas_call | solution.py:916
  5.0 0.5 collective-permute-start.6
  5.5 1.3 %collective-permute-start = (f32[152,8,256]{2,1,0:T(8,128)S(1)}, f32[152,8,256]{2,1,0:T(8,128)S(1)}, u32[]{:S(2)}, u32[]{:S(2)}) collective-permute-start(f32[152,8,256]{2,1,0:T(8,128)S(1)} %get-tuple-element.33), channel_id=1, source_target_pairs={{4,8},{8,4},{20,24},{24,20},{12,28},{16,0},{5,9},{9,5},{21,25},{25... | collective-permute-start | bytes 3735560 | tf_op jit(solution)/shard_map/ppermute | solution.py:957
  6.8 2.7 %collective-permute-start.1 = (f32[26,8,256]{2,1,0:T(8,128)S(1)}, f32[26,8,256]{2,1,0:T(8,128)S(1)}, u32[]{:S(2)}, u32[]{:S(2)}) collective-permute-start(f32[26,8,256]{2,1,0:T(8,128)S(1)} %get-tuple-element.34), channel_id=1, source_target_pairs={{0,1},{1,0},{2,3},{3,2},{4,5},{5,4},{6,7},{7,6},{8,9},{9,8},{10,11... | collective-permute-start | bytes 638984 | tf_op jit(solution)/shard_map/ppermute | solution.py:958
  9.5 2.5 %collective-permute-start.2 = (f32[26,8,256]{2,1,0:T(8,128)S(1)}, f32[26,8,256]{2,1,0:T(8,128)S(1)}, u32[]{:S(2)}, u32[]{:S(2)}) collective-permute-start(f32[26,8,256]{2,1,0:T(8,128)S(1)} %get-tuple-element.35), channel_id=1, source_target_pairs={{1,2},{2,1},{3,0},{0,3},{5,6},{6,5},{7,4},{4,7},{9,10},{10,9},{11,... | collective-permute-start | bytes 638984 | tf_op jit(solution)/shard_map/ppermute | solution.py:959
  12.0 0.7 collective-permute-start.4
  12.7 1.1 collective-permute-done.1.z1_ref.refs_5_.refs_7_
  13.8 7.6 %collective-permute-done.2.z2_ref.refs_6_.refs_8_ = f32[26,8,256]{2,1,0:T(8,128)S(1)} collective-permute-done((f32[26,8,256]{2,1,0:T(8,128)S(1)}, f32[26,8,256]{2,1,0:T(8,128)S(1)}, u32[]{:S(2)}, u32[]{:S(2)}) %collective-permute-start.2) | collective-permute-done | bytes 213024 | tf_op jit(solution)/shard_map/ppermute | solution.py:959
  21.4 2.9 %collective-permute-done.refs_3_ = f32[152,8,256]{2,1,0:T(8,128)S(1)} collective-permute-done((f32[152,8,256]{2,1,0:T(8,128)S(1)}, f32[152,8,256]{2,1,0:T(8,128)S(1)}, u32[]{:S(2)}, u32[]{:S(2)}) %collective-permute-start) | collective-permute-done | bytes 1245216 | tf_op jit(solution)/shard_map/ppermute | solution.py:957
  24.3 2.8 %collective-permute-start.3 = (f32[152,8,256]{2,1,0:T(8,128)S(1)}, f32[152,8,256]{2,1,0:T(8,128)S(1)}, u32[]{:S(2)}, u32[]{:S(2)}) collective-permute-start(f32[152,8,256]{2,1,0:T(8,128)S(1)} %collective-permute-done.refs_3_), channel_id=1, source_target_pairs={{28,16},{0,12},{29,17},{1,13},{30,18},{2,14},{31,19},{3,15}} | collective-permute-start | bytes 3735560 | tf_op jit(solution)/shard_map/ppermute | solution.py:967
  27.1 0.1 shard_map.77
  27.2 4.1 %collective-permute-start.7 = (f32[17,8,256]{2,1,0:T(8,128)S(1)}, f32[17,8,256]{2,1,0:T(8,128)S(1)}, u32[]{:S(2)}, u32[]{:S(2)}) collective-permute-start(f32[17,8,256]{2,1,0:T(8,128)S(1)} %get-tuple-element.42), channel_id=1, source_target_pairs={{0,4},{4,0},{8,12},{12,8},{16,20},{20,16},{24,28},{28,24},{1,5},{5... | collective-permute-start | bytes 417800 | tf_op jit(solution)/shard_map/ppermute | solution.py:964
  31.3 0.7 collective-permute-start.5
  32.6 0.0 collective-permute-done.7.refs_4_
  32.6 0.0 collective-permute-done.6.refs_3_
  32.6 0.0 copy-done.4
  32.6 9.8 %shard_map.78 = (f32[3,2,39,8,256]{4,3,2,1,0:T(8,128)S(1)}, f32[3,2,39,8,256]{4,3,2,1,0:T(8,128)S(1)}, f32[3,33,8,256]{3,2,1,0:T(8,128)S(1)}) custom-call(s32[1]{0:T(128)S(6)} %copy.18.refs_0_.index_ref, f32[3,4,32,8,256]{4,3,2,1,0:T(8,128)S(1)} %get-tuple-element.32.refs_1_, f32[512,128]{1,0:T(8,128)S(1)} %bitcast.31, ...), custom_call_target="tpu_custom_call" | custom-call | flops 100000000 | bytes 11173892 | tf_op jit(solution)/shard_map/pallas_call | solution.py:916
  42.4 0.0 collective-permute-done.5.refs_6_
  42.4 0.0 collective-permute-done.4.refs_5_
  42.4 10.2 %collective-permute-done.3.refs_4_ = f32[152,8,256]{2,1,0:T(8,128)S(1)} collective-permute-done((f32[152,8,256]{2,1,0:T(8,128)S(1)}, f32[152,8,256]{2,1,0:T(8,128)S(1)}, u32[]{:S(2)}, u32[]{:S(2)}) %collective-permute-start.3) | collective-permute-done | bytes 1245216 | tf_op jit(solution)/shard_map/ppermute | solution.py:967
  52.7 0.0 copy-start.1
  52.7 0.0 copy-start.5
  52.7 10.7 %shard_map.79 = (f32[3,4,32,8,256]{4,3,2,1,0:T(8,128)S(1)}, f32[5,32,8,256]{3,2,1,0:T(8,128)S(1)}, f32[5,5,8,256]{3,2,1,0:T(8,128)S(1)}, f32[4,32,8,256]{3,2,1,0...) custom-call(s32[1]{0:T(128)S(6)} %copy.18.refs_0_.index_ref, ...), custom_call_target="tpu_custom_call" | custom-call | flops 100000000 | bytes 19177476 | tf_op jit(solution)/shard_map/pallas_call | solution.py:916
  63.4 1.3 %collective-permute-start.9 = (f32[2,32,8,256]{3,2,1,0:T(8,128)S(1)}, f32[2,32,8,256]{3,2,1,0:T(8,128)S(1)}, u32[]{:S(2)}, u32[]{:S(2)}) collective-permute-start(f32[2,32,8,256]{3,2,1,0:T(8,128)S(1)} %get-tuple-element.49), channel_id=1, source_target_pairs={{4,8},{8,4},{20,24},{24,20},{12,28},{16,0},{5,9},{9,5},{21,25},{25... | collective-permute-start | bytes 1572872 | tf_op jit(solution)/shard_map/ppermute | solution.py:982
  64.7 3.8 %collective-permute-start.8 = (f32[4,32,8,256]{3,2,1,0:T(8,128)S(1)}, f32[4,32,8,256]{3,2,1,0:T(8,128)S(1)}, u32[]{:S(2)}, u32[]{:S(2)}) collective-permute-start(f32[4,32,8,256]{3,2,1,0:T(8,128)S(1)} %get-tuple-element.48), channel_id=1, source_target_pairs={{0,4},{4,0},{8,12},{12,8},{16,20},{20,16},{24,28},{28,24},{1,5},{5... | collective-permute-start | bytes 3145736 | tf_op jit(solution)/shard_map/ppermute | solution.py:989
  68.5 2.2 %collective-permute-start.10 = (f32[5,5,8,256]{3,2,1,0:T(8,128)S(1)}, f32[5,5,8,256]{3,2,1,0:T(8,128)S(1)}, u32[]{:S(2)}, u32[]{:S(2)}) collective-permute-start(f32[5,5,8,256]{3,2,1,0:T(8,128)S(1)} %get-tuple-element.50.states_ref), channel_id=1, source_target_pairs={{0,1},{1,0},{2,3},{3,2},{4,5},{5,4},{6,7},{7,6},{8,9},{9,8},{10,11... | collective-permute-start | bytes 614408 | tf_op jit(solution)/shard_map/ppermute | solution.py:984
  70.7 0.7 collective-permute-start.12
  71.4 4.6 %collective-permute-done.10.partner_ref = f32[5,5,8,256]{3,2,1,0:T(8,128)S(1)} collective-permute-done((f32[5,5,8,256]{3,2,1,0:T(8,128)S(1)}, f32[5,5,8,256]{3,2,1,0:T(8,128)S(1)}, u32[]{:S(2)}, u32[]{:S(2)}) %collective-permute-start.10) | collective-permute-done | bytes 204832 | tf_op jit(solution)/shard_map/ppermute | solution.py:984
  76.0 0.0 collective-permute-done.9.b1_ref
  76.0 3.4 %collective-permute-start.11 = (f32[2,32,8,256]{3,2,1,0:T(8,128)S(1)}, f32[2,32,8,256]{3,2,1,0:T(8,128)S(1)}, u32[]{:S(2)}, u32[]{:S(2)}) collective-permute-start(f32[2,32,8,256]{3,2,1,0:T(8,128)S(1)} %collective-permute-done.9.b1_ref), channel_id=1, source_target_pairs={{28,16},{0,12},{29,17},{1,13},{30,18},{2,14},{31,19},{3,15}} | collective-permute-start | bytes 1572872 | tf_op jit(solution)/shard_map/ppermute | solution.py:988
  79.5 3.7 %collective-permute-start.13 = (f32[5,5,8,256]{3,2,1,0:T(8,128)S(1)}, f32[5,5,8,256]{3,2,1,0:T(8,128)S(1)}, u32[]{:S(2)}, u32[]{:S(2)}) collective-permute-start(f32[5,5,8,256]{3,2,1,0:T(8,128)S(1)} %shard_map.80), channel_id=1, source_target_pairs={{1,2},{2,1},{3,0},{0,3},{5,6},{6,5},{7,4},{4,7},{9,10},{10,9},{11,... | collective-permute-start | bytes 614408 | tf_op jit(solution)/shard_map/ppermute | solution.py:986
  83.2 5.4 %collective-permute-done.13.other_ref = f32[5,5,8,256]{3,2,1,0:T(8,128)S(1)} collective-permute-done((f32[5,5,8,256]{3,2,1,0:T(8,128)S(1)}, f32[5,5,8,256]{3,2,1,0:T(8,128)S(1)}, u32[]{:S(2)}, u32[]{:S(2)}) %collective-permute-start.13) | collective-permute-done | bytes 204832 | tf_op jit(solution)/shard_map/ppermute | solution.py:986
  88.6 0.1 shard_map.81
  88.7 0.1 collective-permute-start.14
  88.8 0.7 collective-permute-start.15
  89.4 0.0 collective-permute-done.12.b2_ref
  89.5 0.7 collective-permute-done.14.ia_ref
  90.2 0.0 collective-permute-done.15.ib_ref
  90.2 0.0 collective-permute-done.11.b3_ref
  90.2 0.0 collective-permute-done.8.ba_ref
  90.2 0.0 copy-done.1
  90.2 0.0 copy-done.5
  90.2 0.0 copy-start.2
  90.2 14.2 %shard_map.82 = (f32[6144,128]{1,0:T(8,128)}, f32[6144,128]{1,0:T(8,128)S(1)}, f32[1,128]{1,0:T(1,128)S(1)}) custom-call(s32[1]{0:T(128)S(6)} %copy.18.refs_0_.index_ref, s32[4,4]{1,0:T(4,128)S(1)} %copy-done.5, f32[3,4,32,8,256]{4,3,2,1,0:T(8,128)S(1)} %get-tuple-element.46.v_ref, f32[5,32,8,256]{3,2,1,0:T(8,128)S(1)} %get-tuple-element.47.bw_ref, ...), custom_call_target="tpu_custom_call" | custom-call | flops 100000000 | bytes 17048132 | tf_op jit(solution)/shard_map/pallas_call | solution.py:916
  104.4 20.0 %all_to_all.5 = f32[32,1,128]{2,1,0:T(1,128)S(1)} all-to-all(f32[32,1,128]{2,1,0:T(1,128)S(1)} %broadcast_in_dim.9), channel_id=1, replica_groups=mesh['gx'=8,'gz'=4] {'gx','gz'}, dimensions={0} | all-to-all | bytes 32768 | tf_op jit(solution)/shard_map/all_to_all | solution.py:1008
  124.5 0.0 copy-done.2
  124.5 2.6 %shard_map.83 = (f32[6144,128]{1,0:T(8,128)}, f32[4,4]{1,0:T(4,128)}) custom-call(s32[1]{0:T(128)S(6)} %copy.18.refs_0_.index_ref, f32[32,128]{1,0:T(8,128)S(1)} %bitcast.33, f32[6144,128]{1,0:T(8,128)S(1)} %bitcast.29, f32[6144,128]{1,0:T(8,128)S(1)} %get-tuple-element.58.solved_ref), custom_call_target="tpu_custom_call" | custom-call | flops 10000000 | bytes 9453636 | tf_op jit(solution)/shard_map/pallas_call | solution.py:916
  (2 shorter events, 0.1 us)
Async XLA Ops:
  0.6 1.9 %copy-start = (f32[3,64,4,4,256]{4,3,2,1,0:T(4,128)S(1)}, f32[3,64,4,4,256]{4,3,2,1,0:T(4,128)}, u32[]{:S(2)}) copy-start(f32[3,64,4,4,256]{4,3,2,1,0:T(4,128)} %param.5) | copy-start | bytes 9437188
  2.5 0.9 copy-start.3
  3.5 29.1 %copy-start.4 = (f32[64,4,256]{2,1,0:T(4,128)S(1)}, f32[64,4,256]{2,1,0:T(4,128)}, u32[]{:S(2)}) copy-start(f32[64,4,256]{2,1,0:T(4,128)} %param.7) | copy-start | bytes 786436
  5.0 27.6 %collective-permute-start.6 = (f32[312,8,256]{2,1,0:T(8,128)S(1)}, f32[312,8,256]{2,1,0:T(8,128)S(1)}, u32[]{:S(2)}, u32[]{:S(2)}) collective-permute-start(f32[312,8,256]{2,1,0:T(8,128)S(1)} %get-tuple-element.41), channel_id=1, source_target_pairs={{0,4},{4,0},{8,12},{12,8},{16,20},{20,16},{24,28},{28,24},{1,5},{5... | collective-permute-start | bytes 7667720 | tf_op jit(solution)/shard_map/ppermute | solution.py:961
  5.5 18.8 %collective-permute-start = (f32[152,8,256]{2,1,0:T(8,128)S(1)}, f32[152,8,256]{2,1,0:T(8,128)S(1)}, u32[]{:S(2)}, u32[]{:S(2)}) collective-permute-start(f32[152,8,256]{2,1,0:T(8,128)S(1)} %get-tuple-element.33), channel_id=1, source_target_pairs={{4,8},{8,4},{20,24},{24,20},{12,28},{16,0},{5,9},{9,5},{21,25},{25... | collective-permute-start | bytes 3735560 | tf_op jit(solution)/shard_map/ppermute | solution.py:957
  6.8 7.0 %collective-permute-start.1 = (f32[26,8,256]{2,1,0:T(8,128)S(1)}, f32[26,8,256]{2,1,0:T(8,128)S(1)}, u32[]{:S(2)}, u32[]{:S(2)}) collective-permute-start(f32[26,8,256]{2,1,0:T(8,128)S(1)} %get-tuple-element.34), channel_id=1, source_target_pairs={{0,1},{1,0},{2,3},{3,2},{4,5},{5,4},{6,7},{7,6},{8,9},{9,8},{10,11... | collective-permute-start | bytes 638984 | tf_op jit(solution)/shard_map/ppermute | solution.py:958
  9.5 12.0 %collective-permute-start.2 = (f32[26,8,256]{2,1,0:T(8,128)S(1)}, f32[26,8,256]{2,1,0:T(8,128)S(1)}, u32[]{:S(2)}, u32[]{:S(2)}) collective-permute-start(f32[26,8,256]{2,1,0:T(8,128)S(1)} %get-tuple-element.35), channel_id=1, source_target_pairs={{1,2},{2,1},{3,0},{0,3},{5,6},{6,5},{7,4},{4,7},{9,10},{10,9},{11,... | collective-permute-start | bytes 638984 | tf_op jit(solution)/shard_map/ppermute | solution.py:959
  12.0 30.5 %collective-permute-start.4 = (f32[160,8,256]{2,1,0:T(8,128)S(1)}, f32[160,8,256]{2,1,0:T(8,128)S(1)}, u32[]{:S(2)}, u32[]{:S(2)}) collective-permute-start(f32[160,8,256]{2,1,0:T(8,128)S(1)} %get-tuple-element.37), channel_id=1, source_target_pairs={{4,8},{8,4},{12,16},{16,12},{20,24},{24,20},{5,9},{9,5},{13,17},{1... | collective-permute-start | bytes 3932168 | tf_op jit(solution)/shard_map/ppermute | solution.py:960
  24.3 28.3 %collective-permute-start.3 = (f32[152,8,256]{2,1,0:T(8,128)S(1)}, f32[152,8,256]{2,1,0:T(8,128)S(1)}, u32[]{:S(2)}, u32[]{:S(2)}) collective-permute-start(f32[152,8,256]{2,1,0:T(8,128)S(1)} %collective-permute-done.refs_3_), channel_id=1, source_target_pairs={{28,16},{0,12},{29,17},{1,13},{30,18},{2,14},{31,19},{3,15}} | collective-permute-start | bytes 3735560 | tf_op jit(solution)/shard_map/ppermute | solution.py:967
  27.2 5.4 %collective-permute-start.7 = (f32[17,8,256]{2,1,0:T(8,128)S(1)}, f32[17,8,256]{2,1,0:T(8,128)S(1)}, u32[]{:S(2)}, u32[]{:S(2)}) collective-permute-start(f32[17,8,256]{2,1,0:T(8,128)S(1)} %get-tuple-element.42), channel_id=1, source_target_pairs={{0,4},{4,0},{8,12},{12,8},{16,20},{20,16},{24,28},{28,24},{1,5},{5... | collective-permute-start | bytes 417800 | tf_op jit(solution)/shard_map/ppermute | solution.py:964
  31.3 11.1 %collective-permute-start.5 = (f32[17,8,256]{2,1,0:T(8,128)S(1)}, f32[17,8,256]{2,1,0:T(8,128)S(1)}, u32[]{:S(2)}, u32[]{:S(2)}) collective-permute-start(f32[17,8,256]{2,1,0:T(8,128)S(1)} %get-tuple-element.38), channel_id=1, source_target_pairs={{4,8},{8,4},{12,16},{16,12},{20,24},{24,20},{5,9},{9,5},{13,17},{1... | collective-permute-start | bytes 417800 | tf_op jit(solution)/shard_map/ppermute | solution.py:965
  52.7 37.5 %copy-start.1 = (f32[3,64,4,4,256]{4,3,2,1,0:T(4,128)S(1)}, f32[3,64,4,4,256]{4,3,2,1,0:T(4,128)}, u32[]{:S(2)}) copy-start(f32[3,64,4,4,256]{4,3,2,1,0:T(4,128)} %param.5) | copy-start | bytes 9437188
  52.7 37.5 %copy-start.5 = (s32[4,4]{1,0:T(4,128)S(1)}, s32[4,4]{1,0:T(4,128)}, u32[]{:S(2)}) copy-start(s32[4,4]{1,0:T(4,128)} %cells_ref.1) | copy-start | bytes 196
  63.4 12.6 %collective-permute-start.9 = (f32[2,32,8,256]{3,2,1,0:T(8,128)S(1)}, f32[2,32,8,256]{3,2,1,0:T(8,128)S(1)}, u32[]{:S(2)}, u32[]{:S(2)}) collective-permute-start(f32[2,32,8,256]{3,2,1,0:T(8,128)S(1)} %get-tuple-element.49), channel_id=1, source_target_pairs={{4,8},{8,4},{20,24},{24,20},{12,28},{16,0},{5,9},{9,5},{21,25},{25... | collective-permute-start | bytes 1572872 | tf_op jit(solution)/shard_map/ppermute | solution.py:982
  64.7 25.4 %collective-permute-start.8 = (f32[4,32,8,256]{3,2,1,0:T(8,128)S(1)}, f32[4,32,8,256]{3,2,1,0:T(8,128)S(1)}, u32[]{:S(2)}, u32[]{:S(2)}) collective-permute-start(f32[4,32,8,256]{3,2,1,0:T(8,128)S(1)} %get-tuple-element.48), channel_id=1, source_target_pairs={{0,4},{4,0},{8,12},{12,8},{16,20},{20,16},{24,28},{28,24},{1,5},{5... | collective-permute-start | bytes 3145736 | tf_op jit(solution)/shard_map/ppermute | solution.py:989
  68.5 7.5 %collective-permute-start.10 = (f32[5,5,8,256]{3,2,1,0:T(8,128)S(1)}, f32[5,5,8,256]{3,2,1,0:T(8,128)S(1)}, u32[]{:S(2)}, u32[]{:S(2)}) collective-permute-start(f32[5,5,8,256]{3,2,1,0:T(8,128)S(1)} %get-tuple-element.50.states_ref), channel_id=1, source_target_pairs={{0,1},{1,0},{2,3},{3,2},{4,5},{5,4},{6,7},{7,6},{8,9},{9,8},{10,11... | collective-permute-start | bytes 614408 | tf_op jit(solution)/shard_map/ppermute | solution.py:984
  70.7 18.8 %collective-permute-start.12 = (f32[2,32,8,256]{3,2,1,0:T(8,128)S(1)}, f32[2,32,8,256]{3,2,1,0:T(8,128)S(1)}, u32[]{:S(2)}, u32[]{:S(2)}) collective-permute-start(f32[2,32,8,256]{3,2,1,0:T(8,128)S(1)} %get-tuple-element.52), channel_id=1, source_target_pairs={{4,8},{8,4},{12,16},{16,12},{20,24},{24,20},{5,9},{9,5},{13,17},{1... | collective-permute-start | bytes 1572872 | tf_op jit(solution)/shard_map/ppermute | solution.py:983
  76.0 14.1 %collective-permute-start.11 = (f32[2,32,8,256]{3,2,1,0:T(8,128)S(1)}, f32[2,32,8,256]{3,2,1,0:T(8,128)S(1)}, u32[]{:S(2)}, u32[]{:S(2)}) collective-permute-start(f32[2,32,8,256]{3,2,1,0:T(8,128)S(1)} %collective-permute-done.9.b1_ref), channel_id=1, source_target_pairs={{28,16},{0,12},{29,17},{1,13},{30,18},{2,14},{31,19},{3,15}} | collective-permute-start | bytes 1572872 | tf_op jit(solution)/shard_map/ppermute | solution.py:988
  79.5 9.1 %collective-permute-start.13 = (f32[5,5,8,256]{3,2,1,0:T(8,128)S(1)}, f32[5,5,8,256]{3,2,1,0:T(8,128)S(1)}, u32[]{:S(2)}, u32[]{:S(2)}) collective-permute-start(f32[5,5,8,256]{3,2,1,0:T(8,128)S(1)} %shard_map.80), channel_id=1, source_target_pairs={{1,2},{2,1},{3,0},{0,3},{5,6},{6,5},{7,4},{4,7},{9,10},{10,9},{11,... | collective-permute-start | bytes 614408 | tf_op jit(solution)/shard_map/ppermute | solution.py:986
  88.7 1.5 %collective-permute-start.14 = (f32[5,4,8,256]{3,2,1,0:T(8,128)S(1)}, f32[5,4,8,256]{3,2,1,0:T(8,128)S(1)}, u32[]{:S(2)}, u32[]{:S(2)}) collective-permute-start(f32[5,4,8,256]{3,2,1,0:T(8,128)S(1)} %get-tuple-element.54), channel_id=1, source_target_pairs={{0,4},{4,0},{8,12},{12,8},{16,20},{20,16},{24,28},{28,24},{1,5},{5... | collective-permute-start | bytes 491528 | tf_op jit(solution)/shard_map/ppermute | solution.py:996
  88.8 1.4 %collective-permute-start.15 = (f32[5,4,8,256]{3,2,1,0:T(8,128)S(1)}, f32[5,4,8,256]{3,2,1,0:T(8,128)S(1)}, u32[]{:S(2)}, u32[]{:S(2)}) collective-permute-start(f32[5,4,8,256]{3,2,1,0:T(8,128)S(1)} %get-tuple-element.55), channel_id=1, source_target_pairs={{4,8},{8,4},{12,16},{16,12},{20,24},{24,20},{5,9},{9,5},{13,17},{1... | collective-permute-start | bytes 491528 | tf_op jit(solution)/shard_map/ppermute | solution.py:995
  90.2 34.3 %copy-start.2 = (f32[3,64,4,4,256]{4,3,2,1,0:T(4,128)S(1)}, f32[3,64,4,4,256]{4,3,2,1,0:T(4,128)}, u32[]{:S(2)}) copy-start(f32[3,64,4,4,256]{4,3,2,1,0:T(4,128)} %param.6) | copy-start | bytes 9437188

commit v7 on v6

--- a/solution.py
+++ b/solution.py
@@ -234,7 +234,7 @@
         forward, backward = carry
         return cascade(forward, read(t)), cascade(backward, read(HALF - 1 - t))
 
-    return lax.fori_loop(0, HALF, body, ((zero,) * POISSON, (zero,) * POISSON), unroll=HALF)
+    return lax.fori_loop(0, HALF, body, ((zero,) * POISSON, (zero,) * POISSON), unroll=8)
 
 
 def turned(table, states, row):
@@ -508,7 +508,7 @@
                         hand(x, zz + k, cells)
                 return 0
 
-            lax.fori_loop(0, -(-extent // depth), body, 0, unroll=2)
+            lax.fori_loop(0, -(-extent // depth), body, 0, unroll=3)
 
         handed_first, handed_second, handed_third = HANDED[parity]
         for component in range(3):
@@ -603,7 +603,7 @@
                 return past
 
             start = tuple(finished(-1, 1)[0]) if component == 2 else 0
-            lax.fori_loop(0, HALF // 4, diverge, start, unroll=2)
+            lax.fori_loop(0, HALF // 4, diverge, start, unroll=4)
 
     for parity in (0, 1):
 
@@ -633,7 +633,7 @@
         s_ref[POISSON, layer] = bw_ref[layer, 0]
         return 0
 
-    lax.fori_loop(0, 5, states, 0)
+    lax.fori_loop(0, 5, states, 0, unroll=5)
 
 
 def pressure_kernel(
@@ -697,48 +697,65 @@
                 else:
                     gather(inside, outside, enter_inside, enter_outside)
 
-    def solve(x, _):
-        forward, backward = half_states(lambda t: f_ref[x, t])
-        arriving = [i_ref[i, x] for i in range(POISSON)]
-        swapped = [swap(entry) for entry in arriving]
+    def solve(layers, least):
+        count = len(layers)
+        zero = (jnp.zeros((8, 256), jnp.float32),) * POISSON
+
+        def halves(t, carry):
+            return tuple(
+                (cascade(up, f_ref[x, t]), cascade(down, f_ref[x, HALF - 1 - t]))
+                for x, (up, down) in zip(layers, carry)
+            )
+
+        ends = lax.fori_loop(0, HALF, halves, ((zero, zero),) * count, unroll=8)
         onward = []
         back = []
-        for i in range(POISSON):
-            carried = turned(HALF_TABLE, swapped, i)
-            onward.append(swap(jnp.where(lower, forward[i] + carried, arriving[i])))
-            back.append(swap(jnp.where(lower, arriving[i], backward[i] + carried)))
-
-        def ahead(zz, state):
-            state = cascade(state, f_ref[x, zz])
-            for i in range(POISSON):
-                u_ref[i, zz] = state[i]
-            return state
-
-        lax.fori_loop(0, HALF, ahead, tuple(onward), unroll=8)
-        end = cascade([u_ref[i, HALF - 1] for i in range(POISSON)], f_ref[x, HALF])
-        for i in range(POISSON):
-            u_ref[i, HALF] = end[i]
-
-        def mix(zz, state):
-            both = [f_ref[x, zz]] + [u_ref[i, zz] + state[i] for i in range(POISSON)]
-            for power in range(POISSON):
-                total = MIXES[power][0] * both[0]
-                for i in range(1, power + 2):
-                    total = total + MIXES[power][i] * both[i]
-                q_ref[power, x, zz] = total
+        for x, (forward, backward) in zip(layers, ends):
+            arriving = [i_ref[i, x] for i in range(POISSON)]
+            swapped = [swap(entry) for entry in arriving]
+            carried = [turned(HALF_TABLE, swapped, i) for i in range(POISSON)]
+            onward.append(
+                tuple(
+                    swap(jnp.where(lower, forward[i] + carried[i], arriving[i])) for i in range(POISSON)
+                )
+            )
+            back.append(
+                tuple(
+                    swap(jnp.where(lower, arriving[i], backward[i] + carried[i])) for i in range(POISSON)
+                )
+            )
+
+        def ahead(zz, states):
+            states = tuple(cascade(state, f_ref[x, zz]) for x, state in zip(layers, states))
+            for slot, state in enumerate(states):
+                for i in range(POISSON):
+                    u_ref[slot, i, zz] = state[i]
+            return states
+
+        ahead(HALF, lax.fori_loop(0, HALF, ahead, tuple(onward), unroll=8))
+
+        def mix(zz, states):
+            for slot, (x, state) in enumerate(zip(layers, states)):
+                both = [f_ref[x, zz]] + [u_ref[slot, i, zz] + state[i] for i in range(POISSON)]
+                for power in range(least, POISSON):
+                    total = MIXES[power][0] * both[0]
+                    for i in range(1, power + 2):
+                        total = total + MIXES[power][i] * both[i]
+                    q_ref[power, x, zz] = total
 
         mix(HALF, back)
 
-        def behind(t, state):
+        def behind(t, states):
             zz = HALF - 1 - t
-            state = cascade(state, f_ref[x, zz])
-            mix(zz, state)
-            return state
+            states = tuple(cascade(state, f_ref[x, zz]) for x, state in zip(layers, states))
+            mix(zz, states)
+            return states
 
         lax.fori_loop(0, HALF, behind, tuple(back), unroll=8)
-        return 0
-
-    lax.fori_loop(0, 11, solve, 0)
+
+    solve((5,), 0)
+    for distance in (-1, 0, 1, 2, 3):
+        solve((3 - distance, 7 + distance), max(distance, 0))
     for power in (2, 1, 0):
 
         def apply(zz, _, power=power):
@@ -998,7 +1015,7 @@
     new_rows, solved, sums = call(
         pressure_kernel,
         [factor_rows.shape, factor_rows.shape, (1, 128)],
-        [block, (POISSON + 1, 11, *cell), (POISSON, HALF + 1, *cell), (POISSON, *block), (32, 128)]
+        [block, (POISSON + 1, 11, *cell), (2, POISSON, HALF + 1, *cell), (POISSON, *block), (32, 128)]
         + [factor_rows.shape],
         [shift_index, sensor_cells, velocity, sides, pa_in, pb1_in, pb3_in, pb2_in]
         + [entering, enter_a, enter_b, factor_rows],

time: 127 us -> 126 us (level)
  Pallas kernels: 39.1 us -> 36.6 us
    pallas_call x8, Pallas kernels: 39.1 us -> 36.6 us  [call(): pl.pallas_call(kernel, out_shape=arrays, in_specs=places, out_specs=resul...]
  transfers between devices with their start and end apart: 16 -> 16, of which waited for: 7 -> 7; matrix products, arithmetic and copies ran while one was open for 0% -> 0% of each run, Pallas kernels for 8% -> 7%
where the time goes in v7:
time: 126 us
  Pallas kernels  36.6 us (29%)
  waiting for transfers between devices  33.7 us (27%)
  starting transfers between devices  31 us (25%)
  blocking collectives  20 us (16%)
  local copies, waits for them, and re-layouts  2.86 us (2%)
  between operations  1.66 us (1%)
    pallas_call x8, Pallas kernels, call(): pl.pallas_call(kernel, out_shape=arrays, in_specs=places, out_specs=resul...  36.6 us
    all_to_all x1, blocking collectives, fast_shards(): lax.all_to_all(jnp.broadcast_to(sums[None], (devices, 1, 128)), ('gx', 'g...  20 us
    ppermute x1, waiting for transfers between devices, fast_shards(): b3_in = lax.ppermute(b1_in, 'gx', forward_round)  11.3 us
    ppermute x1, waiting for transfers between devices, fast_shards(): z2 = lax.ppermute(z2, 'gz', far)  7.59 us
    ppermute x1, waiting for transfers between devices, fast_shards(): other = lax.ppermute(joined, 'gz', far)  5.44 us
    ppermute x1, waiting for transfers between devices, fast_shards(): partner = lax.ppermute(states, 'gz', near)  4.63 us
    ppermute x1, starting transfers between devices, fast_shards(): ca = lax.ppermute(ca, 'gx', swap_in)  4.12 us
    ppermute x1, starting transfers between devices, fast_shards(): pa_in = lax.ppermute(pa, 'gx', swap_in)  3.8 us
  transfers between devices with their start and end apart: 16, of which 7 were waited for; matrix products, arithmetic and copies ran while one was open for 0% of the time, Pallas kernels for 7%

profile of v7, /device:TPU:0, one launch (start us, length us, event | category | flops | bytes accessed | tf_op | source)
XLA Modules:
  0.0 125.9 jit_solution(823543750725733804)
XLA Ops:
  0.6 0.0 copy-start
  0.6 1.9 %copy-done = f32[3,64,4,4,256]{4,3,2,1,0:T(4,128)S(1)} copy-done((f32[3,64,4,4,256]{4,3,2,1,0:T(4,128)S(1)}, f32[3,64,4,4,256]{4,3,2,1,0:T(4,128)}, u32[]{:S(2)}) %copy-start) | copy-done | bytes 3145752
  2.5 0.0 copy-start.3
  2.5 0.9 copy-done.3
  3.5 0.0 copy-start.4
  3.5 1.5 %shard_map.76 = (f32[3,4,32,8,256]{4,3,2,1,0:T(8,128)S(1)}, f32[312,8,256]{2,1,0:T(8,128)S(1)}, f32[152,8,256]{2,1,0:T(8,128)S(1)}, f32[160,8,256]{2,1,0:T(8,128...) custom-call(f32[6144,128]{1,0:T(8,128)S(1)} %bitcast.27, f32[512,128]{1,0:T(8,128)S(1)} %bitcast.30), custom_call_target="tpu_custom_call" | custom-call | flops 1000000 | bytes 12091392 | tf_op jit(solution)/shard_map/pallas_call | solution.py:933
  5.0 0.5 collective-permute-start.6
  5.5 1.3 %collective-permute-start = (f32[152,8,256]{2,1,0:T(8,128)S(1)}, f32[152,8,256]{2,1,0:T(8,128)S(1)}, u32[]{:S(2)}, u32[]{:S(2)}) collective-permute-start(f32[152,8,256]{2,1,0:T(8,128)S(1)} %get-tuple-element.33), channel_id=1, source_target_pairs={{4,8},{8,4},{20,24},{24,20},{12,28},{16,0},{5,9},{9,5},{21,25},{25... | collective-permute-start | bytes 3735560 | tf_op jit(solution)/shard_map/ppermute | solution.py:974
  6.8 2.7 %collective-permute-start.1 = (f32[26,8,256]{2,1,0:T(8,128)S(1)}, f32[26,8,256]{2,1,0:T(8,128)S(1)}, u32[]{:S(2)}, u32[]{:S(2)}) collective-permute-start(f32[26,8,256]{2,1,0:T(8,128)S(1)} %get-tuple-element.34), channel_id=1, source_target_pairs={{0,1},{1,0},{2,3},{3,2},{4,5},{5,4},{6,7},{7,6},{8,9},{9,8},{10,11... | collective-permute-start | bytes 638984 | tf_op jit(solution)/shard_map/ppermute | solution.py:975
  9.5 2.5 %collective-permute-start.2 = (f32[26,8,256]{2,1,0:T(8,128)S(1)}, f32[26,8,256]{2,1,0:T(8,128)S(1)}, u32[]{:S(2)}, u32[]{:S(2)}) collective-permute-start(f32[26,8,256]{2,1,0:T(8,128)S(1)} %get-tuple-element.35), channel_id=1, source_target_pairs={{1,2},{2,1},{3,0},{0,3},{5,6},{6,5},{7,4},{4,7},{9,10},{10,9},{11,... | collective-permute-start | bytes 638984 | tf_op jit(solution)/shard_map/ppermute | solution.py:976
  12.0 0.7 collective-permute-start.4
  12.7 1.1 collective-permute-done.1.z1_ref.refs_5_.refs_7_
  13.8 7.6 %collective-permute-done.2.z2_ref.refs_6_.refs_8_ = f32[26,8,256]{2,1,0:T(8,128)S(1)} collective-permute-done((f32[26,8,256]{2,1,0:T(8,128)S(1)}, f32[26,8,256]{2,1,0:T(8,128)S(1)}, u32[]{:S(2)}, u32[]{:S(2)}) %collective-permute-start.2) | collective-permute-done | bytes 213024 | tf_op jit(solution)/shard_map/ppermute | solution.py:976
  21.4 2.9 %collective-permute-done.refs_3_ = f32[152,8,256]{2,1,0:T(8,128)S(1)} collective-permute-done((f32[152,8,256]{2,1,0:T(8,128)S(1)}, f32[152,8,256]{2,1,0:T(8,128)S(1)}, u32[]{:S(2)}, u32[]{:S(2)}) %collective-permute-start) | collective-permute-done | bytes 1245216 | tf_op jit(solution)/shard_map/ppermute | solution.py:974
  24.3 2.8 %collective-permute-start.3 = (f32[152,8,256]{2,1,0:T(8,128)S(1)}, f32[152,8,256]{2,1,0:T(8,128)S(1)}, u32[]{:S(2)}, u32[]{:S(2)}) collective-permute-start(f32[152,8,256]{2,1,0:T(8,128)S(1)} %collective-permute-done.refs_3_), channel_id=1, source_target_pairs={{28,16},{0,12},{29,17},{1,13},{30,18},{2,14},{31,19},{3,15}} | collective-permute-start | bytes 3735560 | tf_op jit(solution)/shard_map/ppermute | solution.py:984
  27.1 0.1 shard_map.77
  27.2 4.1 %collective-permute-start.7 = (f32[17,8,256]{2,1,0:T(8,128)S(1)}, f32[17,8,256]{2,1,0:T(8,128)S(1)}, u32[]{:S(2)}, u32[]{:S(2)}) collective-permute-start(f32[17,8,256]{2,1,0:T(8,128)S(1)} %get-tuple-element.42), channel_id=1, source_target_pairs={{0,4},{4,0},{8,12},{12,8},{16,20},{20,16},{24,28},{28,24},{1,5},{5... | collective-permute-start | bytes 417800 | tf_op jit(solution)/shard_map/ppermute | solution.py:981
  31.3 0.7 collective-permute-start.5
  32.6 0.0 collective-permute-done.7.refs_4_
  32.6 0.0 collective-permute-done.6.refs_3_
  32.6 0.0 copy-done.4
  32.6 8.7 %shard_map.78 = (f32[3,2,39,8,256]{4,3,2,1,0:T(8,128)S(1)}, f32[3,2,39,8,256]{4,3,2,1,0:T(8,128)S(1)}, f32[3,33,8,256]{3,2,1,0:T(8,128)S(1)}) custom-call(s32[1]{0:T(128)S(6)} %copy.18.refs_0_.index_ref, f32[3,4,32,8,256]{4,3,2,1,0:T(8,128)S(1)} %get-tuple-element.32.refs_1_, f32[512,128]{1,0:T(8,128)S(1)} %bitcast.31, ...), custom_call_target="tpu_custom_call" | custom-call | flops 100000000 | bytes 11173892 | tf_op jit(solution)/shard_map/pallas_call | solution.py:933
  41.3 0.0 collective-permute-done.5.refs_6_
  41.3 0.0 collective-permute-done.4.refs_5_
  41.4 11.3 %collective-permute-done.3.refs_4_ = f32[152,8,256]{2,1,0:T(8,128)S(1)} collective-permute-done((f32[152,8,256]{2,1,0:T(8,128)S(1)}, f32[152,8,256]{2,1,0:T(8,128)S(1)}, u32[]{:S(2)}, u32[]{:S(2)}) %collective-permute-start.3) | collective-permute-done | bytes 1245216 | tf_op jit(solution)/shard_map/ppermute | solution.py:984
  52.7 0.0 copy-start.1
  52.7 0.0 copy-start.5
  52.7 10.0 %shard_map.79 = (f32[3,4,32,8,256]{4,3,2,1,0:T(8,128)S(1)}, f32[5,32,8,256]{3,2,1,0:T(8,128)S(1)}, f32[5,5,8,256]{3,2,1,0:T(8,128)S(1)}, f32[4,32,8,256]{3,2,1,0...) custom-call(s32[1]{0:T(128)S(6)} %copy.18.refs_0_.index_ref, ...), custom_call_target="tpu_custom_call" | custom-call | flops 100000000 | bytes 19177476 | tf_op jit(solution)/shard_map/pallas_call | solution.py:933
  62.7 1.3 %collective-permute-start.9 = (f32[2,32,8,256]{3,2,1,0:T(8,128)S(1)}, f32[2,32,8,256]{3,2,1,0:T(8,128)S(1)}, u32[]{:S(2)}, u32[]{:S(2)}) collective-permute-start(f32[2,32,8,256]{3,2,1,0:T(8,128)S(1)} %get-tuple-element.49), channel_id=1, source_target_pairs={{4,8},{8,4},{20,24},{24,20},{12,28},{16,0},{5,9},{9,5},{21,25},{25... | collective-permute-start | bytes 1572872 | tf_op jit(solution)/shard_map/ppermute | solution.py:999
  64.0 3.8 %collective-permute-start.8 = (f32[4,32,8,256]{3,2,1,0:T(8,128)S(1)}, f32[4,32,8,256]{3,2,1,0:T(8,128)S(1)}, u32[]{:S(2)}, u32[]{:S(2)}) collective-permute-start(f32[4,32,8,256]{3,2,1,0:T(8,128)S(1)} %get-tuple-element.48), channel_id=1, source_target_pairs={{0,4},{4,0},{8,12},{12,8},{16,20},{20,16},{24,28},{28,24},{1,5},{5... | collective-permute-start | bytes 3145736 | tf_op jit(solution)/shard_map/ppermute | solution.py:1006
  67.8 2.2 %collective-permute-start.10 = (f32[5,5,8,256]{3,2,1,0:T(8,128)S(1)}, f32[5,5,8,256]{3,2,1,0:T(8,128)S(1)}, u32[]{:S(2)}, u32[]{:S(2)}) collective-permute-start(f32[5,5,8,256]{3,2,1,0:T(8,128)S(1)} %get-tuple-element.50.states_ref), channel_id=1, source_target_pairs={{0,1},{1,0},{2,3},{3,2},{4,5},{5,4},{6,7},{7,6},{8,9},{9,8},{10,11... | collective-permute-start | bytes 614408 | tf_op jit(solution)/shard_map/ppermute | solution.py:1001
  70.0 0.7 collective-permute-start.12
  70.7 4.6 %collective-permute-done.10.partner_ref = f32[5,5,8,256]{3,2,1,0:T(8,128)S(1)} collective-permute-done((f32[5,5,8,256]{3,2,1,0:T(8,128)S(1)}, f32[5,5,8,256]{3,2,1,0:T(8,128)S(1)}, u32[]{:S(2)}, u32[]{:S(2)}) %collective-permute-start.10) | collective-permute-done | bytes 204832 | tf_op jit(solution)/shard_map/ppermute | solution.py:1001
  75.3 0.0 collective-permute-done.9.b1_ref
  75.3 3.4 %collective-permute-start.11 = (f32[2,32,8,256]{3,2,1,0:T(8,128)S(1)}, f32[2,32,8,256]{3,2,1,0:T(8,128)S(1)}, u32[]{:S(2)}, u32[]{:S(2)}) collective-permute-start(f32[2,32,8,256]{3,2,1,0:T(8,128)S(1)} %collective-permute-done.9.b1_ref), channel_id=1, source_target_pairs={{28,16},{0,12},{29,17},{1,13},{30,18},{2,14},{31,19},{3,15}} | collective-permute-start | bytes 1572872 | tf_op jit(solution)/shard_map/ppermute | solution.py:1005
  78.8 3.7 %collective-permute-start.13 = (f32[5,5,8,256]{3,2,1,0:T(8,128)S(1)}, f32[5,5,8,256]{3,2,1,0:T(8,128)S(1)}, u32[]{:S(2)}, u32[]{:S(2)}) collective-permute-start(f32[5,5,8,256]{3,2,1,0:T(8,128)S(1)} %shard_map.80), channel_id=1, source_target_pairs={{1,2},{2,1},{3,0},{0,3},{5,6},{6,5},{7,4},{4,7},{9,10},{10,9},{11,... | collective-permute-start | bytes 614408 | tf_op jit(solution)/shard_map/ppermute | solution.py:1003
  82.4 5.4 %collective-permute-done.13.other_ref = f32[5,5,8,256]{3,2,1,0:T(8,128)S(1)} collective-permute-done((f32[5,5,8,256]{3,2,1,0:T(8,128)S(1)}, f32[5,5,8,256]{3,2,1,0:T(8,128)S(1)}, u32[]{:S(2)}, u32[]{:S(2)}) %collective-permute-start.13) | collective-permute-done | bytes 204832 | tf_op jit(solution)/shard_map/ppermute | solution.py:1003
  87.9 0.1 shard_map.81
  88.0 0.1 collective-permute-start.14
  88.1 0.7 collective-permute-start.15
  88.7 0.0 collective-permute-done.12.b2_ref
  88.7 0.7 collective-permute-done.14.ia_ref
  89.4 0.0 collective-permute-done.15.ib_ref
  89.4 0.0 collective-permute-done.11.b3_ref
  89.4 0.0 collective-permute-done.8.ba_ref
  89.4 0.0 copy-done.1
  89.5 0.0 copy-done.5
  89.5 0.0 copy-start.2
  89.5 13.6 %shard_map.82 = (f32[6144,128]{1,0:T(8,128)}, f32[6144,128]{1,0:T(8,128)S(1)}, f32[1,128]{1,0:T(1,128)S(1)}) custom-call(s32[1]{0:T(128)S(6)} %copy.18.refs_0_.index_ref, s32[4,4]{1,0:T(4,128)S(1)} %copy-done.5, f32[3,4,32,8,256]{4,3,2,1,0:T(8,128)S(1)} %get-tuple-element.46.v_ref, f32[5,32,8,256]{3,2,1,0:T(8,128)S(1)} %get-tuple-element.47.bw_ref, ...), custom_call_target="tpu_custom_call" | custom-call | flops 100000000 | bytes 17048132 | tf_op jit(solution)/shard_map/pallas_call | solution.py:933
  103.1 20.0 %all_to_all.5 = f32[32,1,128]{2,1,0:T(1,128)S(1)} all-to-all(f32[32,1,128]{2,1,0:T(1,128)S(1)} %broadcast_in_dim.9), channel_id=1, replica_groups=mesh['gx'=8,'gz'=4] {'gx','gz'}, dimensions={0} | all-to-all | bytes 32768 | tf_op jit(solution)/shard_map/all_to_all | solution.py:1025
  123.1 0.0 copy-done.2
  123.1 2.6 %shard_map.83 = (f32[6144,128]{1,0:T(8,128)}, f32[4,4]{1,0:T(4,128)}) custom-call(s32[1]{0:T(128)S(6)} %copy.18.refs_0_.index_ref, f32[32,128]{1,0:T(8,128)S(1)} %bitcast.33, f32[6144,128]{1,0:T(8,128)S(1)} %bitcast.29, f32[6144,128]{1,0:T(8,128)S(1)} %get-tuple-element.58.solved_ref), custom_call_target="tpu_custom_call" | custom-call | flops 10000000 | bytes 9453636 | tf_op jit(solution)/shard_map/pallas_call | solution.py:933
  (2 shorter events, 0.1 us)
Async XLA Ops:
  0.6 1.9 %copy-start = (f32[3,64,4,4,256]{4,3,2,1,0:T(4,128)S(1)}, f32[3,64,4,4,256]{4,3,2,1,0:T(4,128)}, u32[]{:S(2)}) copy-start(f32[3,64,4,4,256]{4,3,2,1,0:T(4,128)} %param.5) | copy-start | bytes 9437188
  2.5 0.9 copy-start.3
  3.5 29.1 %copy-start.4 = (f32[64,4,256]{2,1,0:T(4,128)S(1)}, f32[64,4,256]{2,1,0:T(4,128)}, u32[]{:S(2)}) copy-start(f32[64,4,256]{2,1,0:T(4,128)} %param.7) | copy-start | bytes 786436
  5.0 27.6 %collective-permute-start.6 = (f32[312,8,256]{2,1,0:T(8,128)S(1)}, f32[312,8,256]{2,1,0:T(8,128)S(1)}, u32[]{:S(2)}, u32[]{:S(2)}) collective-permute-start(f32[312,8,256]{2,1,0:T(8,128)S(1)} %get-tuple-element.41), channel_id=1, source_target_pairs={{0,4},{4,0},{8,12},{12,8},{16,20},{20,16},{24,28},{28,24},{1,5},{5... | collective-permute-start | bytes 7667720 | tf_op jit(solution)/shard_map/ppermute | solution.py:978
  5.5 18.8 %collective-permute-start = (f32[152,8,256]{2,1,0:T(8,128)S(1)}, f32[152,8,256]{2,1,0:T(8,128)S(1)}, u32[]{:S(2)}, u32[]{:S(2)}) collective-permute-start(f32[152,8,256]{2,1,0:T(8,128)S(1)} %get-tuple-element.33), channel_id=1, source_target_pairs={{4,8},{8,4},{20,24},{24,20},{12,28},{16,0},{5,9},{9,5},{21,25},{25... | collective-permute-start | bytes 3735560 | tf_op jit(solution)/shard_map/ppermute | solution.py:974
  6.8 7.0 %collective-permute-start.1 = (f32[26,8,256]{2,1,0:T(8,128)S(1)}, f32[26,8,256]{2,1,0:T(8,128)S(1)}, u32[]{:S(2)}, u32[]{:S(2)}) collective-permute-start(f32[26,8,256]{2,1,0:T(8,128)S(1)} %get-tuple-element.34), channel_id=1, source_target_pairs={{0,1},{1,0},{2,3},{3,2},{4,5},{5,4},{6,7},{7,6},{8,9},{9,8},{10,11... | collective-permute-start | bytes 638984 | tf_op jit(solution)/shard_map/ppermute | solution.py:975
  9.5 12.0 %collective-permute-start.2 = (f32[26,8,256]{2,1,0:T(8,128)S(1)}, f32[26,8,256]{2,1,0:T(8,128)S(1)}, u32[]{:S(2)}, u32[]{:S(2)}) collective-permute-start(f32[26,8,256]{2,1,0:T(8,128)S(1)} %get-tuple-element.35), channel_id=1, source_target_pairs={{1,2},{2,1},{3,0},{0,3},{5,6},{6,5},{7,4},{4,7},{9,10},{10,9},{11,... | collective-permute-start | bytes 638984 | tf_op jit(solution)/shard_map/ppermute | solution.py:976
  12.0 29.4 %collective-permute-start.4 = (f32[160,8,256]{2,1,0:T(8,128)S(1)}, f32[160,8,256]{2,1,0:T(8,128)S(1)}, u32[]{:S(2)}, u32[]{:S(2)}) collective-permute-start(f32[160,8,256]{2,1,0:T(8,128)S(1)} %get-tuple-element.37), channel_id=1, source_target_pairs={{4,8},{8,4},{12,16},{16,12},{20,24},{24,20},{5,9},{9,5},{13,17},{1... | collective-permute-start | bytes 3932168 | tf_op jit(solution)/shard_map/ppermute | solution.py:977
  24.3 28.3 %collective-permute-start.3 = (f32[152,8,256]{2,1,0:T(8,128)S(1)}, f32[152,8,256]{2,1,0:T(8,128)S(1)}, u32[]{:S(2)}, u32[]{:S(2)}) collective-permute-start(f32[152,8,256]{2,1,0:T(8,128)S(1)} %collective-permute-done.refs_3_), channel_id=1, source_target_pairs={{28,16},{0,12},{29,17},{1,13},{30,18},{2,14},{31,19},{3,15}} | collective-permute-start | bytes 3735560 | tf_op jit(solution)/shard_map/ppermute | solution.py:984
  27.2 5.4 %collective-permute-start.7 = (f32[17,8,256]{2,1,0:T(8,128)S(1)}, f32[17,8,256]{2,1,0:T(8,128)S(1)}, u32[]{:S(2)}, u32[]{:S(2)}) collective-permute-start(f32[17,8,256]{2,1,0:T(8,128)S(1)} %get-tuple-element.42), channel_id=1, source_target_pairs={{0,4},{4,0},{8,12},{12,8},{16,20},{20,16},{24,28},{28,24},{1,5},{5... | collective-permute-start | bytes 417800 | tf_op jit(solution)/shard_map/ppermute | solution.py:981
  31.3 10.1 %collective-permute-start.5 = (f32[17,8,256]{2,1,0:T(8,128)S(1)}, f32[17,8,256]{2,1,0:T(8,128)S(1)}, u32[]{:S(2)}, u32[]{:S(2)}) collective-permute-start(f32[17,8,256]{2,1,0:T(8,128)S(1)} %get-tuple-element.38), channel_id=1, source_target_pairs={{4,8},{8,4},{12,16},{16,12},{20,24},{24,20},{5,9},{9,5},{13,17},{1... | collective-permute-start | bytes 417800 | tf_op jit(solution)/shard_map/ppermute | solution.py:982
  52.7 36.8 %copy-start.1 = (f32[3,64,4,4,256]{4,3,2,1,0:T(4,128)S(1)}, f32[3,64,4,4,256]{4,3,2,1,0:T(4,128)}, u32[]{:S(2)}) copy-start(f32[3,64,4,4,256]{4,3,2,1,0:T(4,128)} %param.5) | copy-start | bytes 9437188
  52.7 36.8 %copy-start.5 = (s32[4,4]{1,0:T(4,128)S(1)}, s32[4,4]{1,0:T(4,128)}, u32[]{:S(2)}) copy-start(s32[4,4]{1,0:T(4,128)} %cells_ref.1) | copy-start | bytes 196
  62.7 12.6 %collective-permute-start.9 = (f32[2,32,8,256]{3,2,1,0:T(8,128)S(1)}, f32[2,32,8,256]{3,2,1,0:T(8,128)S(1)}, u32[]{:S(2)}, u32[]{:S(2)}) collective-permute-start(f32[2,32,8,256]{3,2,1,0:T(8,128)S(1)} %get-tuple-element.49), channel_id=1, source_target_pairs={{4,8},{8,4},{20,24},{24,20},{12,28},{16,0},{5,9},{9,5},{21,25},{25... | collective-permute-start | bytes 1572872 | tf_op jit(solution)/shard_map/ppermute | solution.py:999
  64.0 25.4 %collective-permute-start.8 = (f32[4,32,8,256]{3,2,1,0:T(8,128)S(1)}, f32[4,32,8,256]{3,2,1,0:T(8,128)S(1)}, u32[]{:S(2)}, u32[]{:S(2)}) collective-permute-start(f32[4,32,8,256]{3,2,1,0:T(8,128)S(1)} %get-tuple-element.48), channel_id=1, source_target_pairs={{0,4},{4,0},{8,12},{12,8},{16,20},{20,16},{24,28},{28,24},{1,5},{5... | collective-permute-start | bytes 3145736 | tf_op jit(solution)/shard_map/ppermute | solution.py:1006
  67.8 7.5 %collective-permute-start.10 = (f32[5,5,8,256]{3,2,1,0:T(8,128)S(1)}, f32[5,5,8,256]{3,2,1,0:T(8,128)S(1)}, u32[]{:S(2)}, u32[]{:S(2)}) collective-permute-start(f32[5,5,8,256]{3,2,1,0:T(8,128)S(1)} %get-tuple-element.50.states_ref), channel_id=1, source_target_pairs={{0,1},{1,0},{2,3},{3,2},{4,5},{5,4},{6,7},{7,6},{8,9},{9,8},{10,11... | collective-permute-start | bytes 614408 | tf_op jit(solution)/shard_map/ppermute | solution.py:1001
  70.0 18.8 %collective-permute-start.12 = (f32[2,32,8,256]{3,2,1,0:T(8,128)S(1)}, f32[2,32,8,256]{3,2,1,0:T(8,128)S(1)}, u32[]{:S(2)}, u32[]{:S(2)}) collective-permute-start(f32[2,32,8,256]{3,2,1,0:T(8,128)S(1)} %get-tuple-element.52), channel_id=1, source_target_pairs={{4,8},{8,4},{12,16},{16,12},{20,24},{24,20},{5,9},{9,5},{13,17},{1... | collective-permute-start | bytes 1572872 | tf_op jit(solution)/shard_map/ppermute | solution.py:1000
  75.3 14.1 %collective-permute-start.11 = (f32[2,32,8,256]{3,2,1,0:T(8,128)S(1)}, f32[2,32,8,256]{3,2,1,0:T(8,128)S(1)}, u32[]{:S(2)}, u32[]{:S(2)}) collective-permute-start(f32[2,32,8,256]{3,2,1,0:T(8,128)S(1)} %collective-permute-done.9.b1_ref), channel_id=1, source_target_pairs={{28,16},{0,12},{29,17},{1,13},{30,18},{2,14},{31,19},{3,15}} | collective-permute-start | bytes 1572872 | tf_op jit(solution)/shard_map/ppermute | solution.py:1005
  78.8 9.1 %collective-permute-start.13 = (f32[5,5,8,256]{3,2,1,0:T(8,128)S(1)}, f32[5,5,8,256]{3,2,1,0:T(8,128)S(1)}, u32[]{:S(2)}, u32[]{:S(2)}) collective-permute-start(f32[5,5,8,256]{3,2,1,0:T(8,128)S(1)} %shard_map.80), channel_id=1, source_target_pairs={{1,2},{2,1},{3,0},{0,3},{5,6},{6,5},{7,4},{4,7},{9,10},{10,9},{11,... | collective-permute-start | bytes 614408 | tf_op jit(solution)/shard_map/ppermute | solution.py:1003
  88.0 1.5 %collective-permute-start.14 = (f32[5,4,8,256]{3,2,1,0:T(8,128)S(1)}, f32[5,4,8,256]{3,2,1,0:T(8,128)S(1)}, u32[]{:S(2)}, u32[]{:S(2)}) collective-permute-start(f32[5,4,8,256]{3,2,1,0:T(8,128)S(1)} %get-tuple-element.54), channel_id=1, source_target_pairs={{0,4},{4,0},{8,12},{12,8},{16,20},{20,16},{24,28},{28,24},{1,5},{5... | collective-permute-start | bytes 491528 | tf_op jit(solution)/shard_map/ppermute | solution.py:1013
  88.1 1.4 %collective-permute-start.15 = (f32[5,4,8,256]{3,2,1,0:T(8,128)S(1)}, f32[5,4,8,256]{3,2,1,0:T(8,128)S(1)}, u32[]{:S(2)}, u32[]{:S(2)}) collective-permute-start(f32[5,4,8,256]{3,2,1,0:T(8,128)S(1)} %get-tuple-element.55), channel_id=1, source_target_pairs={{4,8},{8,4},{12,16},{16,12},{20,24},{24,20},{5,9},{9,5},{13,17},{1... | collective-permute-start | bytes 491528 | tf_op jit(solution)/shard_map/ppermute | solution.py:1012
  89.5 33.7 %copy-start.2 = (f32[3,64,4,4,256]{4,3,2,1,0:T(4,128)S(1)}, f32[3,64,4,4,256]{4,3,2,1,0:T(4,128)}, u32[]{:S(2)}) copy-start(f32[3,64,4,4,256]{4,3,2,1,0:T(4,128)} %param.6) | copy-start | bytes 9437188

commit v8 on v7

--- a/solution.py
+++ b/solution.py
@@ -770,7 +770,7 @@
                 q_ref[power, x, zz] = q_ref[power, x, zz] + beside
             return 0
 
-        lax.fori_loop(0, HALF + 1, apply, 0, unroll=11)
+        lax.fori_loop(0, HALF + 1, apply, 0, unroll=HALF + 1)
 
     def correct(m, _):
         for x in range(4):
@@ -1002,6 +1002,7 @@
     (joined,) = call(joining_kernel, [states.shape], [], [states, partner], 0, 10**5, 4)
     other = lax.ppermute(joined, "gz", far)
     pb1_in, _ = lax.optimization_barrier((pb1_in, partner))
+    pa, _ = lax.optimization_barrier((pa, partner))
     pb3_in = lax.ppermute(pb1_in, "gx", forward_round)
     pa_in = lax.ppermute(pa, "gx", swap_in)
     entering, enter_a, enter_b = call(

time: 126 us -> 124 us (0.984)
  waiting for transfers between devices: 33.7 us -> 36.6 us
  starting transfers between devices: 31 us -> 28.6 us
  blocking collectives: 20 us -> 18.2 us
    ppermute x1, waiting for transfers between devices: 0.01 us -> 4.03 us  [fast_shards(): pb1_in = lax.ppermute(pb1, 'gx', send_round)]
    all_to_all x1, blocking collectives: 20 us -> 18.2 us  [fast_shards(): lax.all_to_all(jnp.broadcast_to(sums[None], (devices, 1, 128)), ('gx', 'g...]
    ppermute x1, waiting for transfers between devices: 4.63 us -> 2.91 us  [fast_shards(): partner = lax.ppermute(states, 'gz', near)]
  transfers between devices with their start and end apart: 16 -> 16, of which waited for: 7 -> 8; matrix products, arithmetic and copies ran while one was open for 0% -> 0% of each run, Pallas kernels for 7% -> 7%
where the time goes in v8:
time: 124 us
  waiting for transfers between devices  36.6 us (30%)
  Pallas kernels  36.1 us (29%)
  starting transfers between devices  28.6 us (23%)
  blocking collectives  18.2 us (15%)
  local copies, waits for them, and re-layouts  2.86 us (2%)
  between operations  1.66 us (1%)
    pallas_call x8, Pallas kernels, call(): pl.pallas_call(kernel, out_shape=arrays, in_specs=places, out_specs=resul...  36.1 us
    all_to_all x1, blocking collectives, fast_shards(): lax.all_to_all(jnp.broadcast_to(sums[None], (devices, 1, 128)), ('gx', 'g...  18.2 us
    ppermute x1, waiting for transfers between devices, fast_shards(): b3_in = lax.ppermute(b1_in, 'gx', forward_round)  11.3 us
    ppermute x1, waiting for transfers between devices, fast_shards(): z2 = lax.ppermute(z2, 'gz', far)  7.59 us
    ppermute x1, waiting for transfers between devices, fast_shards(): other = lax.ppermute(joined, 'gz', far)  6.01 us
    ppermute x1, starting transfers between devices, fast_shards(): ca = lax.ppermute(ca, 'gx', swap_in)  4.12 us
    ppermute x1, waiting for transfers between devices, fast_shards(): pb1_in = lax.ppermute(pb1, 'gx', send_round)  4.03 us
    ppermute x1, starting transfers between devices, fast_shards(): other = lax.ppermute(joined, 'gz', far)  3.66 us
  transfers between devices with their start and end apart: 16, of which 8 were waited for; matrix products, arithmetic and copies ran while one was open for 0% of the time, Pallas kernels for 7%

profile of v8, /device:TPU:0, one launch (start us, length us, event | category | flops | bytes accessed | tf_op | source)
XLA Modules:
  0.0 124.0 jit_solution(5769304836802125536)
XLA Ops:
  0.6 0.0 copy-start
  0.6 1.9 %copy-done = f32[3,64,4,4,256]{4,3,2,1,0:T(4,128)S(1)} copy-done((f32[3,64,4,4,256]{4,3,2,1,0:T(4,128)S(1)}, f32[3,64,4,4,256]{4,3,2,1,0:T(4,128)}, u32[]{:S(2)}) %copy-start) | copy-done | bytes 3145752
  2.5 0.0 copy-start.3
  2.5 0.9 copy-done.3
  3.5 0.0 copy-start.4
  3.5 1.5 %shard_map.76 = (f32[3,4,32,8,256]{4,3,2,1,0:T(8,128)S(1)}, f32[312,8,256]{2,1,0:T(8,128)S(1)}, f32[152,8,256]{2,1,0:T(8,128)S(1)}, f32[160,8,256]{2,1,0:T(8,128...) custom-call(f32[6144,128]{1,0:T(8,128)S(1)} %bitcast.27, f32[512,128]{1,0:T(8,128)S(1)} %bitcast.30), custom_call_target="tpu_custom_call" | custom-call | flops 1000000 | bytes 12091392 | tf_op jit(solution)/shard_map/pallas_call | solution.py:933
  5.0 0.5 collective-permute-start.6
  5.5 1.3 %collective-permute-start = (f32[152,8,256]{2,1,0:T(8,128)S(1)}, f32[152,8,256]{2,1,0:T(8,128)S(1)}, u32[]{:S(2)}, u32[]{:S(2)}) collective-permute-start(f32[152,8,256]{2,1,0:T(8,128)S(1)} %get-tuple-element.34), channel_id=1, source_target_pairs={{4,8},{8,4},{20,24},{24,20},{12,28},{16,0},{5,9},{9,5},{21,25},{25... | collective-permute-start | bytes 3735560 | tf_op jit(solution)/shard_map/ppermute | solution.py:974
  6.8 2.7 %collective-permute-start.1 = (f32[26,8,256]{2,1,0:T(8,128)S(1)}, f32[26,8,256]{2,1,0:T(8,128)S(1)}, u32[]{:S(2)}, u32[]{:S(2)}) collective-permute-start(f32[26,8,256]{2,1,0:T(8,128)S(1)} %get-tuple-element.35), channel_id=1, source_target_pairs={{0,1},{1,0},{2,3},{3,2},{4,5},{5,4},{6,7},{7,6},{8,9},{9,8},{10,11... | collective-permute-start | bytes 638984 | tf_op jit(solution)/shard_map/ppermute | solution.py:975
  9.5 2.5 %collective-permute-start.2 = (f32[26,8,256]{2,1,0:T(8,128)S(1)}, f32[26,8,256]{2,1,0:T(8,128)S(1)}, u32[]{:S(2)}, u32[]{:S(2)}) collective-permute-start(f32[26,8,256]{2,1,0:T(8,128)S(1)} %get-tuple-element.36), channel_id=1, source_target_pairs={{1,2},{2,1},{3,0},{0,3},{5,6},{6,5},{7,4},{4,7},{9,10},{10,9},{11,... | collective-permute-start | bytes 638984 | tf_op jit(solution)/shard_map/ppermute | solution.py:976
  12.0 0.7 collective-permute-start.4
  12.7 1.1 collective-permute-done.1.z1_ref.refs_5_.refs_7_
  13.8 7.6 %collective-permute-done.2.z2_ref.refs_6_.refs_8_ = f32[26,8,256]{2,1,0:T(8,128)S(1)} collective-permute-done((f32[26,8,256]{2,1,0:T(8,128)S(1)}, f32[26,8,256]{2,1,0:T(8,128)S(1)}, u32[]{:S(2)}, u32[]{:S(2)}) %collective-permute-start.2) | collective-permute-done | bytes 213024 | tf_op jit(solution)/shard_map/ppermute | solution.py:976
  21.4 2.9 %collective-permute-done.refs_3_ = f32[152,8,256]{2,1,0:T(8,128)S(1)} collective-permute-done((f32[152,8,256]{2,1,0:T(8,128)S(1)}, f32[152,8,256]{2,1,0:T(8,128)S(1)}, u32[]{:S(2)}, u32[]{:S(2)}) %collective-permute-start) | collective-permute-done | bytes 1245216 | tf_op jit(solution)/shard_map/ppermute | solution.py:974
  24.3 2.8 %collective-permute-start.3 = (f32[152,8,256]{2,1,0:T(8,128)S(1)}, f32[152,8,256]{2,1,0:T(8,128)S(1)}, u32[]{:S(2)}, u32[]{:S(2)}) collective-permute-start(f32[152,8,256]{2,1,0:T(8,128)S(1)} %collective-permute-done.refs_3_), channel_id=1, source_target_pairs={{28,16},{0,12},{29,17},{1,13},{30,18},{2,14},{31,19},{3,15}} | collective-permute-start | bytes 3735560 | tf_op jit(solution)/shard_map/ppermute | solution.py:984
  27.1 0.1 shard_map.77
  27.2 4.1 %collective-permute-start.7 = (f32[17,8,256]{2,1,0:T(8,128)S(1)}, f32[17,8,256]{2,1,0:T(8,128)S(1)}, u32[]{:S(2)}, u32[]{:S(2)}) collective-permute-start(f32[17,8,256]{2,1,0:T(8,128)S(1)} %get-tuple-element.43), channel_id=1, source_target_pairs={{0,4},{4,0},{8,12},{12,8},{16,20},{20,16},{24,28},{28,24},{1,5},{5... | collective-permute-start | bytes 417800 | tf_op jit(solution)/shard_map/ppermute | solution.py:981
  31.3 0.7 collective-permute-start.5
  32.6 0.0 collective-permute-done.7.refs_4_
  32.6 0.0 collective-permute-done.6.refs_3_
  32.6 0.0 copy-done.4
  32.6 8.7 %shard_map.78 = (f32[3,2,39,8,256]{4,3,2,1,0:T(8,128)S(1)}, f32[3,2,39,8,256]{4,3,2,1,0:T(8,128)S(1)}, f32[3,33,8,256]{3,2,1,0:T(8,128)S(1)}) custom-call(s32[1]{0:T(128)S(6)} %copy.18.refs_0_.index_ref, f32[3,4,32,8,256]{4,3,2,1,0:T(8,128)S(1)} %get-tuple-element.33.refs_1_, f32[512,128]{1,0:T(8,128)S(1)} %bitcast.31, ...), custom_call_target="tpu_custom_call" | custom-call | flops 100000000 | bytes 11173892 | tf_op jit(solution)/shard_map/pallas_call | solution.py:933
  41.3 0.0 collective-permute-done.5.refs_6_
  41.3 0.0 collective-permute-done.4.refs_5_
  41.4 11.3 %collective-permute-done.3.refs_4_ = f32[152,8,256]{2,1,0:T(8,128)S(1)} collective-permute-done((f32[152,8,256]{2,1,0:T(8,128)S(1)}, f32[152,8,256]{2,1,0:T(8,128)S(1)}, u32[]{:S(2)}, u32[]{:S(2)}) %collective-permute-start.3) | collective-permute-done | bytes 1245216 | tf_op jit(solution)/shard_map/ppermute | solution.py:984
  52.7 0.0 copy-start.1
  52.7 0.0 copy-start.5
  52.7 10.0 %shard_map.79 = (f32[3,4,32,8,256]{4,3,2,1,0:T(8,128)S(1)}, f32[5,32,8,256]{3,2,1,0:T(8,128)S(1)}, f32[5,5,8,256]{3,2,1,0:T(8,128)S(1)}, f32[4,32,8,256]{3,2,1,0...) custom-call(s32[1]{0:T(128)S(6)} %copy.18.refs_0_.index_ref, ...), custom_call_target="tpu_custom_call" | custom-call | flops 100000000 | bytes 19177476 | tf_op jit(solution)/shard_map/pallas_call | solution.py:933
  62.7 1.6 %collective-permute-start.8 = (f32[5,5,8,256]{3,2,1,0:T(8,128)S(1)}, f32[5,5,8,256]{3,2,1,0:T(8,128)S(1)}, u32[]{:S(2)}, u32[]{:S(2)}) collective-permute-start(f32[5,5,8,256]{3,2,1,0:T(8,128)S(1)} %get-tuple-element.50.states_ref), channel_id=1, source_target_pairs={{0,1},{1,0},{2,3},{3,2},{4,5},{5,4},{6,7},{7,6},{8,9},{9,8},{10,11... | collective-permute-start | bytes 614408 | tf_op jit(solution)/shard_map/ppermute | solution.py:1001
  64.3 1.3 %collective-permute-start.10 = (f32[2,32,8,256]{3,2,1,0:T(8,128)S(1)}, f32[2,32,8,256]{3,2,1,0:T(8,128)S(1)}, u32[]{:S(2)}, u32[]{:S(2)}) collective-permute-start(f32[2,32,8,256]{3,2,1,0:T(8,128)S(1)} %get-tuple-element.52), channel_id=1, source_target_pairs={{4,8},{8,4},{20,24},{24,20},{12,28},{16,0},{5,9},{9,5},{21,25},{25... | collective-permute-start | bytes 1572872 | tf_op jit(solution)/shard_map/ppermute | solution.py:999
  65.6 2.9 %collective-permute-done.8.partner_ref = f32[5,5,8,256]{3,2,1,0:T(8,128)S(1)} collective-permute-done((f32[5,5,8,256]{3,2,1,0:T(8,128)S(1)}, f32[5,5,8,256]{3,2,1,0:T(8,128)S(1)}, u32[]{:S(2)}, u32[]{:S(2)}) %collective-permute-start.8) | collective-permute-done | bytes 204832 | tf_op jit(solution)/shard_map/ppermute | solution.py:1001
  68.5 2.7 %collective-permute-start.9 = (f32[4,32,8,256]{3,2,1,0:T(8,128)S(1)}, f32[4,32,8,256]{3,2,1,0:T(8,128)S(1)}, u32[]{:S(2)}, u32[]{:S(2)}) collective-permute-start(f32[4,32,8,256]{3,2,1,0:T(8,128)S(1)} %get-tuple-element.51), channel_id=1, source_target_pairs={{0,4},{4,0},{8,12},{12,8},{16,20},{20,16},{24,28},{28,24},{1,5},{5... | collective-permute-start | bytes 3145736 | tf_op jit(solution)/shard_map/ppermute | solution.py:1007
  71.2 0.7 collective-permute-start.12
  71.9 4.0 %collective-permute-done.10.b1_ref = f32[2,32,8,256]{3,2,1,0:T(8,128)S(1)} collective-permute-done((f32[2,32,8,256]{3,2,1,0:T(8,128)S(1)}, f32[2,32,8,256]{3,2,1,0:T(8,128)S(1)}, u32[]{:S(2)}, u32[]{:S(2)}) %collective-permute-start.10) | collective-permute-done | bytes 524320 | tf_op jit(solution)/shard_map/ppermute | solution.py:999
  75.9 2.7 %collective-permute-start.11 = (f32[2,32,8,256]{3,2,1,0:T(8,128)S(1)}, f32[2,32,8,256]{3,2,1,0:T(8,128)S(1)}, u32[]{:S(2)}, u32[]{:S(2)}) collective-permute-start(f32[2,32,8,256]{3,2,1,0:T(8,128)S(1)} %collective-permute-done.10.b1_ref), channel_id=1, source_target_pairs={{28,16},{0,12},{29,17},{1,13},{30,18},{2,14},{31,19},{3,15}} | collective-permute-start | bytes 1572872 | tf_op jit(solution)/shard_map/ppermute | solution.py:1006
  78.7 3.7 %collective-permute-start.13 = (f32[5,5,8,256]{3,2,1,0:T(8,128)S(1)}, f32[5,5,8,256]{3,2,1,0:T(8,128)S(1)}, u32[]{:S(2)}, u32[]{:S(2)}) collective-permute-start(f32[5,5,8,256]{3,2,1,0:T(8,128)S(1)} %shard_map.80), channel_id=1, source_target_pairs={{1,2},{2,1},{3,0},{0,3},{5,6},{6,5},{7,4},{4,7},{9,10},{10,9},{11,... | collective-permute-start | bytes 614408 | tf_op jit(solution)/shard_map/ppermute | solution.py:1003
  82.4 6.0 %collective-permute-done.13.other_ref = f32[5,5,8,256]{3,2,1,0:T(8,128)S(1)} collective-permute-done((f32[5,5,8,256]{3,2,1,0:T(8,128)S(1)}, f32[5,5,8,256]{3,2,1,0:T(8,128)S(1)}, u32[]{:S(2)}, u32[]{:S(2)}) %collective-permute-start.13) | collective-permute-done | bytes 204832 | tf_op jit(solution)/shard_map/ppermute | solution.py:1003
  88.4 0.1 shard_map.81
  88.5 0.1 collective-permute-start.14
  88.6 0.7 collective-permute-start.15
  89.2 0.0 collective-permute-done.12.b2_ref
  89.2 0.7 collective-permute-done.14.ia_ref
  89.9 0.0 collective-permute-done.15.ib_ref
  89.9 0.0 collective-permute-done.11.b3_ref
  89.9 0.0 collective-permute-done.9.ba_ref
  90.0 0.0 copy-done.1
  90.0 0.0 copy-done.5
  90.0 0.0 copy-start.2
  90.0 13.0 %shard_map.82 = (f32[6144,128]{1,0:T(8,128)}, f32[6144,128]{1,0:T(8,128)S(1)}, f32[1,128]{1,0:T(1,128)S(1)}) custom-call(s32[1]{0:T(128)S(6)} %copy.18.refs_0_.index_ref, s32[4,4]{1,0:T(4,128)S(1)} %copy-done.5, f32[3,4,32,8,256]{4,3,2,1,0:T(8,128)S(1)} %get-tuple-element.47.v_ref, f32[5,32,8,256]{3,2,1,0:T(8,128)S(1)} %get-tuple-element.48.bw_ref, ...), custom_call_target="tpu_custom_call" | custom-call | flops 100000000 | bytes 17048132 | tf_op jit(solution)/shard_map/pallas_call | solution.py:933
  103.0 18.2 %all_to_all.5 = f32[32,1,128]{2,1,0:T(1,128)S(1)} all-to-all(f32[32,1,128]{2,1,0:T(1,128)S(1)} %broadcast_in_dim.9), channel_id=1, replica_groups=mesh['gx'=8,'gz'=4] {'gx','gz'}, dimensions={0} | all-to-all | bytes 32768 | tf_op jit(solution)/shard_map/all_to_all | solution.py:1026
  121.3 0.0 copy-done.2
  121.3 2.6 %shard_map.83 = (f32[6144,128]{1,0:T(8,128)}, f32[4,4]{1,0:T(4,128)}) custom-call(s32[1]{0:T(128)S(6)} %copy.18.refs_0_.index_ref, f32[32,128]{1,0:T(8,128)S(1)} %bitcast.33, f32[6144,128]{1,0:T(8,128)S(1)} %bitcast.29, f32[6144,128]{1,0:T(8,128)S(1)} %get-tuple-element.60.solved_ref), custom_call_target="tpu_custom_call" | custom-call | flops 10000000 | bytes 9453636 | tf_op jit(solution)/shard_map/pallas_call | solution.py:933
  (2 shorter events, 0.1 us)
Async XLA Ops:
  0.6 1.9 %copy-start = (f32[3,64,4,4,256]{4,3,2,1,0:T(4,128)S(1)}, f32[3,64,4,4,256]{4,3,2,1,0:T(4,128)}, u32[]{:S(2)}) copy-start(f32[3,64,4,4,256]{4,3,2,1,0:T(4,128)} %param.5) | copy-start | bytes 9437188
  2.5 0.9 copy-start.3
  3.5 29.1 %copy-start.4 = (f32[64,4,256]{2,1,0:T(4,128)S(1)}, f32[64,4,256]{2,1,0:T(4,128)}, u32[]{:S(2)}) copy-start(f32[64,4,256]{2,1,0:T(4,128)} %param.7) | copy-start | bytes 786436
  5.0 27.6 %collective-permute-start.6 = (f32[312,8,256]{2,1,0:T(8,128)S(1)}, f32[312,8,256]{2,1,0:T(8,128)S(1)}, u32[]{:S(2)}, u32[]{:S(2)}) collective-permute-start(f32[312,8,256]{2,1,0:T(8,128)S(1)} %get-tuple-element.42), channel_id=1, source_target_pairs={{0,4},{4,0},{8,12},{12,8},{16,20},{20,16},{24,28},{28,24},{1,5},{5... | collective-permute-start | bytes 7667720 | tf_op jit(solution)/shard_map/ppermute | solution.py:978
  5.5 18.8 %collective-permute-start = (f32[152,8,256]{2,1,0:T(8,128)S(1)}, f32[152,8,256]{2,1,0:T(8,128)S(1)}, u32[]{:S(2)}, u32[]{:S(2)}) collective-permute-start(f32[152,8,256]{2,1,0:T(8,128)S(1)} %get-tuple-element.34), channel_id=1, source_target_pairs={{4,8},{8,4},{20,24},{24,20},{12,28},{16,0},{5,9},{9,5},{21,25},{25... | collective-permute-start | bytes 3735560 | tf_op jit(solution)/shard_map/ppermute | solution.py:974
  6.8 7.0 %collective-permute-start.1 = (f32[26,8,256]{2,1,0:T(8,128)S(1)}, f32[26,8,256]{2,1,0:T(8,128)S(1)}, u32[]{:S(2)}, u32[]{:S(2)}) collective-permute-start(f32[26,8,256]{2,1,0:T(8,128)S(1)} %get-tuple-element.35), channel_id=1, source_target_pairs={{0,1},{1,0},{2,3},{3,2},{4,5},{5,4},{6,7},{7,6},{8,9},{9,8},{10,11... | collective-permute-start | bytes 638984 | tf_op jit(solution)/shard_map/ppermute | solution.py:975
  9.5 12.0 %collective-permute-start.2 = (f32[26,8,256]{2,1,0:T(8,128)S(1)}, f32[26,8,256]{2,1,0:T(8,128)S(1)}, u32[]{:S(2)}, u32[]{:S(2)}) collective-permute-start(f32[26,8,256]{2,1,0:T(8,128)S(1)} %get-tuple-element.36), channel_id=1, source_target_pairs={{1,2},{2,1},{3,0},{0,3},{5,6},{6,5},{7,4},{4,7},{9,10},{10,9},{11,... | collective-permute-start | bytes 638984 | tf_op jit(solution)/shard_map/ppermute | solution.py:976
  12.0 29.4 %collective-permute-start.4 = (f32[160,8,256]{2,1,0:T(8,128)S(1)}, f32[160,8,256]{2,1,0:T(8,128)S(1)}, u32[]{:S(2)}, u32[]{:S(2)}) collective-permute-start(f32[160,8,256]{2,1,0:T(8,128)S(1)} %get-tuple-element.38), channel_id=1, source_target_pairs={{4,8},{8,4},{12,16},{16,12},{20,24},{24,20},{5,9},{9,5},{13,17},{1... | collective-permute-start | bytes 3932168 | tf_op jit(solution)/shard_map/ppermute | solution.py:977
  24.3 28.3 %collective-permute-start.3 = (f32[152,8,256]{2,1,0:T(8,128)S(1)}, f32[152,8,256]{2,1,0:T(8,128)S(1)}, u32[]{:S(2)}, u32[]{:S(2)}) collective-permute-start(f32[152,8,256]{2,1,0:T(8,128)S(1)} %collective-permute-done.refs_3_), channel_id=1, source_target_pairs={{28,16},{0,12},{29,17},{1,13},{30,18},{2,14},{31,19},{3,15}} | collective-permute-start | bytes 3735560 | tf_op jit(solution)/shard_map/ppermute | solution.py:984
  27.2 5.4 %collective-permute-start.7 = (f32[17,8,256]{2,1,0:T(8,128)S(1)}, f32[17,8,256]{2,1,0:T(8,128)S(1)}, u32[]{:S(2)}, u32[]{:S(2)}) collective-permute-start(f32[17,8,256]{2,1,0:T(8,128)S(1)} %get-tuple-element.43), channel_id=1, source_target_pairs={{0,4},{4,0},{8,12},{12,8},{16,20},{20,16},{24,28},{28,24},{1,5},{5... | collective-permute-start | bytes 417800 | tf_op jit(solution)/shard_map/ppermute | solution.py:981
  31.3 10.1 %collective-permute-start.5 = (f32[17,8,256]{2,1,0:T(8,128)S(1)}, f32[17,8,256]{2,1,0:T(8,128)S(1)}, u32[]{:S(2)}, u32[]{:S(2)}) collective-permute-start(f32[17,8,256]{2,1,0:T(8,128)S(1)} %get-tuple-element.39), channel_id=1, source_target_pairs={{4,8},{8,4},{12,16},{16,12},{20,24},{24,20},{5,9},{9,5},{13,17},{1... | collective-permute-start | bytes 417800 | tf_op jit(solution)/shard_map/ppermute | solution.py:982
  52.7 37.3 %copy-start.1 = (f32[3,64,4,4,256]{4,3,2,1,0:T(4,128)S(1)}, f32[3,64,4,4,256]{4,3,2,1,0:T(4,128)}, u32[]{:S(2)}) copy-start(f32[3,64,4,4,256]{4,3,2,1,0:T(4,128)} %param.5) | copy-start | bytes 9437188
  52.7 37.3 %copy-start.5 = (s32[4,4]{1,0:T(4,128)S(1)}, s32[4,4]{1,0:T(4,128)}, u32[]{:S(2)}) copy-start(s32[4,4]{1,0:T(4,128)} %cells_ref.1) | copy-start | bytes 196
  62.7 5.8 %collective-permute-start.8 = (f32[5,5,8,256]{3,2,1,0:T(8,128)S(1)}, f32[5,5,8,256]{3,2,1,0:T(8,128)S(1)}, u32[]{:S(2)}, u32[]{:S(2)}) collective-permute-start(f32[5,5,8,256]{3,2,1,0:T(8,128)S(1)} %get-tuple-element.50.states_ref), channel_id=1, source_target_pairs={{0,1},{1,0},{2,3},{3,2},{4,5},{5,4},{6,7},{7,6},{8,9},{9,8},{10,11... | collective-permute-start | bytes 614408 | tf_op jit(solution)/shard_map/ppermute | solution.py:1001
  64.3 11.6 %collective-permute-start.10 = (f32[2,32,8,256]{3,2,1,0:T(8,128)S(1)}, f32[2,32,8,256]{3,2,1,0:T(8,128)S(1)}, u32[]{:S(2)}, u32[]{:S(2)}) collective-permute-start(f32[2,32,8,256]{3,2,1,0:T(8,128)S(1)} %get-tuple-element.52), channel_id=1, source_target_pairs={{4,8},{8,4},{20,24},{24,20},{12,28},{16,0},{5,9},{9,5},{21,25},{25... | collective-permute-start | bytes 1572872 | tf_op jit(solution)/shard_map/ppermute | solution.py:999
  68.5 21.4 %collective-permute-start.9 = (f32[4,32,8,256]{3,2,1,0:T(8,128)S(1)}, f32[4,32,8,256]{3,2,1,0:T(8,128)S(1)}, u32[]{:S(2)}, u32[]{:S(2)}) collective-permute-start(f32[4,32,8,256]{3,2,1,0:T(8,128)S(1)} %get-tuple-element.51), channel_id=1, source_target_pairs={{0,4},{4,0},{8,12},{12,8},{16,20},{20,16},{24,28},{28,24},{1,5},{5... | collective-permute-start | bytes 3145736 | tf_op jit(solution)/shard_map/ppermute | solution.py:1007
  71.2 18.0 %collective-permute-start.12 = (f32[2,32,8,256]{3,2,1,0:T(8,128)S(1)}, f32[2,32,8,256]{3,2,1,0:T(8,128)S(1)}, u32[]{:S(2)}, u32[]{:S(2)}) collective-permute-start(f32[2,32,8,256]{3,2,1,0:T(8,128)S(1)} %get-tuple-element.54), channel_id=1, source_target_pairs={{4,8},{8,4},{12,16},{16,12},{20,24},{24,20},{5,9},{9,5},{13,17},{1... | collective-permute-start | bytes 1572872 | tf_op jit(solution)/shard_map/ppermute | solution.py:1000
  75.9 14.0 %collective-permute-start.11 = (f32[2,32,8,256]{3,2,1,0:T(8,128)S(1)}, f32[2,32,8,256]{3,2,1,0:T(8,128)S(1)}, u32[]{:S(2)}, u32[]{:S(2)}) collective-permute-start(f32[2,32,8,256]{3,2,1,0:T(8,128)S(1)} %collective-permute-done.10.b1_ref), channel_id=1, source_target_pairs={{28,16},{0,12},{29,17},{1,13},{30,18},{2,14},{31,19},{3,15}} | collective-permute-start | bytes 1572872 | tf_op jit(solution)/shard_map/ppermute | solution.py:1006
  78.7 9.7 %collective-permute-start.13 = (f32[5,5,8,256]{3,2,1,0:T(8,128)S(1)}, f32[5,5,8,256]{3,2,1,0:T(8,128)S(1)}, u32[]{:S(2)}, u32[]{:S(2)}) collective-permute-start(f32[5,5,8,256]{3,2,1,0:T(8,128)S(1)} %shard_map.80), channel_id=1, source_target_pairs={{1,2},{2,1},{3,0},{0,3},{5,6},{6,5},{7,4},{4,7},{9,10},{10,9},{11,... | collective-permute-start | bytes 614408 | tf_op jit(solution)/shard_map/ppermute | solution.py:1003
  88.5 1.5 %collective-permute-start.14 = (f32[5,4,8,256]{3,2,1,0:T(8,128)S(1)}, f32[5,4,8,256]{3,2,1,0:T(8,128)S(1)}, u32[]{:S(2)}, u32[]{:S(2)}) collective-permute-start(f32[5,4,8,256]{3,2,1,0:T(8,128)S(1)} %get-tuple-element.56), channel_id=1, source_target_pairs={{0,4},{4,0},{8,12},{12,8},{16,20},{20,16},{24,28},{28,24},{1,5},{5... | collective-permute-start | bytes 491528 | tf_op jit(solution)/shard_map/ppermute | solution.py:1014
  88.6 1.4 %collective-permute-start.15 = (f32[5,4,8,256]{3,2,1,0:T(8,128)S(1)}, f32[5,4,8,256]{3,2,1,0:T(8,128)S(1)}, u32[]{:S(2)}, u32[]{:S(2)}) collective-permute-start(f32[5,4,8,256]{3,2,1,0:T(8,128)S(1)} %get-tuple-element.57), channel_id=1, source_target_pairs={{4,8},{8,4},{12,16},{16,12},{20,24},{24,20},{5,9},{9,5},{13,17},{1... | collective-permute-start | bytes 491528 | tf_op jit(solution)/shard_map/ppermute | solution.py:1013
  90.0 31.3 %copy-start.2 = (f32[3,64,4,4,256]{4,3,2,1,0:T(4,128)S(1)}, f32[3,64,4,4,256]{4,3,2,1,0:T(4,128)}, u32[]{:S(2)}) copy-start(f32[3,64,4,4,256]{4,3,2,1,0:T(4,128)} %param.6) | copy-start | bytes 9437188
